TPU v7x, 32 devices: a whole 2x2x4 slice. The times are simulated.
32 devices in a mesh: grp: 2 (over core), shard: 16 (over z, y, x).
Axes of the slice: x: 2, y: 2, z: 4, core: 2. Of those that a mesh axis runs over, the one named last changes fastest.
Arguments:
- inputs: bfloat16 [4096, 2048], P(('grp', 'shard')), may hold values from -6 to 6
- positions: int32 [4096], P(('grp', 'shard')), may hold values from 0 to 1023, as said below
- cotangent: bfloat16 [4096, 2048], P(('grp', 'shard')), may hold values from -6 to 6
- w_query: bfloat16 [2048, 2048], P('shard'), may hold values from -0.125 to 0.125
- w_key: bfloat16 [2048, 2048], P('shard'), may hold values from -0.125 to 0.125
- w_value: bfloat16 [2048, 2048], P('shard'), may hold values from -0.125 to 0.125
- w_out: bfloat16 [2048, 2048], P('shard'), may hold values from -0.125 to 0.125
- query_gain: bfloat16 [2048], P('shard'), may hold values from 0.25 to 1.75
- key_gain: bfloat16 [2048], P('shard'), may hold values from 0.25 to 1.75
- attn_gain: bfloat16 [2048], P('shard'), may hold values from 0.5 to 1.5
- w_gate: bfloat16 [2048, 8192], P('shard'), may hold values from -0.125 to 0.125
- w_up: bfloat16 [2048, 8192], P('shard'), may hold values from -0.125 to 0.125
- w_down: bfloat16 [8192, 2048], P('shard'), may hold values from -0.0625 to 0.0625
- mlp_gain: bfloat16 [2048], P('shard'), may hold values from 0.5 to 1.5
Outputs:
- output: bfloat16 [4096, 2048], P(('grp', 'shard'))
- input_grad: float32 [4096, 2048], P(('grp', 'shard'))
- query_grad: float32 [2048, 2048], P('shard')
- key_grad: float32 [2048, 2048], P('shard')
- value_grad: float32 [2048, 2048], P('shard')
- out_grad: float32 [2048, 2048], P('shard')
- querygain_grad: float32 [2048], P('shard')
- keygain_grad: float32 [2048], P('shard')
- attngain_grad: float32 [2048], P('shard')
- gate_grad: float32 [2048, 8192], P('shard')
- up_grad: float32 [2048, 8192], P('shard')
- down_grad: float32 [8192, 2048], P('shard')
- mlpgain_grad: float32 [2048], P('shard')
Inputs may be any that keep to these rules, and one draw needn't show every extreme that they name: positions[t] is t minus the first index of the document that holds token t; documents are contiguous runs of 1 to 1024 tokens, at least one of exactly 1024; positions[0] = 0.
All inputs are finite; a program needn't handle non-finite values.
Results may differ from a plain program's by a relative error of at most 0.02.
Values may be sent and summed in bfloat16 or wider, within the bound.
No kernel may reach another device: no remote copies, remote signals or barrier semaphores. Data moves between devices by JAX's collectives and lax.ppermute only.
A program may use at most 512 MiB of HBM per device.

v0:
```python
import math

import jax
import jax.numpy as jnp
from jax import lax
from jax.sharding import PartitionSpec as P

HEADS = 16
HEAD = 128
DOC_LEN = 1024


def from_behind(value, axis, steps):
    count = lax.axis_size(axis)
    leading, last = (max(0, -steps), min(count, count - steps))
    return lax.ppermute(value, axis, [(source, source + steps) for source in range(leading, last)])


def norm_rows(values, scales):
    return values * lax.rsqrt(jnp.mean(values * values, axis=-1, keepdims=True) + 1e-06) * scales


def rotate(values, cosines, sines):
    row_count = values.shape[0]
    middle = HEAD // 2
    shaped = values.reshape(row_count, HEADS, HEAD)
    first_half = shaped[..., :middle]
    second_half = shaped[..., middle:]
    turned = jnp.concatenate(
        [first_half * cosines - second_half * sines, second_half * cosines + first_half * sines],
        axis=-1,
    )
    return turned.reshape(row_count, HEADS * HEAD)


def activate(gate_in, up_in):
    return jax.nn.silu(gate_in) * up_in


def along_last(left, right):
    return lax.dot_general(
        left, right, (((1,), (1,)), ((), ())), preferred_element_type=jnp.float32
    )


def along_first(left, right):
    return lax.dot_general(
        left, right, (((0,), (0,)), ((), ())), preferred_element_type=jnp.float32
    )


def reduce_three(first_term, second_term, third_term):
    return (
        lax.psum_scatter(first_term, "shard", scatter_dimension=0, tiled=True),
        lax.psum_scatter(second_term, "shard", scatter_dimension=0, tiled=True),
        lax.psum_scatter(third_term, "shard", scatter_dimension=0, tiled=True),
    )


def local(
    inputs,
    positions,
    cotangent,
    w_query,
    w_key,
    w_value,
    w_out,
    query_gain,
    key_gain,
    attn_gain,
    w_gate,
    w_up,
    w_down,
    mlp_gain,
):
    row_count, feature_width = inputs.shape
    reach_back = (DOC_LEN - 2) // row_count + 1
    span_rows = min(row_count, 512)
    key_rows = span_rows + reach_back * row_count
    scaling = 1.0 / math.sqrt(HEAD)
    middle = HEAD // 2
    frequency = jnp.power(500000.0, -2.0 * jnp.arange(middle).astype(jnp.float32) / HEAD)
    angles = positions.astype(jnp.float32)[:, None] * frequency[None, :]
    cosines = jnp.cos(angles)[:, None, :]
    sines = jnp.sin(angles)[:, None, :]
    pieces = (
        lax.all_gather(w_query, "shard", axis=0, tiled=True),
        lax.all_gather(w_key, "shard", axis=0, tiled=True),
        lax.all_gather(w_value, "shard", axis=0, tiled=True),
        lax.all_gather(w_out, "shard", axis=0, tiled=True),
        lax.all_gather(query_gain, "shard", axis=0, tiled=True),
        lax.all_gather(key_gain, "shard", axis=0, tiled=True),
        lax.all_gather(attn_gain, "shard", axis=0, tiled=True),
        lax.all_gather(mlp_gain, "shard", axis=0, tiled=True),
    )
    columns_in = inputs
    acc_query = jnp.dot(columns_in, pieces[0], preferred_element_type=jnp.float32)
    acc_key = jnp.dot(columns_in, pieces[1], preferred_element_type=jnp.float32)
    acc_value = jnp.dot(columns_in, pieces[2], preferred_element_type=jnp.float32)
    out_full = pieces[3]
    gain_block = jnp.stack([pieces[4], pieces[5], pieces[6], pieces[7]]).astype(jnp.float32)
    gain_table = gain_block
    q_raw, k_raw, v_raw, out_full, gain_table = (
        acc_query,
        acc_key,
        acc_value,
        out_full,
        gain_table,
    )

    def prepare(query_in, key_in, query_scale, key_scale):
        return (
            rotate(norm_rows(query_in, query_scale), cosines, sines),
            rotate(norm_rows(key_in, key_scale), cosines, sines),
        )

    rotated, prepare_pull = jax.vjp(prepare, q_raw, k_raw, gain_table[0], gain_table[1])
    query_low = rotated[0].astype(jnp.bfloat16)
    key_value = jnp.stack([rotated[1].astype(jnp.bfloat16), v_raw.astype(jnp.bfloat16)])
    earlier = [
        from_behind(key_value, ("grp", "shard"), distance_back)
        for distance_back in range(reach_back, 0, -1)
    ]
    key_window = jnp.concatenate(earlier + [key_value], axis=1)
    distance = (
        jnp.arange(span_rows)[:, None] + reach_back * row_count - jnp.arange(key_rows)[None, :]
    )

    def block_scores(block_start):
        query_block = query_low.reshape(span_rows, HEADS, HEAD)
        key_block = key_window[0, block_start : block_start + key_rows].reshape(
            key_rows, HEADS, HEAD
        )
        value_block = key_window[1, block_start : block_start + key_rows].reshape(
            key_rows, HEADS, HEAD
        )
        visible = (distance >= 0) & (distance <= positions[:, None])
        scores = (
            jnp.einsum("qhd,khd->hqk", query_block, key_block, preferred_element_type=jnp.float32)
            * scaling
        )
        return (query_block, key_block, value_block, visible, scores)

    block_start = 0
    query_block, key_block, value_block, visible, scores = block_scores(block_start)
    masked = jnp.where(visible[None], scores, -jnp.inf)
    top_score = jnp.max(masked, axis=-1, keepdims=True)
    expo = jnp.exp(masked - top_score)
    totals = jnp.sum(expo, axis=-1, keepdims=True)
    probs_low = (expo / totals).astype(jnp.bfloat16)
    lse_parts = [top_score + jnp.log(totals)]
    mixed = jnp.einsum("hqk,khd->qhd", probs_low, value_block, preferred_element_type=jnp.float32)
    mixed_parts = mixed.reshape(span_rows, feature_width)
    mixed_low = mixed_parts.astype(jnp.bfloat16)
    branch = jnp.dot(mixed_low, out_full, preferred_element_type=jnp.float32)
    branch_normed, attn_pull = jax.vjp(norm_rows, branch, gain_table[2])
    hidden_state = inputs.astype(jnp.float32) + branch_normed
    state_low = hidden_state.astype(jnp.bfloat16)
    pieces = (
        lax.all_gather(w_gate, "shard", axis=0, tiled=True),
        lax.all_gather(w_up, "shard", axis=0, tiled=True),
    )
    columns_in = state_low
    gate_val = jnp.dot(columns_in, pieces[0], preferred_element_type=jnp.float32)
    up_val = jnp.dot(columns_in, pieces[1], preferred_element_type=jnp.float32)
    activated, act_pull = jax.vjp(activate, gate_val, up_val)
    activated_low = activated.astype(jnp.bfloat16)
    columns_in = activated_low
    mlp_out = jnp.dot(
        columns_in,
        lax.all_gather(w_down, "shard", axis=0, tiled=True),
        preferred_element_type=jnp.float32,
    )
    mlp_normed, mlp_pull = jax.vjp(norm_rows, mlp_out, gain_table[3])
    output = (hidden_state + mlp_normed).astype(jnp.bfloat16)
    cot_float = cotangent.astype(jnp.float32)
    d_mlp, d_mlp_gain = mlp_pull(cot_float)
    d_mlp_low = d_mlp.astype(jnp.bfloat16)
    d_hidden = along_last(d_mlp_low, lax.all_gather(w_down, "shard", axis=0, tiled=True))
    d_gate, d_up = act_pull(d_hidden)
    d_gate_low = d_gate.astype(jnp.bfloat16)
    d_up_low = d_up.astype(jnp.bfloat16)
    pieces = lax.all_gather((w_gate, w_up), "shard", axis=0, tiled=True)
    d_state = along_last(d_gate_low, pieces[0]) + along_last(d_up_low, pieces[1])
    d_resid = cot_float + d_state
    gate_term = along_first(state_low, d_gate_low)
    up_term = along_first(state_low, d_up_low)
    down_term = along_first(activated_low, d_mlp_low)
    ffn_sums = reduce_three(gate_term, up_term, down_term)
    d_branch, d_attn_gain = attn_pull(d_resid)
    d_branch_low = d_branch.astype(jnp.bfloat16)
    d_mixed_low = along_last(
        d_branch_low, lax.all_gather(w_out, "shard", axis=0, tiled=True)
    ).astype(jnp.bfloat16)
    dq_parts = []
    grad_window = jnp.zeros((2, (reach_back + 1) * row_count, feature_width), jnp.float32)
    for block_number, block_start in enumerate(range(0, row_count, span_rows)):
        query_block, key_block, value_block, visible, scores = block_scores(block_start)
        probs = jnp.where(visible[None], jnp.exp(scores - lse_parts[block_number]), 0.0)
        grad_block = d_mixed_low.reshape(span_rows, HEADS, HEAD)
        d_probs = jnp.einsum(
            "qhd,khd->hqk", grad_block, value_block, preferred_element_type=jnp.float32
        )
        inner = jnp.sum(probs * d_probs, axis=-1, keepdims=True)
        d_scores = (probs * (d_probs - inner) * scaling).astype(jnp.bfloat16)
        dq_block = jnp.einsum(
            "hqk,khd->qhd", d_scores, key_block, preferred_element_type=jnp.float32
        )
        dq_parts.append(dq_block.reshape(span_rows, feature_width))
        d_keys = jnp.einsum(
            "hqk,qhd->khd", d_scores, query_block, preferred_element_type=jnp.float32
        ).reshape(key_rows, feature_width)
        d_values = jnp.einsum(
            "hqk,qhd->khd",
            probs.astype(jnp.bfloat16),
            grad_block,
            preferred_element_type=jnp.float32,
        ).reshape(key_rows, feature_width)
        grad_window = grad_window.at[:, block_start : block_start + key_rows].add(
            jnp.stack([d_keys, d_values])
        )
    own_grads = grad_window[:, reach_back * row_count :]
    for distance_back in range(1, reach_back + 1):
        lower_row = (reach_back - distance_back) * row_count
        own_grads = own_grads + from_behind(
            grad_window[:, lower_row : lower_row + row_count].astype(jnp.bfloat16),
            ("grp", "shard"),
            -distance_back,
        ).astype(jnp.float32)
    d_query_raw, d_key_raw, d_query_gain, d_key_gain = prepare_pull((dq_parts[0], own_grads[0]))
    d_query_low = d_query_raw.astype(jnp.bfloat16)
    d_key_low = d_key_raw.astype(jnp.bfloat16)
    d_value_low = own_grads[1].astype(jnp.bfloat16)
    pieces = lax.all_gather((w_query, w_key, w_value), "shard", axis=0, tiled=True)
    d_inputs = (
        along_last(d_query_low, pieces[0])
        + along_last(d_key_low, pieces[1])
        + along_last(d_value_low, pieces[2])
    )
    input_grad = d_resid + d_inputs
    qkv_term = along_first(inputs, jnp.concatenate([d_query_low, d_key_low, d_value_low], axis=1))
    out_term = along_first(mixed_low, d_branch_low)
    gain_term = jnp.stack([d_query_gain, d_key_gain, d_attn_gain, d_mlp_gain], axis=1)
    attn_sums = reduce_three(qkv_term, out_term, gain_term)
    gate_sum, up_sum, down_sum, qkv_sum, out_sum, gain_sum = (
        lax.psum(ffn_sums[0].astype(jnp.bfloat16), "grp").astype(jnp.float32),
        lax.psum(ffn_sums[1].astype(jnp.bfloat16), "grp").astype(jnp.float32),
        lax.psum(ffn_sums[2].astype(jnp.bfloat16), "grp").astype(jnp.float32),
        lax.psum(attn_sums[0].astype(jnp.bfloat16), "grp").astype(jnp.float32),
        lax.psum(attn_sums[1].astype(jnp.bfloat16), "grp").astype(jnp.float32),
        lax.psum(attn_sums[2].astype(jnp.bfloat16), "grp").astype(jnp.float32),
    )
    return (
        output,
        input_grad,
        qkv_sum[:, :feature_width],
        qkv_sum[:, feature_width : 2 * feature_width],
        qkv_sum[:, 2 * feature_width :],
        out_sum,
        gain_sum[:, 0],
        gain_sum[:, 1],
        gain_sum[:, 2],
        gate_sum,
        up_sum,
        down_sum,
        gain_sum[:, 3],
    )


def solution(mesh):
    placed = (
        P(("grp", "shard"), None),
        P(("grp", "shard")),
        P(("grp", "shard"), None),
        P("shard", None),
        P("shard", None),
        P("shard", None),
        P("shard", None),
        P("shard"),
        P("shard"),
        P("shard"),
        P("shard", None),
        P("shard", None),
        P("shard", None),
        P("shard"),
    )
    return jax.shard_map(
        local,
        mesh=mesh,
        in_specs=placed,
        out_specs=(
            P(("grp", "shard"), None),
            P(("grp", "shard"), None),
            P("shard", None),
            P("shard", None),
            P("shard", None),
            P("shard", None),
            P("shard"),
            P("shard"),
            P("shard"),
            P("shard", None),
            P("shard", None),
            P("shard", None),
            P("shard"),
        ),
        check_vma=False,
    )
```

profile of v0, /device:TPU:0, one launch (start us, length us, event | category | flops | bytes accessed | tf_op | source)
XLA Modules:
  0.0 7279.7 jit_solution(4245350019325418514)
XLA Ops:
  12.6 42.4 all-gather
  55.1 35.5 all-gather.1
  90.6 37.8 all-gather.2
  128.4 35.3 all-gather.3
  170.2 70.3 all-gather.16.cloned.1.call-done
  249.6 104.7 %all-gather.14.cloned.1.call-done = bf16[2048,2048]{1,0:T(8,128)(2,1)} async-done(((bf16[128,2048]{1,0:T(8,128)(2,1)}), bf16[2048,2048]{1,0:T(8,128)(2,1)}) %all-gather.14.cloned.1.call-update) | async-done | bytes 8388624 | tf_op jit(solution)/shard_map/all_gather | solution.py:89
  419.8 29.6 collective-permute-start.6
  450.5 40.2 collective-permute-start.7
  548.3 70.0 all-gather.18.cloned.1.call-done
  623.4 422.3 %all-gather.20.cloned.1.call-done = bf16[2048,8192]{1,0:T(8,128)(2,1)} async-done(((bf16[128,8192]{1,0:T(8,128)(2,1)}), bf16[2048,8192]{1,0:T(8,128)(2,1)}) %all-gather.20.cloned.1.call-update) | async-done | bytes 33554448 | tf_op jit(solution)/shard_map/all_gather | solution.py:160
  1064.1 333.3 %all-gather.22.cloned.1.call-done = bf16[2048,8192]{1,0:T(8,128)(2,1)} async-done(((bf16[128,8192]{1,0:T(8,128)(2,1)}), bf16[2048,8192]{1,0:T(8,128)(2,1)}) %all-gather.22.cloned.1.call-update) | async-done | bytes 33554448 | tf_op jit(solution)/shard_map/all_gather | solution.py:161
  1418.7 330.6 %all-gather.24.cloned.1.call-done = bf16[8192,2048]{1,0:T(8,128)(2,1)} async-done(((bf16[512,2048]{1,0:T(8,128)(2,1)}), bf16[8192,2048]{1,0:T(8,128)(2,1)}) %all-gather.24.cloned.1.call-update) | async-done | bytes 33554448 | tf_op jit(solution)/shard_map/all_gather | solution.py:171
  1866.3 27.6 fusion.8
  1920.2 66.0 collective-permute-done.8
  2008.7 25.7 fusion.60
  2045.8 78.5 %collective-permute-done.10 = bf16[2,128,2048]{2,1,0:T(8,128)(2,1)} collective-permute-done((bf16[2,128,2048]{2,1,0:T(8,128)(2,1)}, bf16[2,128,2048]{2,1,0:T(8,128)(2,1)}, u32[]{:S(2)}, u32[]{:S(2)}) %collective-permute-start.10) | collective-permute-done | bytes 1048608 | tf_op jit(solution)/shard_map/ppermute | solution.py:16
  2181.7 23.4 fusion.113
  2232.2 81.1 %reduce-scatter.11.cloned.1.call-done = f32[128,2048]{1,0:T(8,128)} async-done(((f32[2048,2048]{1,0:T(8,128)}), f32[128,2048]{1,0:T(8,128)}) %reduce-scatter.11.cloned.1.call-update) | async-done | bytes 1048592 | tf_op jit(solution)/shard_map/reduce_scatter | solution.py:55
  2315.4 722.6 %reduce-scatter.9.cloned.1.call-done = f32[128,6144]{0,1:T(8,128)} async-done(((f32[2048,6144]{0,1:T(8,128)}), f32[128,6144]{0,1:T(8,128)}) %reduce-scatter.9.cloned.1.call-update) | async-done | bytes 3145744 | tf_op jit(solution)/shard_map/reduce_scatter | solution.py:54
  3041.2 1355.7 %reduce-scatter.17.cloned.1.call-done = f32[512,2048]{1,0:T(8,128)} async-done(((f32[8192,2048]{1,0:T(8,128)}), f32[512,2048]{1,0:T(8,128)}) %reduce-scatter.17.cloned.1.call-update) | async-done | bytes 4194320 | tf_op jit(solution)/shard_map/reduce_scatter | solution.py:56
  4400.8 1361.7 %reduce-scatter.15.cloned.1.call-done = f32[128,8192]{1,0:T(8,128)} async-done(((f32[2048,8192]{1,0:T(8,128)}), f32[128,8192]{1,0:T(8,128)}) %reduce-scatter.15.cloned.1.call-update) | async-done | bytes 4194320 | tf_op jit(solution)/shard_map/reduce_scatter | solution.py:55
  5766.3 1361.8 %reduce-scatter.13.cloned.1.call-done = f32[128,8192]{1,0:T(8,128)} async-done(((f32[2048,8192]{1,0:T(8,128)}), f32[128,8192]{1,0:T(8,128)}) %reduce-scatter.13.cloned.1.call-update) | async-done | bytes 4194320 | tf_op jit(solution)/shard_map/reduce_scatter | solution.py:54
  7148.7 65.6 reduce-scatter.19.cloned.1.call-done
  7218.1 36.4 all-reduce.7.cloned.1.call-done
  (267 shorter events, 506.1 us)
Async XLA Ops:
  7.2 156.9 %all-gather.12.cloned.1.call-start = ((), (), s32[]{:S(2)}) async-start(), calls=%async_computation.6 | async-start | bytes 8912896 | tf_op jit(solution)/shard_map/all_gather | solution.py:88
  8.0 232.6 %all-gather.16.cloned.1.call-start = ((), (), s32[]{:S(2)}) async-start(), calls=%async_computation.8 | async-start | bytes 8912896 | tf_op jit(solution)/shard_map/all_gather | solution.py:87
  8.7 345.7 %all-gather.14.cloned.1.call-start = ((), (), s32[]{:S(2)}) async-start(), calls=%async_computation.7 | async-start | bytes 8912896 | tf_op jit(solution)/shard_map/all_gather | solution.py:89
  9.4 608.9 %all-gather.18.cloned.1.call-start = ((), (), s32[]{:S(2)}) async-start(), calls=%async_computation.9 | async-start | bytes 8912896 | tf_op jit(solution)/shard_map/all_gather | solution.py:90
  10.0 1035.7 %all-gather.20.cloned.1.call-start = ((), (), s32[]{:S(2)}) async-start(), calls=%async_computation.10 | async-start | bytes 35651584 | tf_op jit(solution)/shard_map/all_gather | solution.py:160
  10.6 1386.8 %all-gather.22.cloned.1.call-start = ((), (), s32[]{:S(2)}) async-start(), calls=%async_computation.11 | async-start | bytes 35651584 | tf_op jit(solution)/shard_map/all_gather | solution.py:161
  11.2 1738.1 %all-gather.24.cloned.1.call-start = ((), (), s32[]{:S(2)}) async-start(), calls=%async_computation.12 | async-start | bytes 35651584 | tf_op jit(solution)/shard_map/all_gather | solution.py:171
  11.9 2301.4 %reduce-scatter.11.cloned.1.call-start = ((), (), s32[]{:S(2)}) async-start(), calls=%async_computation.14 | async-start | bytes 17825792 | tf_op jit(solution)/shard_map/reduce_scatter | solution.py:55
  368.6 141.1 %collective-permute-start.4 = (bf16[2,128,2048]{2,1,0:T(8,128)(2,1)S(1)}, bf16[2,128,2048]{2,1,0:T(8,128)(2,1)S(1)}, u32[]{:S(2)}, u32[]{:S(2)}) collective-permute-start(bf16[2,128,2048]{2,1,0:T(8,128)(2,1)S(1)} %pad_maximum_fusion.1), channel_id=1, source_target_pairs={{0,4},{1,5},{2,6},{3,7},{4,8},{5,9},{6,10},{7,11},{8,12},{9,13},{1... | collective-permute-start | bytes 3145736 | tf_op jit(solution)/shard_map/ppermute | solution.py:16
  372.3 136.4 %collective-permute-start.3 = (bf16[2,128,2048]{2,1,0:T(8,128)(2,1)S(1)}, bf16[2,128,2048]{2,1,0:T(8,128)(2,1)S(1)}, u32[]{:S(2)}, u32[]{:S(2)}) collective-permute-start(bf16[2,128,2048]{2,1,0:T(8,128)(2,1)S(1)} %pad_maximum_fusion.1), channel_id=1, source_target_pairs={{0,5},{1,6},{2,7},{3,8},{4,9},{5,10},{6,11},{7,12},{8,13},{9,14},{... | collective-permute-start | bytes 3145736 | tf_op jit(solution)/shard_map/ppermute | solution.py:16
  394.1 116.7 %collective-permute-start.5 = (bf16[2,128,2048]{2,1,0:T(8,128)(2,1)S(1)}, bf16[2,128,2048]{2,1,0:T(8,128)(2,1)S(1)}, u32[]{:S(2)}, u32[]{:S(2)}) collective-permute-start(bf16[2,128,2048]{2,1,0:T(8,128)(2,1)S(1)} %pad_maximum_fusion.1), channel_id=1, source_target_pairs={{0,3},{1,4},{2,5},{3,6},{4,7},{5,8},{6,9},{7,10},{8,11},{9,12},{10... | collective-permute-start | bytes 3145736 | tf_op jit(solution)/shard_map/ppermute | solution.py:16
  419.8 92.0 %collective-permute-start.6 = (bf16[2,128,2048]{2,1,0:T(8,128)(2,1)S(1)}, bf16[2,128,2048]{2,1,0:T(8,128)(2,1)S(1)}, u32[]{:S(2)}, u32[]{:S(2)}) collective-permute-start(bf16[2,128,2048]{2,1,0:T(8,128)(2,1)S(1)} %pad_maximum_fusion.1), channel_id=1, source_target_pairs={{0,2},{1,3},{2,4},{3,5},{4,6},{5,7},{6,8},{7,9},{8,10},{9,11},{10,... | collective-permute-start | bytes 3145736 | tf_op jit(solution)/shard_map/ppermute | solution.py:16
  1831.5 1206.5 %reduce-scatter.9.cloned.1.call-start = ((), (), s32[]{:S(2)}) async-start(), calls=%async_computation.13 | async-start | bytes 53477376 | tf_op jit(solution)/shard_map/reduce_scatter | solution.py:54
  1915.0 90.0 %collective-permute-start.15 = (bf16[2,128,2048]{2,1,0:T(8,128)(2,1)S(1)}, bf16[2,128,2048]{2,1,0:T(8,128)(2,1)S(1)}, u32[]{:S(2)}, u32[]{:S(2)}) collective-permute-start(bf16[2,128,2048]{2,1,0:T(8,128)(2,1)S(1)} %get-tuple-element.73), channel_id=1, source_target_pairs={{8,0},{9,1},{10,2},{11,3},{12,4},{13,5},{14,6},{15,7},{16,8},{17,9... | collective-permute-start | bytes 3145736 | tf_op jit(solution)/shard_map/ppermute | solution.py:16
  1916.3 90.0 %collective-permute-start.14 = (bf16[2,128,2048]{2,1,0:T(8,128)(2,1)S(1)}, bf16[2,128,2048]{2,1,0:T(8,128)(2,1)S(1)}, u32[]{:S(2)}, u32[]{:S(2)}) collective-permute-start(bf16[2,128,2048]{2,1,0:T(8,128)(2,1)S(1)} %get-tuple-element.74), channel_id=1, source_target_pairs={{7,0},{8,1},{9,2},{10,3},{11,4},{12,5},{13,6},{14,7},{15,8},{16,9}... | collective-permute-start | bytes 3145736 | tf_op jit(solution)/shard_map/ppermute | solution.py:16
  1917.6 116.8 %collective-permute-start.13 = (bf16[2,128,2048]{2,1,0:T(8,128)(2,1)}, bf16[2,128,2048]{2,1,0:T(8,128)(2,1)}, u32[]{:S(2)}, u32[]{:S(2)}) collective-permute-start(bf16[2,128,2048]{2,1,0:T(8,128)(2,1)} %get-tuple-element.75), channel_id=1, source_target_pairs={{6,0},{7,1},{8,2},{9,3},{10,4},{11,5},{12,6},{13,7},{14,8},{15,9},... | collective-permute-start | bytes 3145736 | tf_op jit(solution)/shard_map/ppermute | solution.py:16
  1918.9 115.5 %collective-permute-start.12 = (bf16[2,128,2048]{2,1,0:T(8,128)(2,1)}, bf16[2,128,2048]{2,1,0:T(8,128)(2,1)}, u32[]{:S(2)}, u32[]{:S(2)}) collective-permute-start(bf16[2,128,2048]{2,1,0:T(8,128)(2,1)} %get-tuple-element.76), channel_id=1, source_target_pairs={{5,0},{6,1},{7,2},{8,3},{9,4},{10,5},{11,6},{12,7},{13,8},{14,9},{... | collective-permute-start | bytes 3145736 | tf_op jit(solution)/shard_map/ppermute | solution.py:16
  2005.1 119.2 %collective-permute-start.10 = (bf16[2,128,2048]{2,1,0:T(8,128)(2,1)}, bf16[2,128,2048]{2,1,0:T(8,128)(2,1)}, u32[]{:S(2)}, u32[]{:S(2)}) collective-permute-start(bf16[2,128,2048]{2,1,0:T(8,128)(2,1)} %get-tuple-element.78), channel_id=1, source_target_pairs={{3,0},{4,1},{5,2},{6,3},{7,4},{8,5},{9,6},{10,7},{11,8},{12,9},{13... | collective-permute-start | bytes 3145736 | tf_op jit(solution)/shard_map/ppermute | solution.py:16
  2007.4 116.9 %collective-permute-start.9 = (bf16[2,128,2048]{2,1,0:T(8,128)(2,1)}, bf16[2,128,2048]{2,1,0:T(8,128)(2,1)}, u32[]{:S(2)}, u32[]{:S(2)}) collective-permute-start(bf16[2,128,2048]{2,1,0:T(8,128)(2,1)} %get-tuple-element.79), channel_id=1, source_target_pairs={{2,0},{3,1},{4,2},{5,3},{6,4},{7,5},{8,6},{9,7},{10,8},{11,9},{12,... | collective-permute-start | bytes 3145736 | tf_op jit(solution)/shard_map/ppermute | solution.py:16
  2155.0 2241.9 %reduce-scatter.17.cloned.1.call-start = ((), (), s32[]{:S(2)}) async-start(), calls=%async_computation.17 | async-start | bytes 71303168 | tf_op jit(solution)/shard_map/reduce_scatter | solution.py:56
  2180.1 3582.4 %reduce-scatter.15.cloned.1.call-start = ((), (), s32[]{:S(2)}) async-start(), calls=%async_computation.16 | async-start | bytes 71303168 | tf_op jit(solution)/shard_map/reduce_scatter | solution.py:55
  2205.1 4923.0 %reduce-scatter.13.cloned.1.call-start = ((), (), s32[]{:S(2)}) async-start(), calls=%async_computation.15 | async-start | bytes 71303168 | tf_op jit(solution)/shard_map/reduce_scatter | solution.py:54
  2229.8 4984.4 %reduce-scatter.19.cloned.1.call-start = ((), (), s32[]{:S(2)}) async-start(), calls=%async_computation.18 | async-start | bytes 1114112
  2231.9 5022.6 %all-reduce.7.cloned.1.call-start = ((), (), s32[]{:S(2)}) async-start(), calls=%async_computation.19 | async-start | bytes 16777216 | tf_op jit(solution)/shard_map/psum | solution.py:249
  (61 other events, 2924.7 us)
Sparse Core Ops, SparseCore 0:
  10.8 115.8 all-gather.11
  129.5 111.0 all-gather.15
  243.3 111.0 all-gather.13
  357.0 261.3 all-gather.17
  621.0 424.6 all-gather.19
  1048.3 349.0 all-gather.21
  1400.2 349.0 all-gather.23
  1831.6 481.6 reduce-scatter.10
  2319.3 718.6 reduce-scatter.8
  3040.3 1356.5 reduce-scatter.16
  4399.3 1363.1 reduce-scatter.14
  5764.8 1363.1 reduce-scatter.12
  7130.9 83.2 reduce-scatter.18
  7218.5 35.9 all-reduce.6
where the time goes:
time: 7290 us; the launch traced here: 7280 us
  waiting for transfers between devices  6550 us (90%)
  matrix products  332 us (5%)
  blocking collectives  153 us (2%)
  starting transfers between devices  99.6 us (1%)
    reduce_scatter x2, waiting for transfers between devices, reduce_three(): lax.psum_scatter(first_term, 'shard', scatter_dimension=0, tiled=True)  2080 us
    reduce_scatter x2, waiting for transfers between devices, reduce_three(): lax.psum_scatter(second_term, 'shard', scatter_dimension=0, tiled=True)  1440 us
    reduce_scatter x1, waiting for transfers between devices, reduce_three(): lax.psum_scatter(third_term, 'shard', scatter_dimension=0, tiled=True)  1360 us
    all_gather x1, waiting for transfers between devices, local(): lax.all_gather(w_gate, 'shard', axis=0, tiled=True)  422 us
    all_gather x1, waiting for transfers between devices, local(): lax.all_gather(w_up, 'shard', axis=0, tiled=True)  333 us
    all_gather x1, waiting for transfers between devices, local(): lax.all_gather(w_down, 'shard', axis=0, tiled=True)  331 us
    ppermute x16, waiting for transfers between devices, from_behind(): lax.ppermute(value, axis, [(source, source + steps) for source in range(l...  231 us
  transfers between devices with their start and end apart: 30, of which 21 were waited for; matrix products, arithmetic and copies ran while one was open for 5% of the time, Pallas kernels for 0%

commit v1 on v0

--- a/solution.py
+++ b/solution.py
@@ -3,6 +3,8 @@
 import jax
 import jax.numpy as jnp
 from jax import lax
+from jax.experimental import pallas as pl
+from jax.experimental.pallas import tpu as pltpu
 from jax.sharding import PartitionSpec as P
 
 HEADS = 16
@@ -57,7 +59,7 @@
     )
 
 
-def local(
+def local_general(
     inputs,
     positions,
     cotangent,
@@ -267,7 +269,507 @@
     )
 
 
+X, Y, Z, FAR = 1, 2, 4, 8
+AXIS = {Z: 0, Y: 1, X: 2}
+TRIPLE = ((X, Y, Z), (Y, Z, X), (Z, X, Y))
+CUTS = (0, 768, 1408, 2048)
+ROWS = 128
+SLOTS = 16
+WINDOW = 1152
+SCALING = 1.0 / math.sqrt(HEAD)
+
+
+def swap(value, bit):
+    return lax.ppermute(value, "shard", [(source, source ^ bit) for source in range(16)])
+
+
+def swap_core(value):
+    return lax.ppermute(value, "grp", [(0, 1), (1, 0)])
+
+
+def bit_of(bit):
+    return (lax.axis_index("shard") & bit) != 0
+
+
+def half(value, axis, number):
+    return lax.slice_in_dim(value, number, number + 1, axis=axis)
+
+
+def pick(value, axis, flag):
+    return jnp.where(flag, half(value, axis, 1), half(value, axis, 0))
+
+
+def ordered(mine, other, flag, axis):
+    return jnp.concatenate(
+        [jnp.where(flag, other, mine), jnp.where(flag, mine, other)], axis=axis
+    )
+
+
+def cube_gather(value):
+    pieces = []
+    for number, order in enumerate(TRIPLE):
+        part = value[:, CUTS[number] : CUTS[number + 1]][None, None, None]
+        for bit in order:
+            part = jnp.concatenate([part, swap(part, bit)], axis=AXIS[bit])
+        pieces.append(part)
+    full = jnp.concatenate(pieces, axis=-1)
+    return full.reshape(8 * value.shape[0], value.shape[1])
+
+
+def cube_scatter(value):
+    rows, width = value.shape[0] // 8, value.shape[1]
+    shaped = value.reshape(2, 2, 2, rows, width)
+    pieces = []
+    for number, order in enumerate(TRIPLE):
+        part = shaped[..., CUTS[number] : CUTS[number + 1]]
+        for bit in order:
+            part = part.astype(jnp.bfloat16)
+            came = swap(half(part, AXIS[bit], 1), bit)
+            part = half(part, AXIS[bit], 0).astype(jnp.float32) + came.astype(jnp.float32)
+        pieces.append(part.reshape(rows, -1))
+    return jnp.concatenate(pieces, axis=-1)
+
+
+def turn(value, order):
+    for bit in order:
+        axis, flag = AXIS[bit], bit_of(bit)
+        kept = pick(value, axis, flag)
+        came = swap(pick(value, axis, ~flag), bit)
+        value = ordered(kept, came, flag, axis)
+    return value
+
+
+def columns_weight(block, order):
+    rows, width = block.shape[1:]
+    turned = turn(block.reshape(2, 2, 2, rows, width), order)[None]
+    whole = ordered(turned, swap(turned, FAR), bit_of(FAR), 0)
+    return whole.reshape(16 * rows, width)
+
+
+def columns_grad(grad, order, core):
+    rows, width = grad.shape[0] // 16, grad.shape[1]
+    shaped = grad.reshape(2, 2, 2, 2, rows, width)
+    far = bit_of(FAR)
+    came = swap(pick(shaped, 0, ~far).astype(jnp.bfloat16), FAR)
+    summed = (pick(shaped, 0, far) + came.astype(jnp.float32)).astype(jnp.bfloat16)
+    turned = turn(summed[0], order)[None]
+    both = ordered(turned, swap_core(turned), core, 0)
+    return both.reshape(2, 8, rows, width)
+
+
+def add_up(value):
+    came = swap_core(value)
+    value = value + jnp.flip(came, 1)
+    for bit, axis in ((Z, 2), (Y, 3), (X, 4)):
+        value = value + jnp.flip(swap(value, bit), axis)
+    return value
+
+
+def visible_of(place):
+    row = lax.broadcasted_iota(jnp.int32, (ROWS, WINDOW), 0)
+    column = lax.broadcasted_iota(jnp.int32, (ROWS, WINDOW), 1)
+    distance = row - column + (WINDOW - ROWS)
+    return (distance >= 0) & (distance <= place)
+
+
+def dot_last(left, right):
+    return lax.dot_general(
+        left, right, (((1,), (1,)), ((), ())), preferred_element_type=jnp.float32
+    )
+
+
+def fill(me, source, before, target):
+    def put(number, carry):
+        group, place = number // 8, number % 8
+        slot = number ^ me
+        target[group, pl.ds(pl.multiple_of(place * ROWS, ROWS), ROWS), :] = before[slot]
+        target[group, pl.ds(pl.multiple_of((place + 8) * ROWS, ROWS), ROWS), :] = source[slot]
+        return carry
+
+    lax.fori_loop(0, SLOTS, put, 0)
+
+
+def attend_kernel(me_ref, q_ref, k_ref, v_ref, pk_ref, pv_ref, pos_ref, o_ref, lse_ref, keys, values):
+    me = me_ref[0]
+    fill(me, k_ref, pk_ref, keys)
+    fill(me, v_ref, pv_ref, values)
+
+    def step(slot, carry):
+        number = slot ^ me
+        group, place = number // 8, number % 8
+        rows = pl.ds(pl.multiple_of(place * ROWS, ROWS), WINDOW)
+        scores = dot_last(q_ref[slot], keys[group, rows, :]) * SCALING
+        masked = jnp.where(visible_of(pos_ref[slot]), scores, -jnp.inf)
+        top = jnp.max(masked, axis=-1, keepdims=True)
+        expo = jnp.exp(masked - top)
+        total = jnp.sum(expo, axis=-1, keepdims=True)
+        probs = (expo / total).astype(jnp.bfloat16)
+        mixed = jnp.dot(probs, values[group, rows, :], preferred_element_type=jnp.float32)
+        o_ref[slot] = mixed.astype(jnp.bfloat16)
+        lse_ref[slot] = top + jnp.log(total)
+        return carry
+
+    lax.fori_loop(0, SLOTS, step, 0)
+
+
+def attend_back_kernel(
+    me_ref,
+    q_ref,
+    k_ref,
+    v_ref,
+    pk_ref,
+    pv_ref,
+    pos_ref,
+    lse_ref,
+    do_ref,
+    dq_ref,
+    dk_ref,
+    dv_ref,
+    dpk_ref,
+    dpv_ref,
+    keys,
+    values,
+    d_keys,
+    d_values,
+):
+    me = me_ref[0]
+    fill(me, k_ref, pk_ref, keys)
+    fill(me, v_ref, pv_ref, values)
+    d_keys[...] = jnp.zeros_like(d_keys)
+    d_values[...] = jnp.zeros_like(d_values)
+
+    def step(slot, carry):
+        number = slot ^ me
+        group, place = number // 8, number % 8
+        rows = pl.ds(pl.multiple_of(place * ROWS, ROWS), WINDOW)
+        query, grad = q_ref[slot], do_ref[slot]
+        key, value = keys[group, rows, :], values[group, rows, :]
+        scores = dot_last(query, key) * SCALING
+        probs = jnp.where(visible_of(pos_ref[slot]), jnp.exp(scores - lse_ref[slot]), 0.0)
+        d_probs = dot_last(grad, value)
+        inner = jnp.sum(probs * d_probs, axis=-1, keepdims=True)
+        d_scores = (probs * (d_probs - inner) * SCALING).astype(jnp.bfloat16)
+        dq_ref[slot] = jnp.dot(d_scores, key, preferred_element_type=jnp.float32)
+        d_keys[group, rows, :] += along_first(d_scores, query)
+        d_values[group, rows, :] += along_first(probs.astype(jnp.bfloat16), grad)
+        return carry
+
+    lax.fori_loop(0, SLOTS, step, 0)
+
+    def take(number, carry):
+        group, place = number // 8, number % 8
+        slot = number ^ me
+        before = pl.ds(pl.multiple_of(place * ROWS, ROWS), ROWS)
+        own = pl.ds(pl.multiple_of((place + 8) * ROWS, ROWS), ROWS)
+        dpk_ref[slot] = d_keys[group, before, :].astype(jnp.bfloat16)
+        dpv_ref[slot] = d_values[group, before, :].astype(jnp.bfloat16)
+        dk_ref[slot] = d_keys[group, own, :]
+        dv_ref[slot] = d_values[group, own, :]
+        return carry
+
+    lax.fori_loop(0, SLOTS, take, 0)
+
+
+def in_vmem(count):
+    return [pl.BlockSpec(memory_space=pltpu.SMEM)] + [pl.BlockSpec(memory_space=pltpu.VMEM)] * count
+
+
+def attend(me, query, key, value, key_before, value_before, place):
+    shape = (SLOTS, ROWS, HEAD)
+    return pl.pallas_call(
+        attend_kernel,
+        out_shape=(
+            jax.ShapeDtypeStruct(shape, jnp.bfloat16),
+            jax.ShapeDtypeStruct((SLOTS, ROWS, 1), jnp.float32),
+        ),
+        in_specs=in_vmem(6),
+        out_specs=[pl.BlockSpec(memory_space=pltpu.VMEM)] * 2,
+        scratch_shapes=[pltpu.VMEM((2, 2048, HEAD), jnp.bfloat16)] * 2,
+        compiler_params=pltpu.CompilerParams(vmem_limit_bytes=40 * 2**20),
+        cost_estimate=pl.CostEstimate(
+            flops=4 * 2048 * WINDOW * HEAD,
+            bytes_accessed=6 * 2**20,
+            transcendentals=2048 * WINDOW,
+        ),
+    )(me, query, key, value, key_before, value_before, place)
+
+
+def attend_back(me, query, key, value, key_before, value_before, place, lse, grad):
+    shape = (SLOTS, ROWS, HEAD)
+    wide = jax.ShapeDtypeStruct(shape, jnp.float32)
+    narrow = jax.ShapeDtypeStruct(shape, jnp.bfloat16)
+    return pl.pallas_call(
+        attend_back_kernel,
+        out_shape=(wide, wide, wide, narrow, narrow),
+        in_specs=in_vmem(8),
+        out_specs=[pl.BlockSpec(memory_space=pltpu.VMEM)] * 5,
+        scratch_shapes=[pltpu.VMEM((2, 2048, HEAD), jnp.bfloat16)] * 2
+        + [pltpu.VMEM((2, 2048, HEAD), jnp.float32)] * 2,
+        compiler_params=pltpu.CompilerParams(vmem_limit_bytes=40 * 2**20),
+        cost_estimate=pl.CostEstimate(
+            flops=10 * 2048 * WINDOW * HEAD,
+            bytes_accessed=12 * 2**20,
+            transcendentals=2048 * WINDOW,
+        ),
+    )(me, query, key, value, key_before, value_before, place, lse, grad)
+
+
+def local_cube(
+    inputs,
+    positions,
+    cotangent,
+    w_query,
+    w_key,
+    w_value,
+    w_out,
+    query_gain,
+    key_gain,
+    attn_gain,
+    w_gate,
+    w_up,
+    w_down,
+    mlp_gain,
+):
+    bf16, f32 = jnp.bfloat16, jnp.float32
+    width = inputs.shape[1]
+    core_index = lax.axis_index("grp")
+    shard_index = lax.axis_index("shard")
+    core = core_index == 1
+    far = bit_of(FAR)
+    cube_index = shard_index % 8
+    me = (core_index * 8 + cube_index).astype(jnp.int32).reshape(1)
+    head = core_index * 8 + cube_index
+    hidden = w_down.shape[0]
+
+    def with_other(own):
+        return own, swap_core(own)
+
+    def head_columns(weight, order):
+        blocks = weight.reshape(ROWS, 2, 8, HEAD).transpose(1, 2, 0, 3)
+        return columns_weight(pick(blocks, 0, core)[0], order)
+
+    def hidden_columns(weight, order):
+        part = hidden // 2
+        blocks = weight.reshape(ROWS, 2, 8, 2, part).transpose(3, 2, 0, 1, 4)
+        return columns_weight(pick(blocks, 0, core)[0].reshape(8, ROWS, 2 * part), order)
+
+    key_w = head_columns(w_key, TRIPLE[0])
+    value_w = head_columns(w_value, TRIPLE[1])
+    query_w = head_columns(w_query, TRIPLE[2])
+    qkv_w = jnp.concatenate([query_w, key_w, value_w], axis=1)
+    gate_w = hidden_columns(w_gate, TRIPLE[0])
+    up_w = hidden_columns(w_up, TRIPLE[1])
+    down_own = pick(w_down.reshape(2, hidden // 2, width), 0, core)
+    down_w = ordered(down_own, swap(down_own, FAR), far, 0).reshape(hidden, width)
+    to_far = [(s, s + 8) for s in range(8)] + [(24 + s, 16 + s) for s in range(8)]
+    out_came = lax.ppermute(w_out, ("grp", "shard"), to_far)
+    out_w = jnp.where(core == far, w_out, out_came)
+
+    gains = jnp.stack([query_gain, key_gain, attn_gain, mlp_gain])[None]
+    for bit in (X, Y, Z, FAR):
+        gains = ordered(gains, swap(gains, bit), bit_of(bit), 0)
+    gains = gains.astype(f32)
+    head_gain = lax.dynamic_index_in_dim(gains, head, 0, keepdims=False)[:2]
+    gains = gains.transpose(1, 0, 2).reshape(4, width)
+
+    place = positions.reshape(1, 1, 1, ROWS)
+    for bit in (X, Y, Z):
+        place = jnp.concatenate([place, swap(place, bit)], axis=AXIS[bit])
+    place = jnp.concatenate([place[None], swap_core(place)[None]], axis=0).reshape(SLOTS, ROWS, 1)
+
+    middle = HEAD // 2
+    frequency = jnp.power(500000.0, -2.0 * jnp.arange(middle).astype(f32) / HEAD)
+    angles = place.astype(f32).reshape(SLOTS * ROWS, 1) * frequency[None, :]
+    cosines = jnp.cos(angles)
+    sines = jnp.sin(angles)
+    cosines = jnp.concatenate([cosines, cosines], axis=1)
+    sines = jnp.concatenate([-sines, sines], axis=1)
+
+    def rotated(values):
+        return values * cosines + jnp.roll(values, middle, axis=1) * sines
+
+    def rotated_back(values):
+        return values * cosines - jnp.roll(values, middle, axis=1) * sines
+
+    def row_sums(first, second):
+        sums = jnp.stack([jnp.sum(first, axis=-1), jnp.sum(second, axis=-1)])
+        total = add_up(sums.reshape(2, 2, 2, 2, 2, ROWS))
+        return total.reshape(2, SLOTS * ROWS, 1) / width
+
+    x_own, x_other = with_other(cube_gather(inputs))
+    raw = jnp.concatenate(
+        [
+            jnp.dot(x_own, qkv_w, preferred_element_type=f32),
+            jnp.dot(x_other, qkv_w, preferred_element_type=f32),
+        ]
+    )
+    q_raw, k_raw, v_raw = raw[:, :HEAD], raw[:, HEAD : 2 * HEAD], raw[:, 2 * HEAD :]
+    means = row_sums(q_raw * q_raw, k_raw * k_raw)
+    q_scale, k_scale = lax.rsqrt(means[0] + 1e-06), lax.rsqrt(means[1] + 1e-06)
+    shape = (SLOTS, ROWS, HEAD)
+    query = rotated(q_raw * q_scale * head_gain[0]).astype(bf16).reshape(shape)
+    key = rotated(k_raw * k_scale * head_gain[1]).astype(bf16).reshape(shape)
+    value = v_raw.astype(bf16).reshape(shape)
+
+    onward = [(s, s + 8) for s in range(8)]
+    backward = [(s + 8, s) for s in range(8)]
+
+    def before(values):
+        own, other = values[:8], values[8:]
+        first, second = jnp.where(core, other, own), jnp.where(core, own, other)
+        came_first = swap(first, FAR)
+        came_second = lax.ppermute(second, "shard", onward)
+        second = jnp.where(far, came_second, came_first)
+        return jnp.concatenate(
+            [jnp.where(core, second, came_first), jnp.where(core, came_first, second)]
+        )
+
+    def after(values):
+        own, other = values[:8], values[8:]
+        first, second = jnp.where(core, other, own), jnp.where(core, own, other)
+        came_first = swap(jnp.where(far, first, second), FAR)
+        came_second = lax.ppermute(second, "shard", backward)
+        return jnp.concatenate(
+            [jnp.where(core, came_second, came_first), jnp.where(core, came_first, came_second)]
+        )
+
+    value_before = before(value)
+    key_before = before(key)
+    mixed, lse = attend(me, query, key, value, key_before, value_before, place)
+    mixed = mixed.reshape(SLOTS * ROWS, HEAD)
+    block = 8 * ROWS
+
+    def reduce_rows(other_part, own_part):
+        came = swap_core(other_part.astype(bf16))
+        return cube_scatter((own_part + came.astype(f32)).astype(bf16))
+
+    branch = reduce_rows(
+        jnp.dot(mixed[block:], out_w, preferred_element_type=f32),
+        jnp.dot(mixed[:block], out_w, preferred_element_type=f32),
+    )
+    branch_scale = lax.rsqrt(jnp.mean(branch * branch, axis=-1, keepdims=True) + 1e-06)
+    hidden_state = inputs.astype(f32) + branch * branch_scale * gains[2]
+    state_low = hidden_state.astype(bf16)
+
+    state = with_other(cube_gather(state_low))
+    gate = [jnp.dot(part, gate_w, preferred_element_type=f32) for part in state]
+    up = [jnp.dot(part, up_w, preferred_element_type=f32) for part in state]
+    active = [(jax.nn.silu(g) * u).astype(bf16) for g, u in zip(gate, up)]
+    mlp = reduce_rows(
+        jnp.dot(active[1], down_w, preferred_element_type=f32),
+        jnp.dot(active[0], down_w, preferred_element_type=f32),
+    )
+    mlp_scale = lax.rsqrt(jnp.mean(mlp * mlp, axis=-1, keepdims=True) + 1e-06)
+    output = (hidden_state + mlp * mlp_scale * gains[3]).astype(bf16)
+
+    cot = cotangent.astype(f32)
+    mlp_gain_part = jnp.sum(cot * mlp * mlp_scale, axis=0)
+    scaled = cot * gains[3]
+    d_mlp = mlp_scale * scaled - mlp * mlp_scale**3 * jnp.mean(mlp * scaled, axis=-1, keepdims=True)
+    d_mlp = with_other(cube_gather(d_mlp.astype(bf16)))
+    d_gate, d_up = [], []
+    for part, g, u in zip(d_mlp, gate, up):
+        d_active = along_last(part, down_w)
+        sigma = jax.nn.sigmoid(g)
+        d_gate.append((d_active * u * sigma * (1.0 + g * (1.0 - sigma))).astype(bf16))
+        d_up.append((d_active * g * sigma).astype(bf16))
+    d_state = reduce_rows(
+        along_last(d_gate[1], gate_w) + along_last(d_up[1], up_w),
+        along_last(d_gate[0], gate_w) + along_last(d_up[0], up_w),
+    )
+
+    def over_tokens(left, right):
+        return along_first(left[0], right[0]) + along_first(left[1], right[1])
+
+    down_grad = over_tokens(active, d_mlp).reshape(2, hidden // 2, width)
+    came = swap(pick(down_grad, 0, ~far).astype(bf16), FAR)
+    down_part = (pick(down_grad, 0, far) + came.astype(f32)).astype(bf16)
+    down_grad = ordered(down_part, swap_core(down_part), core, 0).reshape(hidden, width).astype(f32)
+
+    def hidden_grad(grad, order):
+        both = columns_grad(grad, order, core).reshape(2, 8, ROWS, 2, hidden // 2)
+        return both.transpose(2, 3, 1, 0, 4).reshape(ROWS, -1).astype(f32)
+
+    gate_grad = hidden_grad(over_tokens(state, d_gate), TRIPLE[0])
+    up_grad = hidden_grad(over_tokens(state, d_up), TRIPLE[1])
+
+    d_resid = cot + d_state
+    attn_gain_part = jnp.sum(d_resid * branch * branch_scale, axis=0)
+    scaled = d_resid * gains[2]
+    d_branch = branch_scale * scaled - branch * branch_scale**3 * jnp.mean(
+        branch * scaled, axis=-1, keepdims=True
+    )
+    d_branch = with_other(cube_gather(d_branch.astype(bf16)))
+    d_mixed = jnp.concatenate([along_last(part, out_w).astype(bf16) for part in d_branch])
+    d_query, d_key, d_value, d_key_before, d_value_before = attend_back(
+        me, query, key, value, key_before, value_before, place, lse, d_mixed.reshape(shape)
+    )
+    flat = (SLOTS * ROWS, HEAD)
+    d_value = (d_value + after(d_value_before).astype(f32)).reshape(flat)
+    d_key = (d_key + after(d_key_before).astype(f32)).reshape(flat)
+    d_query = rotated_back(d_query.reshape(flat))
+    d_key = rotated_back(d_key)
+    query_gain_part = jnp.sum(d_query * q_raw * q_scale, axis=0)
+    key_gain_part = jnp.sum(d_key * k_raw * k_scale, axis=0)
+    d_query = d_query * head_gain[0]
+    d_key = d_key * head_gain[1]
+    means = row_sums(d_query * q_raw, d_key * k_raw)
+    d_query = d_query * q_scale - q_raw * q_scale**3 * means[0]
+    d_key = d_key * k_scale - k_raw * k_scale**3 * means[1]
+    d_qkv = jnp.concatenate([d_query, d_key, d_value], axis=1).astype(bf16)
+    d_inputs = reduce_rows(along_last(d_qkv[block:], qkv_w), along_last(d_qkv[:block], qkv_w))
+    input_grad = d_resid + d_inputs
+
+    qkv_grad = over_tokens((x_own, x_other), (d_qkv[:block], d_qkv[block:]))
+
+    def head_grad(grad, order):
+        both = columns_grad(grad, order, core)
+        return both.transpose(2, 0, 1, 3).reshape(ROWS, -1).astype(f32)
+
+    query_grad = head_grad(qkv_grad[:, :HEAD], TRIPLE[0])
+    key_grad = head_grad(qkv_grad[:, HEAD : 2 * HEAD], TRIPLE[1])
+    value_grad = head_grad(qkv_grad[:, 2 * HEAD :], TRIPLE[2])
+
+    out_grad = over_tokens((mixed[:block], mixed[block:]), d_branch)
+    to_owner = [(s + 8, s) for s in range(8)] + [(16 + s, 24 + s) for s in range(8)]
+    out_grad = (
+        out_grad + lax.ppermute(out_grad.astype(bf16), ("grp", "shard"), to_owner).astype(f32)
+    ).astype(bf16)
+    to_core = [(s, 16 + s) for s in range(8)] + [(24 + s, 8 + s) for s in range(8)]
+    out_came = lax.ppermute(out_grad, ("grp", "shard"), to_core)
+    out_grad = jnp.where(core == far, out_grad, out_came).astype(f32)
+
+    gain_part = jnp.stack([query_gain_part, key_gain_part])
+    gain_part = gain_part + swap(gain_part, FAR)
+    gain_came = swap_core(gain_part)
+    head_grads = jnp.where(core == far, gain_part, gain_came)
+    norm_part = jnp.stack([attn_gain_part, mlp_gain_part])
+    norm_part = norm_part + swap_core(norm_part)
+    norm_part = norm_part.reshape(2, 2, 2, 2, 2, ROWS)
+    for bit, axis in ((FAR, 1), (Z, 2), (Y, 3), (X, 4)):
+        flag = bit_of(bit)
+        norm_part = pick(norm_part, axis, flag) + swap(pick(norm_part, axis, ~flag), bit)
+    norm_grads = norm_part.reshape(2, ROWS)
+
+    return (
+        output,
+        input_grad,
+        query_grad,
+        key_grad,
+        value_grad,
+        out_grad,
+        head_grads[0],
+        head_grads[1],
+        norm_grads[0],
+        gate_grad,
+        up_grad,
+        down_grad,
+        norm_grads[1],
+    )
+
+
 def solution(mesh):
+    in_cube = mesh.shape["grp"] == 2 and mesh.shape["shard"] == 16
     placed = (
         P(("grp", "shard"), None),
         P(("grp", "shard")),
@@ -285,7 +787,7 @@
         P("shard"),
     )
     return jax.shard_map(
-        local,
+        local_cube if in_cube else local_general,
         mesh=mesh,
         in_specs=placed,
         out_specs=(

time: 7290 us -> 1110 us (0.15)
  waiting for transfers between devices: 6550 us -> 593 us
  matrix products: 332 us -> 102 us
  blocking collectives: 153 us -> 0 us
  starting transfers between devices: 99.6 us -> 192 us
    reduce_scatter x5 -> x0, waiting for transfers between devices: 4880 us -> none  [the longest x2 2080 us: reduce_three(): lax.psum_scatter(first_term, 'shard', scatter_dimension=0, tiled=True)]
    all_gather x7 -> x0, waiting for transfers between devices: 1330 us -> none  [the longest x1 422 us: local(): lax.all_gather(w_gate, 'shard', axis=0, tiled=True)]
    ppermute x16 -> x162, waiting for transfers between devices: 231 us -> 593 us  [the longest x136 552 us: swap(): lax.ppermute(value, 'shard', [(source, source ^ bit) for source in range(...]
    all_gather x4 -> x0, blocking collectives: 151 us -> none  [the longest x1 42.4 us: local(): lax.all_gather(query_gain, 'shard', axis=0, tiled=True)]
    dot_general x13 -> x10, matrix products: 154 us -> 24.7 us  [the longest x2 7.83 us: local_cube(): up = [jnp.dot(part, up_w, preferred_element_type=f32) for part in state]]
    ppermute x16 -> x162, starting transfers between devices: 98.8 us -> 192 us  [the longest x136 172 us: swap(): lax.ppermute(value, 'shard', [(source, source ^ bit) for source in range(...]
  transfers between devices with their start and end apart: 30 -> 162, of which waited for: 21 -> 106; matrix products, arithmetic and copies ran while one was open for 5% -> 20% of each run, Pallas kernels for 0% -> 0%
where the time goes in v1:
time: 1110 us; the launch traced here: 1100 us
  waiting for transfers between devices  593 us (53%)
  starting transfers between devices  192 us (17%)
  matrix products  102 us (9%)
  other arithmetic  91.5 us (8%)
  local copies, waits for them, and re-layouts  86.5 us (8%)
  Pallas kernels  26 us (2%)
    ppermute x136, waiting for transfers between devices, swap(): lax.ppermute(value, 'shard', [(source, source ^ bit) for source in range(...  552 us
    ppermute x136, starting transfers between devices, swap(): lax.ppermute(value, 'shard', [(source, source ^ bit) for source in range(...  172 us
    dot_general x10, matrix products, along_last(): lax.dot_general(left, right, (((1,), (1,)), ((), ())), preferred_element_...  45.1 us
    convert_element_type x6, local copies, waits for them, and re-layouts, hidden_grad(): return both.transpose(2, 3, 1, 0, 4).reshape(ROWS, -1).astype(f32)  39.9 us
    dot_general x10, matrix products, along_first(): lax.dot_general(left, right, (((0,), (0,)), ((), ())), preferred_element_...  32.5 us
    ppermute x2, waiting for transfers between devices, after(): came_second = lax.ppermute(second, 'shard', backward)  26.8 us
  transfers between devices with their start and end apart: 162, of which 106 were waited for; matrix products, arithmetic and copies ran while one was open for 20% of the time, Pallas kernels for 0%

profile of v1, /device:TPU:0, one launch (start us, length us, event | category | flops | bytes accessed | tf_op | source)
XLA Modules:
  0.0 1097.0 jit_solution(13020282298612387047)
XLA Ops:
  94.4 19.8 %collective-permute-done.12 = bf16[1,2,2,2,128,128]{5,4,3,2,1,0:T(8,128)(2,1)S(1)} collective-permute-done((bf16[1,2,2,2,128,128]{5,4,3,2,1,0:T(8,128)(2,1)S(1)}, bf16[1,2,2,2,128,128]{5,4,3,2,1,0:T(8,128)(2,1)S(1)}, u32[]{:S(2)}, u32[]{:S(2)}) %collective-permute-start.12) | collective-permute-done | bytes 262176 | tf_op jit(solution)/shard_map/ppermute | solution.py:283
  155.3 9.4 collective-permute-done.37
  170.1 11.7 %shard_map.237 = (bf16[16,128,128]{2,1,0:T(8,128)(2,1)S(1)}, f32[16,128,1]{2,1,0:T(8,128)S(1)}) custom-call(s32[1]{0:T(128)} %bitcast.me_ref, bf16[16,128,128]{2,1,0:T(8,128)(2,1)S(1)} %bitcast.328, bf16[16,128,128]{2,1,0:T(8,128)(2,1)S(1)} %bitcast.326, bf16[16,128,128]{2,1,0:T(8,128)(2,1)S(1)} %bitcast.330, ...), custom_call_target="tpu_custom_call" | custom-call | flops 1207959552 | bytes 6291456 | tf_op jit(solution)/shard_map/pallas_call | solution.py:479
  194.4 20.3 %collective-permute-start.46 = (bf16[1,2,2,128,640]{4,3,2,1,0:T(8,128)(2,1)}, bf16[1,2,2,128,640]{4,3,2,1,0:T(8,128)(2,1)}, u32[]{:S(2)}, u32[]{:S(2)}) collective-permute-start(bf16[1,2,2,128,640]{4,3,2,1,0:T(8,128)(2,1)} %slice.1078), channel_id=1, source_target_pairs={{0,4},{1,5},{2,6},{3,7},{4,0},{5,1},{6,2},{7,3},{8,12},{9,13},{10,... | collective-permute-start | bytes 1966088 | tf_op jit(solution)/shard_map/ppermute | solution.py:283
  256.9 7.9 broadcast_select_fusion
  266.8 13.1 %reshape_reshape_squeeze.6 = bf16[2,2,2,128,512]{4,3,2,1,0:T(8,128)(2,1)} reshape(bf16[1,8,128,2,256]{4,3,2,1,0:T(2,128)(2,1)} %copy.43) | data formatting | bytes 2097152 | tf_op jit(solution)/shard_map/reshape;reshape;squeeze | solution.py:344
  331.8 26.0 %collective-permute-done.63 = bf16[1,2,2,128,512]{4,3,2,1,0:T(8,128)(2,1)S(1)} collective-permute-done((bf16[1,2,2,128,512]{4,3,2,1,0:T(8,128)(2,1)S(1)}, bf16[1,2,2,128,512]{4,3,2,1,0:T(8,128)(2,1)S(1)}, u32[]{:S(2)}, u32[]{:S(2)}) %collective-permute-start.63) | collective-permute-done | bytes 524320 | tf_op jit(solution)/shard_map/ppermute | solution.py:283
  369.0 46.4 %collective-permute-done.66 = bf16[1,256,2048]{2,1,0:T(8,128)(2,1)S(1)} collective-permute-done((bf16[1,256,2048]{2,1,0:T(8,128)(2,1)S(1)}, bf16[1,256,2048]{2,1,0:T(8,128)(2,1)S(1)}, u32[]{:S(2)}, u32[]{:S(2)}) %collective-permute-start.66) | collective-permute-done | bytes 1048608 | tf_op jit(solution)/shard_map/ppermute | solution.py:283
  415.9 22.1 %collective-permute-done.61 = bf16[1,2,2,2,128,512]{5,4,3,2,1,0:T(8,128)(2,1)S(1)} collective-permute-done((bf16[1,2,2,2,128,512]{5,4,3,2,1,0:T(8,128)(2,1)S(1)}, bf16[1,2,2,2,128,512]{5,4,3,2,1,0:T(8,128)(2,1)S(1)}, u32[]{:S(2)}, u32[]{:S(2)}) %collective-permute-start.61) | collective-permute-done | bytes 1048608 | tf_op jit(solution)/shard_map/ppermute | solution.py:283
  438.3 21.5 %collective-permute-done.65 = bf16[1,2,2,2,128,512]{5,4,3,2,1,0:T(8,128)(2,1)S(1)} collective-permute-done((bf16[1,2,2,2,128,512]{5,4,3,2,1,0:T(8,128)(2,1)S(1)}, bf16[1,2,2,2,128,512]{5,4,3,2,1,0:T(8,128)(2,1)S(1)}, u32[]{:S(2)}, u32[]{:S(2)}) %collective-permute-start.65) | collective-permute-done | bytes 1048608 | tf_op jit(solution)/shard_map/ppermute | solution.py:283
  481.3 14.4 %collective-permute-done.72 = bf16[2,1,2,128,640]{4,3,2,1,0:T(8,128)(2,1)S(1)} collective-permute-done((bf16[2,1,2,128,640]{4,3,2,1,0:T(8,128)(2,1)S(1)}, bf16[2,1,2,128,640]{4,3,2,1,0:T(8,128)(2,1)S(1)}, u32[]{:S(2)}, u32[]{:S(2)}) %collective-permute-start.72) | collective-permute-done | bytes 655392 | tf_op jit(solution)/shard_map/ppermute | solution.py:283
  542.6 8.3 collective-permute-done.83
  601.7 7.8 add_convert_fusion.2
  610.0 75.2 %collective-permute-done.160 = bf16[1,256,2048]{2,1,0:T(8,128)(2,1)S(1)} collective-permute-done((bf16[1,256,2048]{2,1,0:T(8,128)(2,1)S(1)}, bf16[1,256,2048]{2,1,0:T(8,128)(2,1)S(1)}, u32[]{:S(2)}, u32[]{:S(2)}) %collective-permute-start.160) | collective-permute-done | bytes 1048608 | tf_op jit(solution)/shard_map/ppermute | solution.py:283
  686.0 21.7 %collective-permute-done.155 = bf16[1,2,2,2,128,512]{5,4,3,2,1,0:T(8,128)(2,1)S(1)} collective-permute-done((bf16[1,2,2,2,128,512]{5,4,3,2,1,0:T(8,128)(2,1)S(1)}, bf16[1,2,2,2,128,512]{5,4,3,2,1,0:T(8,128)(2,1)S(1)}, u32[]{:S(2)}, u32[]{:S(2)}) %collective-permute-start.155) | collective-permute-done | bytes 1048608 | tf_op jit(solution)/shard_map/ppermute | solution.py:283
  709.2 20.5 %collective-permute-done.150 = bf16[1,2,2,2,128,512]{5,4,3,2,1,0:T(8,128)(2,1)S(1)} collective-permute-done((bf16[1,2,2,2,128,512]{5,4,3,2,1,0:T(8,128)(2,1)S(1)}, bf16[1,2,2,2,128,512]{5,4,3,2,1,0:T(8,128)(2,1)S(1)}, u32[]{:S(2)}, u32[]{:S(2)}) %collective-permute-start.150) | collective-permute-done | bytes 1048608 | tf_op jit(solution)/shard_map/ppermute | solution.py:283
  734.2 9.6 collective-permute-done.151
  756.9 14.9 %collective-permute-done.92 = bf16[2,1,2,128,640]{4,3,2,1,0:T(8,128)(2,1)S(1)} collective-permute-done((bf16[2,1,2,128,640]{4,3,2,1,0:T(8,128)(2,1)S(1)}, bf16[2,1,2,128,640]{4,3,2,1,0:T(8,128)(2,1)S(1)}, u32[]{:S(2)}, u32[]{:S(2)}) %collective-permute-start.92) | collective-permute-done | bytes 655392 | tf_op jit(solution)/shard_map/ppermute | solution.py:283
  812.8 8.0 collective-permute-done.105
  907.0 14.3 %shard_map.238 = (f32[16,128,128]{2,1,0:T(8,128)S(1)}, f32[16,128,128]{2,1,0:T(8,128)S(1)}, f32[16,128,128]{2,1,0:T(8,128)S(1)}, bf16[16,128,128]{2,1,0:T(8,128)(2,1)S(1)}, bf16[16,128,128]{2,1,0:T(8,128)(2,1)S(1)}) custom-call(s32[1]{0:T(128)} %bitcast.me_ref, bf16[16,128,128]{2,1,0:T(8,128)(2,1)S(1)} %bitcast.329, bf16[16,128,128]{2,1,0:T(8,128)(2,1)S(1)} %bitcast.327, ...), custom_call_target="tpu_custom_call" | custom-call | flops 3019898880 | bytes 12582912 | tf_op jit(solution)/shard_map/pallas_call | solution.py:501
  941.2 17.4 %collective-permute-done.108 = bf16[8,128,128]{2,1,0:T(8,128)(2,1)S(1)} collective-permute-done((bf16[8,128,128]{2,1,0:T(8,128)(2,1)S(1)}, bf16[8,128,128]{2,1,0:T(8,128)(2,1)S(1)}, u32[]{:S(2)}, u32[]{:S(2)}) %collective-permute-start.108) | collective-permute-done | bytes 262176 | tf_op jit(solution)/shard_map/ppermute | solution.py:631
  968.3 9.4 collective-permute-done.114
  1011.4 12.7 %collective-permute-done.136 = bf16[1,2,2,2,128,128]{5,4,3,2,1,0:T(8,128)(2,1)S(1)} collective-permute-done((bf16[1,2,2,2,128,128]{5,4,3,2,1,0:T(8,128)(2,1)S(1)}, bf16[1,2,2,2,128,128]{5,4,3,2,1,0:T(8,128)(2,1)S(1)}, u32[]{:S(2)}, u32[]{:S(2)}) %collective-permute-start.136) | collective-permute-done | bytes 262176 | tf_op jit(solution)/shard_map/ppermute | solution.py:283
  1062.3 10.0 collective-permute-done.120
  (919 shorter events, 649.8 us)
Async XLA Ops:
  2.2 54.8 %collective-permute-start.9 = (bf16[1,2,2,128,128]{4,3,2,1,0:T(8,128)(2,1)S(1)}, bf16[1,2,2,128,128]{4,3,2,1,0:T(8,128)(2,1)S(1)}, u32[]{:S(2)}, u32[]{:S(2)}) collective-permute-start(bf16[1,2,2,128,128]{4,3,2,1,0:T(8,128)(2,1)S(1)} %bitcast.454), channel_id=1, source_target_pairs={{0,4},{1,5},{2,6},{3,7},{4,0},{5,1},{6,2},{7,3},{8,12},{9,13},{10,... | collective-permute-start | bytes 393224 | tf_op jit(solution)/shard_map/ppermute | solution.py:283
  7.2 51.5 %collective-permute-start.13 = (bf16[2,2,1,128,128]{4,3,2,1,0:T(8,128)(2,1)}, bf16[2,2,1,128,128]{4,3,2,1,0:T(8,128)(2,1)}, u32[]{:S(2)}, u32[]{:S(2)}) collective-permute-start(bf16[2,2,1,128,128]{4,3,2,1,0:T(8,128)(2,1)} %broadcast_select_fusion.110), channel_id=1, source_target_pairs={{0,1},{1,0},{2,3},{3,2},{4,5},{5,4},{6,7},{7,6},{8,9},{9,8},{10,11... | collective-permute-start | bytes 393224 | tf_op jit(solution)/shard_map/ppermute | solution.py:283
  58.7 73.8 %collective-permute-start.38 = (bf16[128,2048]{1,0:T(8,128)(2,1)S(1)}, bf16[128,2048]{1,0:T(8,128)(2,1)S(1)}, u32[]{:S(2)}, u32[]{:S(2)}) collective-permute-start(bf16[128,2048]{1,0:T(8,128)(2,1)S(1)} %copy-done.82), channel_id=1, source_target_pairs={{0,8},{1,9},{2,10},{3,11},{4,12},{5,13},{6,14},{7,15},{24,16},{25,... | collective-permute-start | bytes 1572872 | tf_op jit(solution)/shard_map/ppermute | solution.py:565
  78.7 48.4 %collective-permute-start.21 = (bf16[1024,2048]{1,0:T(8,128)(2,1)S(1)}, bf16[1024,2048]{1,0:T(8,128)(2,1)S(1)}, u32[]{:S(2)}, u32[]{:S(2)}) collective-permute-start(bf16[1024,2048]{1,0:T(8,128)(2,1)S(1)} %bitcast.356), channel_id=1, source_target_pairs={{0,16},{16,0},{1,17},{17,1},{2,18},{18,2},{3,19},{19,3},{4,20},{20... | collective-permute-start | bytes 12582920 | tf_op jit(solution)/shard_map/ppermute | solution.py:287
  194.4 37.2 %collective-permute-start.46 = (bf16[1,2,2,128,640]{4,3,2,1,0:T(8,128)(2,1)}, bf16[1,2,2,128,640]{4,3,2,1,0:T(8,128)(2,1)}, u32[]{:S(2)}, u32[]{:S(2)}) collective-permute-start(bf16[1,2,2,128,640]{4,3,2,1,0:T(8,128)(2,1)} %slice.1078), channel_id=1, source_target_pairs={{0,4},{1,5},{2,6},{3,7},{4,0},{5,1},{6,2},{7,3},{8,12},{9,13},{10,... | collective-permute-start | bytes 1966088 | tf_op jit(solution)/shard_map/ppermute | solution.py:283
  317.8 142.3 %collective-permute-start.67 = (bf16[1024,2048]{1,0:T(8,128)(2,1)S(1)}, bf16[1024,2048]{1,0:T(8,128)(2,1)S(1)}, u32[]{:S(2)}, u32[]{:S(2)}) collective-permute-start(bf16[1024,2048]{1,0:T(8,128)(2,1)S(1)} %bitcast.359), channel_id=1, source_target_pairs={{0,16},{16,0},{1,17},{17,1},{2,18},{18,2},{3,19},{19,3},{4,20},{20... | collective-permute-start | bytes 12582920 | tf_op jit(solution)/shard_map/ppermute | solution.py:287
  326.8 38.7 %collective-permute-start.60 = (bf16[1,2,2,128,512]{4,3,2,1,0:T(8,128)(2,1)S(1)}, bf16[1,2,2,128,512]{4,3,2,1,0:T(8,128)(2,1)S(1)}, u32[]{:S(2)}, u32[]{:S(2)}) collective-permute-start(bf16[1,2,2,128,512]{4,3,2,1,0:T(8,128)(2,1)S(1)} %broadcast_select_fusion.49), channel_id=1, source_target_pairs={{0,4},{1,5},{2,6},{3,7},{4,0},{5,1},{6,2},{7,3},{8,12},{9,13},{10,... | collective-permute-start | bytes 1572872 | tf_op jit(solution)/shard_map/ppermute | solution.py:283
  328.3 87.1 %collective-permute-start.66 = (bf16[1,256,2048]{2,1,0:T(8,128)(2,1)S(1)}, bf16[1,256,2048]{2,1,0:T(8,128)(2,1)S(1)}, u32[]{:S(2)}, u32[]{:S(2)}) collective-permute-start(bf16[1,256,2048]{2,1,0:T(8,128)(2,1)S(1)} %select_bitcast_fusion), channel_id=1, source_target_pairs={{0,8},{1,9},{2,10},{3,11},{4,12},{5,13},{6,14},{7,15},{8,0},{9,1},... | collective-permute-start | bytes 3145736 | tf_op jit(solution)/shard_map/ppermute | solution.py:283
  365.7 72.2 %collective-permute-start.61 = (bf16[1,2,2,2,128,512]{5,4,3,2,1,0:T(8,128)(2,1)S(1)}, bf16[1,2,2,2,128,512]{5,4,3,2,1,0:T(8,128)(2,1)S(1)}, u32[]{:S(2)}, u32[]{:S(2)}) collective-permute-start(bf16[1,2,2,2,128,512]{5,4,3,2,1,0:T(8,128)(2,1)S(1)} %maximum_bitcast_fusion), channel_id=1, source_target_pairs={{0,8},{1,9},{2,10},{3,11},{4,12},{5,13},{6,14},{7,15},{8,0},{9,1},... | collective-permute-start | bytes 3145736 | tf_op jit(solution)/shard_map/ppermute | solution.py:283
  367.6 92.2 %collective-permute-start.65 = (bf16[1,2,2,2,128,512]{5,4,3,2,1,0:T(8,128)(2,1)S(1)}, bf16[1,2,2,2,128,512]{5,4,3,2,1,0:T(8,128)(2,1)S(1)}, u32[]{:S(2)}, u32[]{:S(2)}) collective-permute-start(bf16[1,2,2,2,128,512]{5,4,3,2,1,0:T(8,128)(2,1)S(1)} %maximum_bitcast_fusion.1), channel_id=1, source_target_pairs={{0,8},{1,9},{2,10},{3,11},{4,12},{5,13},{6,14},{7,15},{8,0},{9,1},... | collective-permute-start | bytes 3145736 | tf_op jit(solution)/shard_map/ppermute | solution.py:283
  590.8 94.3 %collective-permute-start.160 = (bf16[1,256,2048]{2,1,0:T(8,128)(2,1)S(1)}, bf16[1,256,2048]{2,1,0:T(8,128)(2,1)S(1)}, u32[]{:S(2)}, u32[]{:S(2)}) collective-permute-start(bf16[1,256,2048]{2,1,0:T(8,128)(2,1)S(1)} %fusion.11), channel_id=1, source_target_pairs={{0,8},{1,9},{2,10},{3,11},{4,12},{5,13},{6,14},{7,15},{8,0},{9,1},... | collective-permute-start | bytes 3145736 | tf_op jit(solution)/shard_map/ppermute | solution.py:283
  593.5 114.2 %collective-permute-start.155 = (bf16[1,2,2,2,128,512]{5,4,3,2,1,0:T(8,128)(2,1)S(1)}, bf16[1,2,2,2,128,512]{5,4,3,2,1,0:T(8,128)(2,1)S(1)}, u32[]{:S(2)}, u32[]{:S(2)}) collective-permute-start(bf16[1,2,2,2,128,512]{5,4,3,2,1,0:T(8,128)(2,1)S(1)} %bitcast.408), channel_id=1, source_target_pairs={{0,8},{1,9},{2,10},{3,11},{4,12},{5,13},{6,14},{7,15},{8,0},{9,1},... | collective-permute-start | bytes 3145736 | tf_op jit(solution)/shard_map/ppermute | solution.py:283
  599.1 130.6 %collective-permute-start.150 = (bf16[1,2,2,2,128,512]{5,4,3,2,1,0:T(8,128)(2,1)S(1)}, bf16[1,2,2,2,128,512]{5,4,3,2,1,0:T(8,128)(2,1)S(1)}, u32[]{:S(2)}, u32[]{:S(2)}) collective-permute-start(bf16[1,2,2,2,128,512]{5,4,3,2,1,0:T(8,128)(2,1)S(1)} %bitcast.409), channel_id=1, source_target_pairs={{0,8},{1,9},{2,10},{3,11},{4,12},{5,13},{6,14},{7,15},{8,0},{9,1},... | collective-permute-start | bytes 3145736 | tf_op jit(solution)/shard_map/ppermute | solution.py:283
  609.5 136.7 %collective-permute-start.88 = (bf16[1024,2048]{1,0:T(8,128)(2,1)}, bf16[1024,2048]{1,0:T(8,128)(2,1)}, u32[]{:S(2)}, u32[]{:S(2)}) collective-permute-start(bf16[1024,2048]{1,0:T(8,128)(2,1)} %add_convert_fusion.2), channel_id=1, source_target_pairs={{0,16},{16,0},{1,17},{17,1},{2,18},{18,2},{3,19},{19,3},{4,20},{20... | collective-permute-start | bytes 12582920 | tf_op jit(solution)/shard_map/ppermute | solution.py:287
  685.9 60.0 %collective-permute-start.161 = (bf16[1,256,2048]{2,1,0:T(8,128)(2,1)S(1)}, bf16[1,256,2048]{2,1,0:T(8,128)(2,1)S(1)}, u32[]{:S(2)}, u32[]{:S(2)}) collective-permute-start(bf16[1,256,2048]{2,1,0:T(8,128)(2,1)S(1)} %fusion.1), channel_id=1, source_target_pairs={{0,16},{16,0},{1,17},{17,1},{2,18},{18,2},{3,19},{19,3},{4,20},{20... | collective-permute-start | bytes 3145736 | tf_op jit(solution)/shard_map/ppermute | solution.py:287
  744.8 58.7 %collective-permute-start.152 = (bf16[2,1,2,128,512]{4,3,2,1,0:T(8,128)(2,1)}, bf16[2,1,2,128,512]{4,3,2,1,0:T(8,128)(2,1)}, u32[]{:S(2)}, u32[]{:S(2)}) collective-permute-start(bf16[2,1,2,128,512]{4,3,2,1,0:T(8,128)(2,1)} %broadcast_select_fusion.31), channel_id=1, source_target_pairs={{0,2},{1,3},{2,0},{3,1},{4,6},{5,7},{6,4},{7,5},{8,10},{9,11},{10,... | collective-permute-start | bytes 1572872 | tf_op jit(solution)/shard_map/ppermute | solution.py:283
  837.0 66.3 %collective-permute-start.107 = (bf16[1024,2048]{1,0:T(8,128)(2,1)}, bf16[1024,2048]{1,0:T(8,128)(2,1)}, u32[]{:S(2)}, u32[]{:S(2)}) collective-permute-start(bf16[1024,2048]{1,0:T(8,128)(2,1)} %bitcast.77), channel_id=1, source_target_pairs={{0,16},{16,0},{1,17},{17,1},{2,18},{18,2},{3,19},{19,3},{4,20},{20... | collective-permute-start | bytes 12582920 | tf_op jit(solution)/shard_map/ppermute | solution.py:287
  856.0 43.2 %collective-permute-start.149 = (f32[2,1,1,1,1,128]{5,4,3,2,1,0:T(1,128)S(1)}, f32[2,1,1,1,1,128]{5,4,3,2,1,0:T(1,128)S(1)}, u32[]{:S(2)}, u32[]{:S(2)}) collective-permute-start(f32[2,1,1,1,1,128]{5,4,3,2,1,0:T(1,128)S(1)} %broadcast_select_fusion.160), channel_id=1, source_target_pairs={{0,1},{1,0},{2,3},{3,2},{4,5},{5,4},{6,7},{7,6},{8,9},{9,8},{10,11... | collective-permute-start | bytes 3080 | tf_op jit(solution)/shard_map/ppermute | solution.py:283
  922.8 41.4 %collective-permute-start.109 = (bf16[8,128,128]{2,1,0:T(8,128)(2,1)S(1)}, bf16[8,128,128]{2,1,0:T(8,128)(2,1)S(1)}, u32[]{:S(2)}, u32[]{:S(2)}) collective-permute-start(bf16[8,128,128]{2,1,0:T(8,128)(2,1)S(1)} %get-tuple-element.37), channel_id=1, source_target_pairs={{0,8},{1,9},{2,10},{3,11},{4,12},{5,13},{6,14},{7,15},{8,0},{9,1},... | collective-permute-start | bytes 786440 | tf_op jit(solution)/shard_map/ppermute | solution.py:283
  933.8 73.7 %collective-permute-start.141 = (bf16[128,2048]{1,0:T(8,128)(2,1)}, bf16[128,2048]{1,0:T(8,128)(2,1)}, u32[]{:S(2)}, u32[]{:S(2)}) collective-permute-start(bf16[128,2048]{1,0:T(8,128)(2,1)} %get-tuple-element.214), channel_id=1, source_target_pairs={{8,0},{9,1},{10,2},{11,3},{12,4},{13,5},{14,6},{15,7},{16,24},{17,... | collective-permute-start | bytes 1572872 | tf_op jit(solution)/shard_map/ppermute | solution.py:736
  935.2 42.4 %collective-permute-start.114 = (bf16[8,128,128]{2,1,0:T(8,128)(2,1)S(1)}, bf16[8,128,128]{2,1,0:T(8,128)(2,1)S(1)}, u32[]{:S(2)}, u32[]{:S(2)}) collective-permute-start(bf16[8,128,128]{2,1,0:T(8,128)(2,1)S(1)} %get-tuple-element.40), channel_id=1, source_target_pairs={{8,0},{9,1},{10,2},{11,3},{12,4},{13,5},{14,6},{15,7},{24,16},{25,... | collective-permute-start | bytes 786440 | tf_op jit(solution)/shard_map/ppermute | solution.py:631
  936.8 43.7 %collective-permute-start.115 = (bf16[8,128,128]{2,1,0:T(8,128)(2,1)S(1)}, bf16[8,128,128]{2,1,0:T(8,128)(2,1)S(1)}, u32[]{:S(2)}, u32[]{:S(2)}) collective-permute-start(bf16[8,128,128]{2,1,0:T(8,128)(2,1)S(1)} %get-tuple-element.39), channel_id=1, source_target_pairs={{0,8},{1,9},{2,10},{3,11},{4,12},{5,13},{6,14},{7,15},{8,0},{9,1},... | collective-permute-start | bytes 786440 | tf_op jit(solution)/shard_map/ppermute | solution.py:283
  1007.3 45.3 %collective-permute-start.116 = (bf16[1024,2048]{1,0:T(8,128)(2,1)S(1)}, bf16[1024,2048]{1,0:T(8,128)(2,1)S(1)}, u32[]{:S(2)}, u32[]{:S(2)}) collective-permute-start(bf16[1024,2048]{1,0:T(8,128)(2,1)S(1)} %convolution_convert_fusion), channel_id=1, source_target_pairs={{0,16},{16,0},{1,17},{17,1},{2,18},{18,2},{3,19},{19,3},{4,20},{20... | collective-permute-start | bytes 12582920 | tf_op jit(solution)/shard_map/ppermute | solution.py:287
  1009.7 40.1 %collective-permute-start.142 = (bf16[128,2048]{1,0:T(8,128)(2,1)S(1)}, bf16[128,2048]{1,0:T(8,128)(2,1)S(1)}, u32[]{:S(2)}, u32[]{:S(2)}) collective-permute-start(bf16[128,2048]{1,0:T(8,128)(2,1)S(1)} %add_convert_fusion.19), channel_id=1, source_target_pairs={{0,16},{1,17},{2,18},{3,19},{4,20},{5,21},{6,22},{7,23},{24,8},{25... | collective-permute-start | bytes 1572872 | tf_op jit(solution)/shard_map/ppermute | solution.py:739
  (261 other events, 3444.9 us)

commit v2 on v0

--- a/solution.py
+++ b/solution.py
@@ -1,8 +1,11 @@
+import functools
 import math
 
 import jax
 import jax.numpy as jnp
 from jax import lax
+from jax.experimental import pallas as pl
+from jax.experimental.pallas import tpu as pltpu
 from jax.sharding import PartitionSpec as P
 
 HEADS = 16
@@ -57,7 +60,7 @@
     )
 
 
-def local(
+def local_general(
     inputs,
     positions,
     cotangent,
@@ -267,7 +270,869 @@
     )
 
 
+LINE = 4
+SQUARE = 4
+X, Y, Z, FAR = 1, 2, 4, 8
+ROWS = 128
+BLOCKS = 16
+WINDOW = 1152
+SHARE = 256
+SCALING = 1.0 / math.sqrt(HEAD)
+SQUARES = [[SQUARE * z + r for r in range(SQUARE)] for z in range(LINE)]
+
+
+def swap(value, bit):
+    return lax.ppermute(value, "shard", [(source, source ^ bit) for source in range(BLOCKS)])
+
+
+def swap_core(value):
+    return lax.ppermute(value, "grp", [(0, 1), (1, 0)])
+
+
+def along(bit):
+    return lambda value: swap(value, bit)
+
+
+def line_place():
+    return lax.axis_index("shard") // SQUARE
+
+
+def square_place():
+    return lax.axis_index("shard") % SQUARE
+
+
+def line_move(pairs):
+    pairs = [(SQUARE * z + r, SQUARE * to + r) for z, to in pairs for r in range(SQUARE)]
+    return lambda value: lax.ppermute(value, "shard", pairs)
+
+
+RIGHT, LEFT = ((0, 1), (1, 2), (2, 3)), ((3, 2), (2, 1), (1, 0))
+
+
+def line_turn(distance):
+    pairs = [(s, (s + SQUARE * distance) % BLOCKS) for s in range(BLOCKS)]
+    return lambda value: lax.ppermute(value, "shard", pairs)
+
+
+def hold(values, *later):
+    return lax.optimization_barrier((values, later))[0]
+
+
+def together(*values):
+    return lax.optimization_barrier(values)
+
+
+def run(*tracks):
+    live, results = {}, {}
+
+    def advance(name, generator, came):
+        try:
+            live[name] = (generator, generator.send(came))
+        except StopIteration as end:
+            live.pop(name, None)
+            results[name] = end.value
+
+    for name, generator in enumerate(tracks):
+        advance(name, generator, None)
+    while live:
+        requests = [request for _, asked in live.values() for request in asked]
+        given = lax.optimization_barrier(tuple(value for value, _ in requests))
+        came = [move(value) for value, (_, move) in zip(given, requests)]
+        came = list(lax.optimization_barrier(tuple(came)))
+        for name, (generator, asked) in list(live.items()):
+            mine, came = came[: len(asked)], came[len(asked) :]
+            advance(name, generator, mine)
+    return [results[name] for name in range(len(tracks))]
+
+
+def alone(track):
+    return run(track)[0]
+
+
+def gather_first(value):
+    right, left = yield [(value, line_move(RIGHT)), (value, line_move(LEFT))]
+    return value, right, left
+
+
+def gather_second(value, right, left):
+    place = line_place()
+    further = jnp.where(place == 1, right, left)
+    rights, lefts, further = yield [
+        (right, line_move(RIGHT[1:])),
+        (left, line_move(LEFT[1:])),
+        (further, line_move(((1, 3), (2, 0)))),
+    ]
+    rows, width = value.shape
+    shape = jax.ShapeDtypeStruct((LINE * rows, width), value.dtype)
+    arrays = [value, right, left, rights, lefts, further]
+    return whole_call(gather_kernel, [shape], [place.astype(jnp.int32).reshape(1)], arrays)
+
+
+def gather_kernel(place_ref, own_ref, right_ref, left_ref, rights_ref, lefts_ref, further_ref, out_ref):
+    place, rows = place_ref[0], own_ref.shape[0]
+
+    def put(slot, condition, ref):
+        @pl.when(condition)
+        def _():
+            out_ref[slot * rows : (slot + 1) * rows, :] = ref[...]
+
+    out_ref[:rows, :] = own_ref[...]
+    put(1, place >= 1, right_ref)
+    put(1, place == 0, further_ref)
+    put(2, place >= 2, rights_ref)
+    put(2, place < 2, lefts_ref)
+    put(3, place == 3, further_ref)
+    put(3, place < 3, left_ref)
+
+
+def gather_line(value):
+    came = yield from gather_first(value)
+    return (yield from gather_second(*came))
+
+
+def join_kernel(own_ref, other_ref, out_ref):
+    rows = own_ref.shape[0]
+    out_ref[:rows, :] = own_ref[...]
+    out_ref[rows:, :] = other_ref[...]
+
+
+def both_cores(own):
+    shape = jax.ShapeDtypeStruct((2 * own.shape[0], own.shape[1]), own.dtype)
+    return whole_call(join_kernel, [shape], [], [own, swap_core(own)])
+
+
+def scatter_first(total):
+    parts = total.reshape(LINE, -1, total.shape[-1])
+    further = jnp.where(line_place() == 0, parts[1], parts[3])
+    return (
+        yield [
+            (parts[2], line_move(RIGHT[:2])),
+            (parts[2], line_move(LEFT[:2])),
+            (further, line_move(((0, 2), (3, 1)))),
+        ]
+    )
+
+
+def scatter_second(total, right, left, further):
+    parts = total.reshape(LINE, -1, total.shape[-1])
+    place, nothing = line_place(), jnp.zeros((), total.dtype)
+    right, left = yield [
+        (add_low(parts[3], right, jnp.where(place == 2, further, nothing)), line_move(RIGHT)),
+        (add_low(parts[1], left, jnp.where(place == 1, further, nothing)), line_move(LEFT)),
+    ]
+    return add_wide(parts[0], right, left)
+
+
+def scatter_line(total):
+    came = yield from scatter_first(total)
+    return (yield from scatter_second(total, *came))
+
+
+def add_wide(*values):
+    return sum(value.astype(jnp.float32) for value in values)
+
+
+def add_low(*values):
+    return add_wide(*values).astype(jnp.bfloat16)
+
+
+def turn_line(block):
+    place = line_place()
+    came = yield [
+        (lax.dynamic_index_in_dim(block, (place + k) % LINE, 0, keepdims=False), line_turn(k))
+        for k in range(1, LINE)
+    ]
+    own = lax.dynamic_index_in_dim(block, place, 0, keepdims=False)
+    return jnp.stack([own, *came])
+
+
+def to_slots(value):
+    place = line_place()
+    return jnp.stack(
+        [lax.dynamic_index_in_dim(value, (place - k) % LINE, 0, keepdims=False) for k in range(LINE)]
+    )
+
+
+def in_two(value):
+    return jnp.split(value, 2, axis=-1)
+
+
+def square_first(value):
+    first, second = in_two(value)
+    return swap(first, X), swap(second, Y)
+
+
+def square_track(value):
+    came = yield [(part, along(bit)) for part, bit in zip(in_two(value), (X, Y))]
+    return tuple(came)
+
+
+def second_kernel(own_ref, first_ref, second_ref, to_first_ref, to_second_ref):
+    half = own_ref.shape[-1] // 2
+    to_first_ref[0] = own_ref[..., :half]
+    to_first_ref[1] = first_ref[...]
+    to_second_ref[0] = own_ref[..., half:]
+    to_second_ref[1] = second_ref[...]
+
+
+def second_parts(value, came):
+    shape = jax.ShapeDtypeStruct((2,) + came[0].shape, value.dtype)
+    return whole_call(second_kernel, [shape] * 2, [], [value, *came])
+
+
+def square_second(value, came):
+    first, second = second_parts(value, came)
+    return swap(first, Y), swap(second, X)
+
+
+def second_track(value, came):
+    first, second = second_parts(value, came)
+    later = yield [(first, along(Y)), (second, along(X))]
+    return tuple(later)
+
+
+def square_kernel(index_ref, own_ref, first_ref, second_ref, firsts_ref, seconds_ref, out_ref):
+    half, count = own_ref.shape[-1] // 2, own_ref.shape[0]
+    firsts = (own_ref, first_ref, firsts_ref.at[0], firsts_ref.at[1])
+    seconds = (own_ref, seconds_ref.at[0], second_ref, seconds_ref.at[1])
+    for corner in range(SQUARE):
+        for number in range(count):
+            target = index_ref[corner * count + number]
+            out_ref[target, :, :half] = firsts[corner][number, :, :half]
+            lanes = slice(half, None) if corner == 0 else slice(None)
+            out_ref[target, :, half:] = seconds[corner][number, :, lanes]
+
+
+def square_join(index, value, came, later):
+    count, rows, width = value.shape
+    shape = jax.ShapeDtypeStruct((SQUARE * count, rows, width), value.dtype)
+    return whole_call(square_kernel, [shape], [index], [value, *came, *later])
+
+
+def split_kernel(index_ref, grad_ref, kept_first, sent_first, kept_second, sent_second):
+    half, count = grad_ref.shape[-1] // 2, kept_first.shape[1]
+    firsts = ((kept_first, 0), (kept_first, 1), (sent_first, 0), (sent_first, 1))
+    seconds = ((kept_second, 0), (sent_second, 0), (kept_second, 1), (sent_second, 1))
+    for corner in range(SQUARE):
+        for number in range(count):
+            block = grad_ref[index_ref[corner * count + number]]
+            for (target, place), lanes in (
+                (firsts[corner], slice(0, half)),
+                (seconds[corner], slice(half, 2 * half)),
+            ):
+                target[place, number] = block[:, lanes]
+
+
+def sum_split(index, grad):
+    blocks, rows, width = grad.shape
+    shape = jax.ShapeDtypeStruct((2, blocks // SQUARE, rows, width // 2), grad.dtype)
+    return whole_call(split_kernel, [shape] * 4, [index], [grad])
+
+
+def sum_first(split):
+    return swap(split[1], Y), swap(split[3], X)
+
+
+def low_sum(first, second):
+    return (first.astype(jnp.float32) + second.astype(jnp.float32)).astype(jnp.bfloat16)
+
+
+def add_kernel(kept_first, came_first, kept_second, came_second, *targets):
+    for number, (kept, came) in enumerate(((kept_first, came_first), (kept_second, came_second))):
+        for place in range(2):
+            for block in range(kept.shape[1]):
+                targets[2 * number + place][block] = low_sum(kept[place, block], came[place, block])
+
+
+def sum_second(split, came):
+    shape = jax.ShapeDtypeStruct(came[0].shape[1:], jnp.bfloat16)
+    arrays = [split[0], came[0], split[2], came[1]]
+    first, to_first, second, to_second = whole_call(add_kernel, [shape] * 4, [], arrays)
+    return (first, second), (swap(to_first, X), swap(to_second, Y))
+
+
+def end_kernel(first_ref, came_first, second_ref, came_second, out_ref):
+    half = first_ref.shape[-1]
+    for block in range(out_ref.shape[0]):
+        out_ref[block, :, :half] = low_sum(first_ref[block], came_first[block])
+        out_ref[block, :, half:] = low_sum(second_ref[block], came_second[block])
+
+
+def sum_end(kept, came):
+    count, rows, half = kept[0].shape
+    shape = jax.ShapeDtypeStruct((count, rows, 2 * half), jnp.bfloat16)
+    return whole_call(end_kernel, [shape], [], [kept[0], came[0], kept[1], came[1]])
+
+
+def in_vmem(count, scalars=1):
+    return [pl.BlockSpec(memory_space=pltpu.SMEM)] * scalars + [
+        pl.BlockSpec(memory_space=pltpu.VMEM)
+    ] * count
+
+
+def whole_call(kernel, shapes, scalars, arrays, scratch=(), megabytes=40, cost=None):
+    specs = [pl.BlockSpec(memory_space=pltpu.VMEM)] * len(shapes)
+    single = len(shapes) == 1
+    size = sum(array.size * array.dtype.itemsize for array in arrays)
+    return pl.pallas_call(
+        kernel,
+        out_shape=shapes[0] if single else shapes,
+        in_specs=in_vmem(len(arrays), len(scalars)),
+        out_specs=specs[0] if single else specs,
+        scratch_shapes=list(scratch),
+        compiler_params=pltpu.CompilerParams(vmem_limit_bytes=megabytes * 2**20),
+        cost_estimate=cost or pl.CostEstimate(flops=0, bytes_accessed=2 * size, transcendentals=0),
+    )(*scalars, *arrays)
+
+
+def column_start(columns, parts, place, part, core):
+    return pl.multiple_of(place * (columns // LINE) + part * 2 * SHARE + core * SHARE, SHARE)
+
+
+def pick_kernel(parts, core_ref, *refs):
+    *weight_refs, block_ref = refs
+    columns = weight_refs[0].shape[1]
+    for place in range(LINE):
+        for number, weight_ref in enumerate(weight_refs):
+            for part in range(parts):
+                start = column_start(columns, parts, place, part, core_ref[0])
+                lane = (number * parts + part) * SHARE
+                block_ref[place, :ROWS, lane : lane + SHARE] = weight_ref[:, pl.ds(start, SHARE)]
+
+
+def pick_more_kernel(parts, core_ref, *refs):
+    *weight_refs, more_ref, block_ref = refs
+    pick_kernel(parts, core_ref, *weight_refs, block_ref)
+    for place in range(LINE):
+        for lane in range(0, block_ref.shape[2], HEAD):
+            block_ref[place, ROWS:, lane : lane + HEAD] = more_ref[...]
+
+
+def spread_kernel(parts, core_ref, mine_ref, came_ref, place_ref, *grad_refs):
+    columns = grad_refs[0].shape[1]
+    for slot in range(LINE):
+        for number, grad_ref in enumerate(grad_refs):
+            for part in range(parts):
+                lane = (number * parts + part) * SHARE
+                for source, core in ((mine_ref, core_ref[0]), (came_ref, 1 - core_ref[0])):
+                    start = column_start(columns, parts, place_ref[slot], part, core)
+                    grad_ref[:, pl.ds(start, SHARE)] = source[slot, :, lane : lane + SHARE].astype(
+                        jnp.float32
+                    )
+
+
+def spread_scalars_kernel(parts, core_ref, place_ref, mine_ref, came_ref, *grad_refs):
+    spread_kernel(parts, core_ref, mine_ref, came_ref, place_ref, *grad_refs)
+
+
+def pick_columns(core_ref, weights, parts, more=None):
+    rows, columns = weights[0].shape
+    extra = [] if more is None else [more]
+    rows += sum(array.shape[0] for array in extra)
+    shape = jax.ShapeDtypeStruct((LINE, rows, len(weights) * columns // 8), jnp.bfloat16)
+    kernel = functools.partial(pick_more_kernel if extra else pick_kernel, parts)
+    return whole_call(kernel, [shape], [core_ref], [*weights, *extra])
+
+
+def spread_columns(core_ref, place_ref, mine, came, count, parts):
+    shape = jax.ShapeDtypeStruct((mine.shape[1], 8 * mine.shape[2] // count), jnp.float32)
+    kernel = functools.partial(spread_scalars_kernel, parts)
+    return whole_call(kernel, [shape] * count, [core_ref, place_ref], [mine, came])
+
+
+def head_lanes(head):
+    return slice(head * HEAD, (head + 1) * HEAD)
+
+
+def halo_slots(place):
+    return lax.rem(place + 2, LINE), lax.rem(place + 1, LINE)
+
+
+def pack_kernel(core_ref, place_ref, q_ref, k_ref, v_ref, out_ref):
+    for group in range(2):
+        part = core_ref[0] if group == 0 else 1 - core_ref[0]
+        for head in range(2):
+            lanes, target = head_lanes(head), 2 * group + head
+            for slot in range(LINE):
+                for number, ref in enumerate((q_ref, k_ref, v_ref)):
+                    out_ref[target, LINE * number + slot] = ref[part, slot, :, lanes]
+            for number, slot in enumerate(halo_slots(place_ref[0])):
+                out_ref[target, 12 + number] = k_ref[core_ref[0], slot, :, lanes]
+                out_ref[target, 14 + number] = v_ref[core_ref[0], slot, :, lanes]
+
+
+def unpack_kernel(core_ref, came_ref, out_ref):
+    for group in range(2):
+        part = core_ref[0] if group == 0 else 1 - core_ref[0]
+        for head in range(2):
+            for slot in range(LINE):
+                out_ref[part, slot, :, head_lanes(head)] = came_ref[2 * group + head, slot]
+
+
+def pack_grad_kernel(core_ref, grad_ref, out_ref):
+    for group in range(2):
+        part = core_ref[0] if group == 0 else 1 - core_ref[0]
+        for head in range(2):
+            for slot in range(LINE):
+                out_ref[2 * group + head, slot] = grad_ref[part, slot, :, head_lanes(head)]
+
+
+def unpack_grad_kernel(core_ref, place_ref, came_ref, dq_ref, dk_ref, dv_ref):
+    for group in range(2):
+        part = core_ref[0] if group == 0 else 1 - core_ref[0]
+        for head in range(2):
+            for slot in range(LINE):
+                for number, ref in enumerate((dq_ref, dk_ref, dv_ref)):
+                    ref[part, slot, :, head_lanes(head)] = came_ref[
+                        2 * group + head, LINE * number + slot
+                    ].astype(jnp.float32)
+    for head in range(2):
+        for number, slot in enumerate(halo_slots(place_ref[0])):
+            dk_ref[core_ref[0], slot, :, head_lanes(head)] += came_ref[2 + head, 12 + number].astype(
+                jnp.float32
+            )
+            dv_ref[core_ref[0], slot, :, head_lanes(head)] += came_ref[2 + head, 14 + number].astype(
+                jnp.float32
+            )
+
+
+def visible_of(place):
+    row = lax.broadcasted_iota(jnp.int32, (ROWS, WINDOW), 0)
+    column = lax.broadcasted_iota(jnp.int32, (ROWS, WINDOW), 1)
+    distance = row - column + (WINDOW - ROWS)
+    return (distance >= 0) & (distance <= place)
+
+
+def dot_last(left, right):
+    return lax.dot_general(
+        left, right, (((1,), (1,)), ((), ())), preferred_element_type=jnp.float32
+    )
+
+
+def stream_row(place, source, slot):
+    block = lax.rem(place - slot + LINE, LINE) * SQUARE + source
+    return block, pl.multiple_of(block * ROWS, ROWS)
+
+
+def rows_at(start):
+    return pl.ds(pl.multiple_of(start, ROWS), ROWS)
+
+
+def fill(place, message_ref, keys, values):
+    for source in range(SQUARE):
+        for slot in range(LINE):
+            _, start = stream_row(place, source, slot)
+            keys[rows_at(start + DOC_LEN), :] = message_ref[source, LINE + slot]
+            values[rows_at(start + DOC_LEN), :] = message_ref[source, 2 * LINE + slot]
+        for number in range(2):
+            start = (number * SQUARE + source) * ROWS
+            keys[start : start + ROWS, :] = message_ref[source, 12 + number]
+            values[start : start + ROWS, :] = message_ref[source, 14 + number]
+
+
+def attend_kernel(place_ref, message_ref, pos_ref, o_ref, lse_ref, keys, values):
+    place = place_ref[0]
+    fill(place, message_ref, keys, values)
+
+    def step(number, carry):
+        source, slot = number // LINE, number % LINE
+        block, start = stream_row(place, source, slot)
+        rows = pl.ds(start, WINDOW)
+        scores = dot_last(message_ref[source, slot], keys[rows, :]) * SCALING
+        masked = jnp.where(visible_of(pos_ref[block]), scores, -jnp.inf)
+        top = jnp.max(masked, axis=-1, keepdims=True)
+        expo = jnp.exp(masked - top)
+        total = jnp.sum(expo, axis=-1, keepdims=True)
+        probs = (expo / total).astype(jnp.bfloat16)
+        mixed = jnp.dot(probs, values[rows, :], preferred_element_type=jnp.float32)
+        o_ref[source, slot] = mixed.astype(jnp.bfloat16)
+        lse_ref[number] = top + jnp.log(total)
+        return carry
+
+    lax.fori_loop(0, BLOCKS, step, 0)
+
+
+def attend_back_kernel(
+    place_ref, message_ref, pos_ref, lse_ref, do_ref, out_ref, keys, values, d_keys, d_values
+):
+    place = place_ref[0]
+    fill(place, message_ref, keys, values)
+    d_keys[...] = jnp.zeros_like(d_keys)
+    d_values[...] = jnp.zeros_like(d_values)
+
+    def step(number, carry):
+        source, slot = number // LINE, number % LINE
+        block, start = stream_row(place, source, slot)
+        rows = pl.ds(start, WINDOW)
+        query, grad = message_ref[source, slot], do_ref[source, slot]
+        key, value = keys[rows, :], values[rows, :]
+        scores = dot_last(query, key) * SCALING
+        probs = jnp.where(visible_of(pos_ref[block]), jnp.exp(scores - lse_ref[number]), 0.0)
+        d_probs = dot_last(grad, value)
+        inner = jnp.sum(probs * d_probs, axis=-1, keepdims=True)
+        d_scores = (probs * (d_probs - inner) * SCALING).astype(jnp.bfloat16)
+        d_query = jnp.dot(d_scores, key, preferred_element_type=jnp.float32)
+        out_ref[source, slot] = d_query.astype(jnp.bfloat16)
+        d_keys[rows, :] += along_first(d_scores, query)
+        d_values[rows, :] += along_first(probs.astype(jnp.bfloat16), grad)
+        return carry
+
+    lax.fori_loop(0, BLOCKS, step, 0)
+    for source in range(SQUARE):
+        for slot in range(LINE):
+            _, start = stream_row(place, source, slot)
+            out_ref[source, LINE + slot] = d_keys[rows_at(start + DOC_LEN), :].astype(jnp.bfloat16)
+            out_ref[source, 2 * LINE + slot] = d_values[rows_at(start + DOC_LEN), :].astype(jnp.bfloat16)
+        for number in range(2):
+            start = (number * SQUARE + source) * ROWS
+            out_ref[source, 12 + number] = d_keys[start : start + ROWS, :].astype(jnp.bfloat16)
+            out_ref[source, 14 + number] = d_values[start : start + ROWS, :].astype(jnp.bfloat16)
+
+
+KEPT = [pltpu.VMEM((3 * DOC_LEN, HEAD), jnp.bfloat16)] * 2
+SUMMED = [pltpu.VMEM((3 * DOC_LEN, HEAD), jnp.float32)] * 2
+
+
+def attend(place_ref, message, positions):
+    shapes = [
+        jax.ShapeDtypeStruct((SQUARE, LINE, ROWS, HEAD), jnp.bfloat16),
+        jax.ShapeDtypeStruct((BLOCKS, ROWS, 1), jnp.float32),
+    ]
+    return whole_call(attend_kernel, shapes, [place_ref], [message, positions], KEPT)
+
+
+def attend_back(place_ref, message, positions, lse, grad):
+    shape = jax.ShapeDtypeStruct(message.shape, jnp.bfloat16)
+    arrays = [message, positions, lse, grad]
+    return whole_call(attend_back_kernel, [shape], [place_ref], arrays, KEPT + SUMMED)
+
+
+def turn_square(message):
+    return lax.all_to_all(message, "shard", 0, 0, tiled=True, axis_index_groups=SQUARES)
+
+
+def local_line(
+    inputs,
+    positions,
+    cotangent,
+    w_query,
+    w_key,
+    w_value,
+    w_out,
+    query_gain,
+    key_gain,
+    attn_gain,
+    w_gate,
+    w_up,
+    w_down,
+    mlp_gain,
+):
+    bf16, f32 = jnp.bfloat16, jnp.float32
+    width = inputs.shape[1]
+    core_index = lax.axis_index("grp")
+    shard_index = lax.axis_index("shard")
+    core = core_index == 1
+    place, corner = line_place(), square_place()
+    core_ref = core_index.astype(jnp.int32).reshape(1)
+    place_ref = place.astype(jnp.int32).reshape(1)
+    slots = jnp.arange(LINE, dtype=jnp.int32)
+    slot_places = (place - slots) % LINE
+    hidden = w_down.shape[0] * 2
+    tokens = 2 * LINE * ROWS
+    part_tokens = tokens // 2
+    heads = 2 * HEAD
+    from_slots = (slot_places[None, :] * SQUARE + (corner ^ slots)[:, None]).reshape(-1)
+    from_order = (slots[None, :] * SQUARE + (corner ^ slots)[:, None]).reshape(-1)
+    from_corner = corner ^ slots
+
+    def region(function, *given):
+        shapes = jax.eval_shape(function, *given)
+        empty = lambda *given: jax.tree.map(lambda leaf: jnp.zeros(leaf.shape, leaf.dtype), shapes)
+        return lax.cond(positions[0] >= 0, function, empty, *given)
+
+    def across_cores(left, right, product):
+        other = product(left[part_tokens:], right).astype(bf16)
+        own = product(left[:part_tokens], right)
+        return add_low(own, swap_core(other))
+
+    def dot(left, right):
+        return jnp.dot(left, right, preferred_element_type=f32)
+
+    small = jnp.concatenate(
+        [
+            jnp.stack([query_gain, key_gain, attn_gain, mlp_gain]),
+            jnp.stack([positions // 32, positions % 32]).astype(bf16),
+            jnp.zeros((10, ROWS), bf16),
+        ]
+    )
+    down_own = lax.dynamic_index_in_dim(w_down.reshape(2, 1, hidden // SQUARE, width), core_index, 0, keepdims=False)
+    out_own = w_out[None]
+    head_block, out_came, down_came = run(
+        turn_line(pick_columns(core_ref, (w_query, w_key, w_value), 1, small)),
+        square_track(out_own),
+        square_track(down_own),
+    )
+    x_came, head_came = run(gather_first(inputs), square_track(head_block))
+    x_own, head_later = run(gather_second(*x_came), second_track(head_block, head_came))
+    out_own, down_own = hold((out_own, down_own), x_own)
+    out_later = square_second(out_own, out_came)
+    down_later = square_second(down_own, down_came)
+    x_all = both_cores(x_own)
+    head_block = square_join(from_slots, head_block, head_came, head_later)
+    qkv_w = head_block[:, :ROWS].reshape(width, 3 * heads)
+    gains = head_block[:, ROWS : ROWS + 4, :HEAD].astype(f32)
+    first_head = place * SQUARE + core_index * 2
+    head_gain = lax.dynamic_slice_in_dim(gains, first_head, 2, 0)[:, :2].transpose(1, 0, 2).reshape(2, heads)
+    gains = gains.transpose(1, 0, 2).reshape(4, width)
+    stream = head_block[:, ROWS + 4 : ROWS + 6, :HEAD].astype(jnp.int32)
+    stream = stream[:, 0] * 32 + stream[:, 1]
+    stream_other = swap_core(stream)
+    query_places = jnp.where((corner >= 2) == core, stream, stream_other).reshape(BLOCKS, ROWS, 1)
+    held = [
+        to_slots(lax.dynamic_index_in_dim(part.reshape(LINE, SQUARE, ROWS), corner, 1, keepdims=False))
+        for part in (stream, stream_other)
+    ]
+    middle = HEAD // 2
+    frequency = jnp.power(500000.0, -2.0 * jnp.arange(middle).astype(f32) / HEAD)
+    angles = jnp.stack(held).astype(f32).reshape(tokens, 1) * frequency[None, :]
+    cosines, sines = together(jnp.cos(angles), jnp.sin(angles))
+    cosines = jnp.concatenate([cosines] * 4, axis=1)
+    sines = jnp.concatenate([-sines, sines] * 2, axis=1)
+
+    def halves_swapped(values):
+        return jnp.concatenate(
+            [jnp.roll(values[:, head_lanes(head)], middle, axis=1) for head in range(2)], axis=1
+        )
+
+    def rotated(values):
+        return values * cosines + halves_swapped(values) * sines
+
+    def rotated_back(values):
+        return values * cosines - halves_swapped(values) * sines
+
+    def row_sums(first, second):
+        sums = jnp.stack([jnp.sum(first, axis=-1), jnp.sum(second, axis=-1)])
+        return to_slots(sums.reshape(2, 2, LINE, ROWS).transpose(2, 0, 1, 3))
+
+    def sums_track(value):
+        for bit in (Z, FAR):
+            (came,) = yield [(value, along(bit))]
+            value = value + came
+        (came,) = yield [(value, swap_core)]
+        return value + jnp.flip(came, 2)
+
+    def row_means(sums):
+        return to_slots(sums).transpose(1, 2, 0, 3).reshape(2, tokens, 1) / width
+
+    raw = dot(x_all, qkv_w)
+    q_raw, k_raw, v_raw = raw[:, :heads], raw[:, heads : 2 * heads], raw[:, 2 * heads :]
+    sums = region(lambda sums: alone(sums_track(sums)), row_sums(q_raw * q_raw, k_raw * k_raw))
+    sums, out_later, down_later = together(sums, out_later, down_later)
+    down_w = square_join(from_corner, down_own, down_came, down_later).reshape(-1, width)
+    out_w = square_join(from_corner, out_own, out_came, out_later)
+    out_w = lax.dynamic_slice_in_dim(out_w, core_index * 2, 2, 0).reshape(heads, width)
+
+    hidden_block = hold(pick_columns(core_ref, (w_gate, w_up), SQUARE), sums)
+    line_came = [
+        line_turn(k)(lax.dynamic_index_in_dim(hidden_block, (place + k) % LINE, 0, keepdims=False))
+        for k in range(1, LINE)
+    ]
+    means = row_means(sums)
+    q_scale, k_scale = lax.rsqrt(means[0] + 1e-06), lax.rsqrt(means[1] + 1e-06)
+    shape = (2, LINE, ROWS, heads)
+    query = rotated(q_raw * q_scale * head_gain[0]).astype(bf16).reshape(shape)
+    key = rotated(k_raw * k_scale * head_gain[1]).astype(bf16).reshape(shape)
+    value = v_raw.astype(bf16).reshape(shape)
+    message_shape = jax.ShapeDtypeStruct((SQUARE, 16, ROWS, HEAD), bf16)
+    heads_shape = jax.ShapeDtypeStruct((SQUARE, LINE, ROWS, HEAD), bf16)
+    tokens_shape = jax.ShapeDtypeStruct(shape, bf16)
+
+    def attended(query, key, value):
+        message = turn_square(
+            whole_call(pack_kernel, [message_shape], [core_ref, place_ref], [query, key, value])
+        )
+        mixed, lse = attend(place_ref, message, query_places)
+        mixed = whole_call(unpack_kernel, [tokens_shape], [core_ref], [turn_square(mixed)])
+        return message, lse, mixed.reshape(tokens, heads)
+
+    message, lse, mixed = region(attended, query, key, value)
+    mixed, line_came = together(mixed, line_came)
+    hidden_own = jnp.stack(
+        [lax.dynamic_index_in_dim(hidden_block, place, 0, keepdims=False), *line_came]
+    )
+    hidden_came = square_first(hidden_own)
+    branch = region(lambda mixed: alone(scatter_line(across_cores(mixed, out_w, dot))), mixed)
+    branch, hidden_came = together(branch, hidden_came)
+    hidden_later = square_second(hidden_own, hidden_came)
+
+    def state_of(branch):
+        branch_scale = lax.rsqrt(jnp.mean(branch * branch, axis=-1, keepdims=True) + 1e-06)
+        hidden_state = inputs.astype(f32) + branch * branch_scale * gains[2]
+        state = both_cores(alone(gather_line(hidden_state.astype(bf16))))
+        return branch_scale, hidden_state, state
+
+    branch_scale, hidden_state, state = region(state_of, branch)
+    state, hidden_later = together(state, hidden_later)
+    hidden_w = square_join(from_slots, hidden_own, hidden_came, hidden_later).reshape(width, -1)
+
+    both = dot(state, hidden_w)
+    gate, up = in_two(both)
+    active = (jax.nn.silu(gate) * up).astype(bf16)
+    mlp = alone(scatter_line(across_cores(active, down_w, dot)))
+    mlp_scale = lax.rsqrt(jnp.mean(mlp * mlp, axis=-1, keepdims=True) + 1e-06)
+    cot = cotangent.astype(f32)
+    scaled = cot * gains[3]
+    d_mlp = mlp_scale * scaled - mlp * mlp_scale**3 * jnp.mean(mlp * scaled, axis=-1, keepdims=True)
+    d_mlp = both_cores(alone(gather_line(d_mlp.astype(bf16))))
+    output = (hidden_state + mlp * mlp_scale * gains[3]).astype(bf16)
+    mlp_gain_part = jnp.sum(cot * mlp * mlp_scale, axis=0)
+
+    d_active = along_last(d_mlp, down_w)
+    sigma = jax.nn.sigmoid(gate)
+    d_gate = (d_active * up * sigma * (1.0 + gate * (1.0 - sigma))).astype(bf16)
+    d_up = (d_active * gate * sigma).astype(bf16)
+    d_both = jnp.concatenate([d_gate, d_up], axis=1)
+
+    total = across_cores(d_both, hidden_w, along_last)
+    hidden_split = sum_split(
+        from_order, along_first(state, d_both).astype(bf16).reshape(BLOCKS, ROWS, -1)
+    )
+    down_split = sum_split(
+        from_corner, along_first(active, d_mlp).astype(bf16).reshape(SQUARE, -1, width)
+    )
+    split = [
+        jnp.concatenate([first, second.reshape(2, -1, ROWS, second.shape[-1])], axis=1)
+        for first, second in zip(hidden_split, down_split)
+    ]
+    total, split = together(total, split)
+    grads_came = sum_first(split)
+    d_resid = region(lambda total: cot + alone(scatter_line(total)), total)
+    def d_branch_begun(d_resid):
+        scaled = d_resid * gains[2]
+        d_branch = branch_scale * scaled - branch * branch_scale**3 * jnp.mean(
+            branch * scaled, axis=-1, keepdims=True
+        )
+        attn_gain_part = jnp.sum(d_resid * branch * branch_scale, axis=0)
+        return alone(gather_first(d_branch.astype(bf16))), jnp.stack([attn_gain_part, mlp_gain_part])
+
+    def d_branch_of(*came):
+        d_branch = both_cores(alone(gather_second(*came)))
+        return d_branch, along_last(d_branch, out_w).astype(bf16)
+
+    d_branch, norms = region(d_branch_begun, d_resid)
+    d_branch, grads_came = together(d_branch, grads_came)
+    grads_kept, grads_came = sum_second(split, grads_came)
+    d_branch, d_mixed = region(d_branch_of, *d_branch)
+    d_mixed, grads_came = together(d_mixed, grads_came)
+    grads = sum_end(grads_kept, grads_came)
+    hidden_grad, down_grad = grads[:LINE], grads[LINE:].reshape(-1, width)
+    line_came = [
+        line_turn(k)(lax.dynamic_index_in_dim(hidden_grad, (place + k) % LINE, 0, keepdims=False))
+        for k in range(1, LINE)
+    ]
+
+    def attended_back(d_mixed, message, lse, d_branch, mixed):
+        grad = whole_call(pack_grad_kernel, [heads_shape], [core_ref], [d_mixed.reshape(shape)])
+        grads = attend_back(place_ref, message, query_places, lse, turn_square(grad))
+        grads = turn_square(grads)
+        wide = jax.ShapeDtypeStruct(shape, f32)
+        out_grad = along_first(mixed, d_branch).reshape(1, 2, ROWS, width)
+        out_grad = jnp.where(core == jnp.arange(2).reshape(2, 1, 1, 1), out_grad, 0.0).astype(bf16)
+        return (
+            whole_call(unpack_grad_kernel, [wide] * 3, [core_ref, place_ref], [grads]),
+            sum_split(from_corner, out_grad.reshape(SQUARE, ROWS, width)),
+        )
+
+    (d_query, d_key, d_value), out_split = region(attended_back, d_mixed, message, lse, d_branch, mixed)
+    d_query, line_came = together(d_query, line_came)
+    hidden_grad = jnp.stack(
+        [lax.dynamic_index_in_dim(hidden_grad, place, 0, keepdims=False), *line_came]
+    )
+    hidden_other = swap_core(hidden_grad)
+    down_other = swap_core(down_grad)
+    out_came = sum_first(out_split)
+    d_query = rotated_back(d_query.reshape(tokens, heads))
+    d_key = rotated_back(d_key.reshape(tokens, heads))
+    d_value = d_value.reshape(tokens, heads).astype(bf16)
+    query_gain_part = jnp.sum(d_query * q_raw * q_scale, axis=0)
+    key_gain_part = jnp.sum(d_key * k_raw * k_scale, axis=0)
+    d_query = d_query * head_gain[0]
+    d_key = d_key * head_gain[1]
+
+    def head_gains(value):
+        for move in (along(X), along(Y), swap_core):
+            (came,) = yield [(value, move)]
+            value = value + came
+        return value
+
+    def all_norms(value):
+        for move in (along(Z), along(FAR), swap_core, along(X), along(Y)):
+            (came,) = yield [(value, move)]
+            value = value + came
+        return value
+
+    head_part = jnp.stack([query_gain_part, key_gain_part]).reshape(2, 1, 2, HEAD)
+    head_part = jnp.where(core == jnp.arange(2).reshape(1, 2, 1, 1), head_part, 0.0)
+    sums, head_grads, norms = region(
+        lambda *given: run(sums_track(given[0]), head_gains(given[1]), all_norms(given[2])),
+        row_sums(d_query * q_raw, d_key * k_raw),
+        head_part,
+        norms,
+    )
+    sums, out_came = together(sums, out_came)
+    out_kept, out_came = sum_second(out_split, out_came)
+    head_grads = lax.dynamic_index_in_dim(head_grads.reshape(2, SQUARE, HEAD), corner, 1, keepdims=False)
+    norms = lax.dynamic_index_in_dim(norms.reshape(2, BLOCKS, ROWS), shard_index, 1, keepdims=False)
+    means = row_means(sums)
+    d_query = (d_query * q_scale - q_raw * q_scale**3 * means[0]).astype(bf16)
+    d_key = (d_key * k_scale - k_raw * k_scale**3 * means[1]).astype(bf16)
+    d_qkv = jnp.concatenate([d_query, d_key, d_value], axis=1)
+    total = across_cores(d_qkv, qkv_w, along_last)
+    qkv_split = sum_split(
+        from_order, along_first(x_all, d_qkv).astype(bf16).reshape(BLOCKS, ROWS, -1)
+    )
+    total, qkv_split = together(total, qkv_split)
+    qkv_came = sum_first(qkv_split)
+
+    def inputs_begun(total, hidden_grad, hidden_other):
+        hidden_grads = spread_columns(core_ref, slot_places, hidden_grad, hidden_other, 2, SQUARE)
+        return alone(scatter_first(total)), hidden_grads
+
+    carried, (gate_grad, up_grad) = region(inputs_begun, total, hidden_grad, hidden_other)
+    total, carried, qkv_came, out_came = together(total, carried, qkv_came, out_came)
+    qkv_kept, qkv_came = sum_second(qkv_split, qkv_came)
+    out_grad = sum_end(out_kept, out_came)[0]
+    out_other = swap_core(out_grad)
+    input_grad = region(
+        lambda total, carried: d_resid + alone(scatter_second(total, *carried)), total, carried
+    )
+    input_grad, qkv_came = together(input_grad, qkv_came)
+    qkv_grad = alone(turn_line(sum_end(qkv_kept, qkv_came)))
+    query_grad, key_grad, value_grad = spread_columns(
+        core_ref, slot_places, qkv_grad, swap_core(qkv_grad), 3, 1
+    )
+    down_grad = jnp.concatenate(
+        [jnp.where(core, down_other, down_grad), jnp.where(core, down_grad, down_other)]
+    )
+    return (
+        output,
+        input_grad,
+        query_grad,
+        key_grad,
+        value_grad,
+        out_grad.astype(f32) + out_other.astype(f32),
+        head_grads[0],
+        head_grads[1],
+        norms[0],
+        gate_grad,
+        up_grad,
+        down_grad.astype(f32),
+        norms[1],
+    )
+
+
 def solution(mesh):
+    on_line = mesh.shape["grp"] == 2 and mesh.shape["shard"] == 16
     placed = (
         P(("grp", "shard"), None),
         P(("grp", "shard")),
@@ -285,7 +1150,7 @@
         P("shard"),
     )
     return jax.shard_map(
-        local,
+        local_line if on_line else local_general,
         mesh=mesh,
         in_specs=placed,
         out_specs=(

time: 7290 us -> 913 us (0.13)
  waiting for transfers between devices: 6550 us -> 378 us
  matrix products: 332 us -> 94 us
  blocking collectives: 153 us -> 10.4 us
  Pallas kernels: 0 us -> 97.6 us
    reduce_scatter x5 -> x0, waiting for transfers between devices: 4880 us -> none  [the longest x2 2080 us: reduce_three(): lax.psum_scatter(first_term, 'shard', scatter_dimension=0, tiled=True)]
    all_gather x7 -> x0, waiting for transfers between devices: 1330 us -> none  [the longest x1 422 us: local(): lax.all_gather(w_gate, 'shard', axis=0, tiled=True)]
    all_gather x4 -> x0, blocking collectives: 151 us -> none  [the longest x1 42.4 us: local(): lax.all_gather(query_gain, 'shard', axis=0, tiled=True)]
    dot_general x13 -> x6, matrix products: 154 us -> 31.2 us  [dot(): return jnp.dot(left, right, preferred_element_type=f32)]
    ppermute x16 -> x107, waiting for transfers between devices: 231 us -> 330 us  [the longest x40 228 us: line_move(): return lambda value: lax.ppermute(value, 'shard', pairs)]
    pallas_call x0 -> x36, Pallas kernels: none -> 97.6 us  [whole_call(): pl.pallas_call(kernel, out_shape=shapes[0] if single else shapes, in_spec...]
    ppermute x16 -> x107, starting transfers between devices: 98.8 us -> 158 us  [the longest x40 99.2 us: line_move(): return lambda value: lax.ppermute(value, 'shard', pairs)]
  transfers between devices with their start and end apart: 30 -> 110, of which waited for: 21 -> 58; matrix products, arithmetic and copies ran while one was open for 5% -> 14% of each run, Pallas kernels for 0% -> 8%
where the time goes in v2:
time: 913 us; the launch traced here: 900 us
  waiting for transfers between devices  378 us (41%)
  starting transfers between devices  171 us (19%)
  Pallas kernels  97.6 us (11%)
  matrix products  94 us (10%)
  local copies, waits for them, and re-layouts  78.2 us (9%)
  other arithmetic  66.8 us (7%)
  blocking collectives  10.4 us (1%)
    ppermute x40, waiting for transfers between devices, line_move(): return lambda value: lax.ppermute(value, 'shard', pairs)  228 us
    ppermute x40, starting transfers between devices, line_move(): return lambda value: lax.ppermute(value, 'shard', pairs)  99.2 us
    pallas_call x36, Pallas kernels, whole_call(): pl.pallas_call(kernel, out_shape=shapes[0] if single else shapes, in_spec...  97.6 us
    all_to_all x3, waiting for transfers between devices, turn_square(): lax.all_to_all(message, 'shard', 0, 0, tiled=True, axis_index_groups=SQUA...  48.2 us
    ppermute x38, waiting for transfers between devices, swap(): lax.ppermute(value, 'shard', [(source, source ^ bit) for source in range(...  47.1 us
    ppermute x38, starting transfers between devices, swap(): lax.ppermute(value, 'shard', [(source, source ^ bit) for source in range(...  39.2 us
    dot_general x6, matrix products, along_last(): lax.dot_general(left, right, (((1,), (1,)), ((), ())), preferred_element_...  36 us
    unnamed x155, local copies, waits for them, and re-layouts  33.4 us
  transfers between devices with their start and end apart: 110, of which 58 were waited for; matrix products, arithmetic and copies ran while one was open for 14% of the time, Pallas kernels for 8%

profile of v2, /device:TPU:0, one launch (start us, length us, event | category | flops | bytes accessed | tf_op | source)
XLA Modules:
  0.0 900.1 jit_solution(7326581008899172942)
XLA Ops:
  44.4 10.4 %collective-permute-done.51.first_ref = bf16[4,144,384]{2,1,0:T(8,128)(2,1)} collective-permute-done((bf16[4,144,384]{2,1,0:T(8,128)(2,1)}, bf16[4,144,384]{2,1,0:T(8,128)(2,1)}, u32[]{:S(2)}, u32[]{:S(2)}) %collective-permute-start.51) | collective-permute-done | bytes 442400 | tf_op jit(solution)/shard_map/ppermute | solution.py:285
  122.5 10.5 %collective-permute-done.61.firsts_ref = bf16[2,1,256,1024]{3,2,1,0:T(8,128)(2,1)} collective-permute-done((bf16[2,1,256,1024]{3,2,1,0:T(8,128)(2,1)}, bf16[2,1,256,1024]{3,2,1,0:T(8,128)(2,1)}, u32[]{:S(2)}, u32[]{:S(2)}) %collective-permute-start.61) | collective-permute-done | bytes 1048608 | tf_op jit(solution)/shard_map/ppermute | solution.py:285
  142.1 59.5 %conditional.12 = (bf16[4,16,128,128]{3,2,1,0:T(8,128)(2,1)}, f32[16,128,1]{2,1,0:T(8,128)}, bf16[1024,256]{1,0:T(8,128)(2,1)}) conditional(s32[]{:T(128)} %bitcast.21, () %tuple.156, (bf16[1024,256]{0,1:T(8,128)(2,1)S(1)}, bf16[1024,256]{0,1:T(8,128)(2,1)S(1)}, bf16[1024,768]{0,1:T(8,128)(2,1)}, s32[1]{0:T(128)}, s32[1]{0:T(128)}, ...), branch_computations={%region_4.5_spmd, %region_5.6_spmd} | conditional | bytes 22052920 | solution.py:851
  152.7 23.8 %all-to-all-done.message_ref = bf16[4,16,128,128]{3,2,1,0:T(8,128)(2,1)} async-done(((bf16[4,16,128,128]{3,2,1,0:T(8,128)(2,1)}), bf16[4,16,128,128]{3,2,1,0:T(8,128)(2,1)}, u32[]{:S(2)}, u32[]{:S(2)}) %all-to-all-start) | async-done | bytes 2097184 | tf_op jit(solution)/shard_map/cond/branch_1_fun/all_to_all | solution.py:811
  176.5 13.8 %branch_1_fun.13 = (bf16[4,4,128,128]{3,2,1,0:T(8,128)(2,1)S(1)}, f32[16,128,1]{2,1,0:T(8,128)}) custom-call(s32[1]{0:T(128)} %get-tuple-element.136.place_ref, bf16[4,16,128,128]{3,2,1,0:T(8,128)(2,1)} %all-to-all-done.message_ref, s32[16,128,1]{2,1,0:T(8,128)S(1)} %copy.69.pos_ref), custom_call_target="tpu_custom_call" | custom-call | bytes 4210688 | tf_op jit(solution)/shard_map/cond/branch_1_fun/pallas_call | solution.py:577
  190.3 10.4 %all_to_all.16.came_ref = bf16[4,4,128,128]{3,2,1,0:T(8,128)(2,1)S(1)} all-to-all(bf16[4,4,128,128]{3,2,1,0:T(8,128)(2,1)S(1)} %get-tuple-element.142), channel_id=1, replica_groups={{0,1,2,3},{4,5,6,7},{8,9,10,11},{12,13,14,15},{16,17,18,19},{20,21,22,2..., dimensions={0} | all-to-all | bytes 1048576 | tf_op jit(solution)/shard_map/cond/branch_1_fun/all_to_all | solution.py:811
  210.8 64.5 %conditional.13 = (f32[128,2048]{1,0:T(8,128)}) conditional(s32[]{:T(128)} %bitcast.21, () %tuple.155, (bf16[1024,256]{1,0:T(8,128)(2,1)}, bf16[256,2048]{1,0:T(8,128)(2,1)}) %tuple.340), branch_computations={%region_6.7_spmd, %region_7.8_spmd} | conditional | flops 1083179008 | bytes 45089240 | solution.py:851
  238.9 10.5 %collective-permute-done.24 = bf16[128,2048]{1,0:T(8,128)(2,1)} collective-permute-done((bf16[128,2048]{1,0:T(8,128)(2,1)}, bf16[128,2048]{1,0:T(8,128)(2,1)}, u32[]{:S(2)}, u32[]{:S(2)}) %collective-permute-start.24) | collective-permute-done | bytes 524320 | tf_op jit(solution)/shard_map/cond/branch_1_fun/ppermute | solution.py:306
  285.6 50.2 %conditional.14 = (f32[128,1]{0,1:T(1,128)S(1)}, f32[128,2048]{1,0:T(8,128)S(1)}, bf16[1024,2048]{1,0:T(8,128)(2,1)}) conditional(s32[]{:T(128)} %bitcast.21, () %tuple.154, (f32[128,2048]{1,0:T(8,128)S(1)}, bf16[128,2048]{1,0:T(8,128)(2,1)}, f32[4,2048]{1,0:T(4,128)S(1)}) %tuple.338), branch_computations={%region_8.9_spmd, %region_9.11_spmd} | conditional | flops 2097298 | bytes 43543512 | solution.py:851
  306.4 12.8 %collective-permute-done.18.lefts_ref = bf16[128,2048]{1,0:T(8,128)(2,1)S(1)} collective-permute-done((bf16[128,2048]{1,0:T(8,128)(2,1)S(1)}, bf16[128,2048]{1,0:T(8,128)(2,1)S(1)}, u32[]{:S(2)}, u32[]{:S(2)}) %collective-permute-start.18) | collective-permute-done | bytes 524320 | tf_op jit(solution)/shard_map/cond/branch_1_fun/ppermute | solution.py:306
  342.9 12.5 %fusion.80 = f32[1024,2048]{1,0:T(8,128)S(1)} fusion(bf16[1024,2048]{1,0:T(8,128)(2,1)} %get-tuple-element.514, bf16[2048,2048]{1,0:T(8,128)(2,1)} %bitcast.212), kind=kOutput, calls=%fused_computation.253 | convolution fusion | flops 8589934592 | bytes 20971520 | tf_op jit(solution)/shard_map/dot_general | solution.py:859
  387.9 10.7 %collective-permute-done.74 = bf16[128,2048]{1,0:T(8,128)(2,1)} collective-permute-done((bf16[128,2048]{1,0:T(8,128)(2,1)}, bf16[128,2048]{1,0:T(8,128)(2,1)}, u32[]{:S(2)}, u32[]{:S(2)}) %collective-permute-start.74) | collective-permute-done | bytes 524320 | tf_op jit(solution)/shard_map/ppermute | solution.py:306
  441.6 13.8 %collective-permute-done.80.lefts_ref = bf16[128,2048]{1,0:T(8,128)(2,1)S(1)} collective-permute-done((bf16[128,2048]{1,0:T(8,128)(2,1)S(1)}, bf16[128,2048]{1,0:T(8,128)(2,1)S(1)}, u32[]{:S(2)}, u32[]{:S(2)}) %collective-permute-start.80) | collective-permute-done | bytes 524320 | tf_op jit(solution)/shard_map/ppermute | solution.py:306
  496.4 13.6 %convolution_convert_fusion.2 = bf16[2048,2048]{1,0:T(8,128)(2,1)} fusion(bf16[1024,2048]{1,0:T(8,128)(2,1)} %get-tuple-element.514, bf16[1024,1024]{1,0:T(8,128)(2,1)S(1)} %copy-done.83, bf16[1024,1024]{1,0:T(8,128)(2,1)S(1)} %copy-done.84), kind=kOutput, calls=%fused_computation.40 | convolution fusion | flops 8602517504 | bytes 16777216 | tf_op jit(solution)/shard_map/dot_general | solution.py:50
  532.2 50.6 %conditional.15 = (f32[128,2048]{1,0:T(8,128)}) conditional(s32[]{:T(128)} %bitcast.21, () %tuple.182, (bf16[512,2048]{1,0:T(8,128)(2,1)}, f32[128,2048]{1,0:T(8,128)}) %tuple.188), branch_computations={%region_13.14_spmd, %region_14.15_spmd} | conditional | flops 5505044 | bytes 24641972 | solution.py:851
  582.9 20.3 %conditional.16 = (bf16[128,2048]{1,0:T(8,128)(2,1)}, bf16[128,2048]{1,0:T(8,128)(2,1)}, bf16[128,2048]{1,0:T(8,128)(2,1)}, f32[2,2048]{1,0:T(2,128)S(1)}) conditional(s32[]{:T(128)} %bitcast.21, () %tuple.181, (f32[128,1]{0,1:T(1,128)S(1)}, f32[4,2048]{1,0:T(4,128)S(1)}, f32[128,2048]{1,0:T(8,128)}, f32[128,2048]{1,0:T(8,128)}, ...), branch_computations={%region_15.16_spmd, %region_16.20_spmd} | conditional | flops 3932416 | bytes 20533928 | solution.py:851
  614.0 39.0 %conditional.17 = (bf16[1024,2048]{1,0:T(8,128)(2,1)}, bf16[1024,256]{1,0:T(8,128)(2,1)}) conditional(s32[]{:T(128)} %bitcast.21, () %tuple.180, (bf16[128,2048]{1,0:T(8,128)(2,1)}, bf16[128,2048]{1,0:T(8,128)(2,1)}, bf16[128,2048]{1,0:T(8,128)(2,1)}, bf16[256,2048]{1,0:T(8,128)(2,1)}) %tuple.341), branch_computations={%region_20.21_spmd, %region_21.22_spmd} | conditional | flops 1074266112 | bytes 40894848 | solution.py:851
  618.4 13.2 %collective-permute-done.28.lefts_ref = bf16[128,2048]{1,0:T(8,128)(2,1)S(1)} collective-permute-done((bf16[128,2048]{1,0:T(8,128)(2,1)}, bf16[128,2048]{1,0:T(8,128)(2,1)S(1)}, u32[]{:S(2)}, u32[]{:S(2)}) %collective-permute-start.28) | collective-permute-done | bytes 524320 | tf_op jit(solution)/shard_map/cond/branch_1_fun/ppermute | solution.py:306
  667.1 83.4 %conditional.18 = (f32[2,4,128,256]{3,2,1,0:T(8,128)}, bf16[2,1,128,1024]{3,2,1,0:T(8,128)(2,1)}, bf16[2,1,128,1024]{3,2,1,0:T(8,128)(2,1)}, bf16[2,1,128,1024]{...) conditional(s32[]{:T(128)} %bitcast.21, () %tuple.179, ...), branch_computations={%region_22.23_spmd, %region_23.24_spmd} | conditional | flops 1075052544 | bytes 59326788 | solution.py:851
  682.5 15.8 %branch_1_fun.20 = bf16[4,16,128,128]{3,2,1,0:T(8,128)(2,1)S(1)} custom-call(s32[1]{0:T(128)} %get-tuple-element.202.place_ref, bf16[4,16,128,128]{3,2,1,0:T(8,128)(2,1)} %get-tuple-element.203.message_ref, s32[16,128,1]{2,1,0:T(8,128)S(1)} %copy-done.13, f32[16,128,1]{2,1,0:T(8,128)} %get-tuple-element.205.lse_ref, ...), custom_call_target="tpu_custom_call" | custom-call | bytes 5275648 | tf_op jit(solution)/shard_map/cond/branch_1_fun/pallas_call | solution.py:577
  710.5 17.6 %all-to-all-done.3.came_ref = bf16[4,16,128,128]{3,2,1,0:T(8,128)(2,1)} async-done(((bf16[4,16,128,128]{3,2,1,0:T(8,128)(2,1)}), bf16[4,16,128,128]{3,2,1,0:T(8,128)(2,1)}, u32[]{:S(2)}, u32[]{:S(2)}) %all-to-all-start.3) | async-done | bytes 2097184 | tf_op jit(solution)/shard_map/cond/branch_1_fun/all_to_all | solution.py:811
  760.8 22.2 %conditional.19 = (f32[4,2,2,128]{3,2,1,0:T(2,128)S(1)}, f32[2,4,128]{2,1,0:T(4,128)S(1)}, f32[2,16,128]{2,1,0:T(8,128)S(1)}) conditional(s32[]{:T(128)} %bitcast.21, () %tuple.195, (s32[]{:T(128)}, s32[1,2,1,1]{1,3,2,0:T(1,128)S(1)}, f32[2,1,2,128]{3,2,1,0:T(2,128)S(1)}, f32[4,2,2,128]{3,2,1,0:T(2,128)S(1)}, f32[2,2048]{1,0:T(2,128)S(1)}) %tuple.196), branch_computations={%region_28.29_spmd, %region_29.30_spmd} | conditional | flops 33794 | bytes 887268 | solution.py:851
  805.6 26.2 %conditional.20 = (bf16[128,2048]{1,0:T(8,128)(2,1)}, bf16[128,2048]{1,0:T(8,128)(2,1)}, bf16[128,2048]{1,0:T(8,128)(2,1)}, f32[128,8192]{1,0:T(8,128)}, f32[128,8192]{1,0:T(8,128)}) conditional(s32[]{:T(128)} %bitcast.21, () %tuple.199, (bf16[512,2048]{1,0:T(8,128)(2,1)}, s32[1]{0:T(128)}, s32[4]{0:T(128)S(1)}, bf16[4,128,2048]{2,1,0:T(8,128)(2,1)}, ...), branch_computations={%region_30.31_spmd, %region_31.32_spmd} | conditional | flops 262162 | bytes 17301844 | solution.py:851
  849.0 26.4 %conditional.21 = (f32[128,2048]{1,0:T(8,128)}) conditional(s32[]{:T(128)} %bitcast.21, () %tuple.178, (bf16[512,2048]{1,0:T(8,128)(2,1)}, bf16[128,2048]{1,0:T(8,128)(2,1)}, bf16[128,2048]{1,0:T(8,128)(2,1)}, bf16[128,2048]{1,0:T(8,128)(2,1)}, f32[128,2048]{1,0:T(8,128)}) %tuple.202), branch_computations={%region_32.33_spmd, %region_33.34_spmd} | conditional | flops 5242899 | bytes 15728946 | solution.py:851
  (584 shorter events, 716.2 us)
Async XLA Ops:
  7.9 30.5 %collective-permute-start.47 = (bf16[1,256,1024]{2,1,0:T(8,128)(2,1)}, bf16[1,256,1024]{2,1,0:T(8,128)(2,1)S(1)}, u32[]{:S(2)}, u32[]{:S(2)}) collective-permute-start(bf16[1,256,1024]{2,1,0:T(8,128)(2,1)} %get-tuple-element.461), channel_id=1, source_target_pairs={{0,1},{1,0},{2,3},{3,2},{4,5},{5,4},{6,7},{7,6},{8,9},{9,8},{10,11... | collective-permute-start | bytes 1572872 | tf_op jit(solution)/shard_map/ppermute | solution.py:285
  99.6 33.4 %collective-permute-start.61 = (bf16[2,1,256,1024]{3,2,1,0:T(8,128)(2,1)}, bf16[2,1,256,1024]{3,2,1,0:T(8,128)(2,1)}, u32[]{:S(2)}, u32[]{:S(2)}) collective-permute-start(bf16[2,1,256,1024]{3,2,1,0:T(8,128)(2,1)} %get-tuple-element.494), channel_id=1, source_target_pairs={{0,2},{1,3},{2,0},{3,1},{4,6},{5,7},{6,4},{7,5},{8,10},{9,11},{10,... | collective-permute-start | bytes 3145736 | tf_op jit(solution)/shard_map/ppermute | solution.py:285
  101.4 32.9 %collective-permute-start.62 = (bf16[2,1,256,1024]{3,2,1,0:T(8,128)(2,1)}, bf16[2,1,256,1024]{3,2,1,0:T(8,128)(2,1)}, u32[]{:S(2)}, u32[]{:S(2)}) collective-permute-start(bf16[2,1,256,1024]{3,2,1,0:T(8,128)(2,1)} %get-tuple-element.495), channel_id=1, source_target_pairs={{0,1},{1,0},{2,3},{3,2},{4,5},{5,4},{6,7},{7,6},{8,9},{9,8},{10,11... | collective-permute-start | bytes 3145736 | tf_op jit(solution)/shard_map/ppermute | solution.py:285
  135.7 65.8 %collective-permute-start.64 = (bf16[128,2048]{1,0:T(8,128)(2,1)}, bf16[128,2048]{1,0:T(8,128)(2,1)}, u32[]{:S(2)}, u32[]{:S(2)}) collective-permute-start(bf16[128,2048]{1,0:T(8,128)(2,1)} %get-tuple-element.751), channel_id=1, source_target_pairs={{0,4},{1,5},{2,6},{3,7},{4,8},{5,9},{6,10},{7,11},{8,12},{9,13},{1... | collective-permute-start | bytes 1572872 | tf_op jit(solution)/shard_map/ppermute | solution.py:314
  135.7 65.8 %collective-permute-start.65 = (bf16[128,2048]{1,0:T(8,128)(2,1)}, bf16[128,2048]{1,0:T(8,128)(2,1)}, u32[]{:S(2)}, u32[]{:S(2)}) collective-permute-start(bf16[128,2048]{1,0:T(8,128)(2,1)} %get-tuple-element.750), channel_id=1, source_target_pairs={{0,8},{1,9},{2,10},{3,11},{4,12},{5,13},{6,14},{7,15},{8,0},{9,1},... | collective-permute-start | bytes 1572872 | tf_op jit(solution)/shard_map/ppermute | solution.py:314
  135.7 65.8 %collective-permute-start.66 = (bf16[128,2048]{1,0:T(8,128)(2,1)}, bf16[128,2048]{1,0:T(8,128)(2,1)}, u32[]{:S(2)}, u32[]{:S(2)}) collective-permute-start(bf16[128,2048]{1,0:T(8,128)(2,1)} %get-tuple-element.749), channel_id=1, source_target_pairs={{0,12},{1,13},{2,14},{3,15},{4,0},{5,1},{6,2},{7,3},{8,4},{9,5},{1... | collective-permute-start | bytes 1572872 | tf_op jit(solution)/shard_map/ppermute | solution.py:314
  204.9 70.4 %collective-permute-start.67 = (bf16[4,128,1024]{2,1,0:T(8,128)(2,1)}, bf16[4,128,1024]{2,1,0:T(8,128)(2,1)}, u32[]{:S(2)}, u32[]{:S(2)}) collective-permute-start(bf16[4,128,1024]{2,1,0:T(8,128)(2,1)} %get-tuple-element.747), channel_id=1, source_target_pairs={{0,1},{1,0},{2,3},{3,2},{4,5},{5,4},{6,7},{7,6},{8,9},{9,8},{10,11... | collective-permute-start | bytes 3145736 | tf_op jit(solution)/shard_map/ppermute | solution.py:285
  205.8 69.5 %collective-permute-start.68 = (bf16[4,128,1024]{2,1,0:T(8,128)(2,1)}, bf16[4,128,1024]{2,1,0:T(8,128)(2,1)}, u32[]{:S(2)}, u32[]{:S(2)}) collective-permute-start(bf16[4,128,1024]{2,1,0:T(8,128)(2,1)} %get-tuple-element.746), channel_id=1, source_target_pairs={{0,2},{1,3},{2,0},{3,1},{4,6},{5,7},{6,4},{7,5},{8,10},{9,11},{10,... | collective-permute-start | bytes 3145736 | tf_op jit(solution)/shard_map/ppermute | solution.py:285
  279.1 56.8 %collective-permute-start.69 = (bf16[2,4,128,1024]{3,2,1,0:T(8,128)(2,1)}, bf16[2,4,128,1024]{3,2,1,0:T(8,128)(2,1)}, u32[]{:S(2)}, u32[]{:S(2)}) collective-permute-start(bf16[2,4,128,1024]{3,2,1,0:T(8,128)(2,1)} %get-tuple-element.512), channel_id=1, source_target_pairs={{0,2},{1,3},{2,0},{3,1},{4,6},{5,7},{6,4},{7,5},{8,10},{9,11},{10,... | collective-permute-start | bytes 6291464 | tf_op jit(solution)/shard_map/ppermute | solution.py:285
  280.6 55.3 %collective-permute-start.70 = (bf16[2,4,128,1024]{3,2,1,0:T(8,128)(2,1)}, bf16[2,4,128,1024]{3,2,1,0:T(8,128)(2,1)}, u32[]{:S(2)}, u32[]{:S(2)}) collective-permute-start(bf16[2,4,128,1024]{3,2,1,0:T(8,128)(2,1)} %get-tuple-element.513), channel_id=1, source_target_pairs={{0,1},{1,0},{2,3},{3,2},{4,5},{5,4},{6,7},{7,6},{8,9},{9,8},{10,11... | collective-permute-start | bytes 6291464 | tf_op jit(solution)/shard_map/ppermute | solution.py:285
  529.6 73.6 %collective-permute-start.84 = (bf16[2,6,128,1024]{3,2,1,0:T(8,128)(2,1)}, bf16[2,6,128,1024]{3,2,1,0:T(8,128)(2,1)}, u32[]{:S(2)}, u32[]{:S(2)}) collective-permute-start(bf16[2,6,128,1024]{3,2,1,0:T(8,128)(2,1)} %pad_maximum_fusion.4), channel_id=1, source_target_pairs={{0,2},{1,3},{2,0},{3,1},{4,6},{5,7},{6,4},{7,5},{8,10},{9,11},{10,... | collective-permute-start | bytes 9437192 | tf_op jit(solution)/shard_map/ppermute | solution.py:285
  530.5 72.8 %collective-permute-start.85 = (bf16[2,6,128,1024]{3,2,1,0:T(8,128)(2,1)}, bf16[2,6,128,1024]{3,2,1,0:T(8,128)(2,1)}, u32[]{:S(2)}, u32[]{:S(2)}) collective-permute-start(bf16[2,6,128,1024]{3,2,1,0:T(8,128)(2,1)} %pad_maximum_fusion.6), channel_id=1, source_target_pairs={{0,1},{1,0},{2,3},{3,2},{4,5},{5,4},{6,7},{7,6},{8,9},{9,8},{10,11... | collective-permute-start | bytes 9437192 | tf_op jit(solution)/shard_map/ppermute | solution.py:285
  611.4 41.5 %collective-permute-start.86 = (bf16[6,128,1024]{2,1,0:T(8,128)(2,1)}, bf16[6,128,1024]{2,1,0:T(8,128)(2,1)S(1)}, u32[]{:S(2)}, u32[]{:S(2)}) collective-permute-start(bf16[6,128,1024]{2,1,0:T(8,128)(2,1)} %get-tuple-element.562), channel_id=1, source_target_pairs={{0,1},{1,0},{2,3},{3,2},{4,5},{5,4},{6,7},{7,6},{8,9},{9,8},{10,11... | collective-permute-start | bytes 4718600 | tf_op jit(solution)/shard_map/ppermute | solution.py:285
  612.8 41.3 %collective-permute-start.87 = (bf16[6,128,1024]{2,1,0:T(8,128)(2,1)}, bf16[6,128,1024]{2,1,0:T(8,128)(2,1)S(1)}, u32[]{:S(2)}, u32[]{:S(2)}) collective-permute-start(bf16[6,128,1024]{2,1,0:T(8,128)(2,1)} %get-tuple-element.563), channel_id=1, source_target_pairs={{0,2},{1,3},{2,0},{3,1},{4,6},{5,7},{6,4},{7,5},{8,10},{9,11},{10,... | collective-permute-start | bytes 4718600 | tf_op jit(solution)/shard_map/ppermute | solution.py:285
  663.2 89.3 %collective-permute-start.88 = (bf16[128,2048]{1,0:T(8,128)(2,1)}, bf16[128,2048]{1,0:T(8,128)(2,1)}, u32[]{:S(2)}, u32[]{:S(2)}) collective-permute-start(bf16[128,2048]{1,0:T(8,128)(2,1)} %get-tuple-element.743), channel_id=1, source_target_pairs={{0,4},{1,5},{2,6},{3,7},{4,8},{5,9},{6,10},{7,11},{8,12},{9,13},{1... | collective-permute-start | bytes 1572872 | tf_op jit(solution)/shard_map/ppermute | solution.py:314
  663.2 89.3 %collective-permute-start.89 = (bf16[128,2048]{1,0:T(8,128)(2,1)}, bf16[128,2048]{1,0:T(8,128)(2,1)}, u32[]{:S(2)}, u32[]{:S(2)}) collective-permute-start(bf16[128,2048]{1,0:T(8,128)(2,1)} %get-tuple-element.742), channel_id=1, source_target_pairs={{0,8},{1,9},{2,10},{3,11},{4,12},{5,13},{6,14},{7,15},{8,0},{9,1},... | collective-permute-start | bytes 1572872 | tf_op jit(solution)/shard_map/ppermute | solution.py:314
  663.2 89.3 %collective-permute-start.90 = (bf16[128,2048]{1,0:T(8,128)(2,1)}, bf16[128,2048]{1,0:T(8,128)(2,1)}, u32[]{:S(2)}, u32[]{:S(2)}) collective-permute-start(bf16[128,2048]{1,0:T(8,128)(2,1)} %get-tuple-element.741), channel_id=1, source_target_pairs={{0,12},{1,13},{2,14},{3,15},{4,0},{5,1},{6,2},{7,3},{8,4},{9,5},{1... | collective-permute-start | bytes 1572872 | tf_op jit(solution)/shard_map/ppermute | solution.py:314
  750.5 32.5 %collective-permute-start.91 = (bf16[2,1,128,1024]{3,2,1,0:T(8,128)(2,1)}, bf16[2,1,128,1024]{3,2,1,0:T(8,128)(2,1)}, u32[]{:S(2)}, u32[]{:S(2)}) collective-permute-start(bf16[2,1,128,1024]{3,2,1,0:T(8,128)(2,1)} %get-tuple-element.581), channel_id=1, source_target_pairs={{0,2},{1,3},{2,0},{3,1},{4,6},{5,7},{6,4},{7,5},{8,10},{9,11},{10,... | collective-permute-start | bytes 1572872 | tf_op jit(solution)/shard_map/ppermute | solution.py:285
  752.0 31.1 %collective-permute-start.92 = (bf16[2,1,128,1024]{3,2,1,0:T(8,128)(2,1)}, bf16[2,1,128,1024]{3,2,1,0:T(8,128)(2,1)}, u32[]{:S(2)}, u32[]{:S(2)}) collective-permute-start(bf16[2,1,128,1024]{3,2,1,0:T(8,128)(2,1)} %get-tuple-element.582), channel_id=1, source_target_pairs={{0,1},{1,0},{2,3},{3,2},{4,5},{5,4},{6,7},{7,6},{8,9},{9,8},{10,11... | collective-permute-start | bytes 1572872 | tf_op jit(solution)/shard_map/ppermute | solution.py:285
  802.5 41.1 %collective-permute-start.95 = (bf16[2,4,128,384]{3,2,1,0:T(8,128)(2,1)}, bf16[2,4,128,384]{3,2,1,0:T(8,128)(2,1)}, u32[]{:S(2)}, u32[]{:S(2)}) collective-permute-start(bf16[2,4,128,384]{3,2,1,0:T(8,128)(2,1)} %get-tuple-element.596), channel_id=1, source_target_pairs={{0,2},{1,3},{2,0},{3,1},{4,6},{5,7},{6,4},{7,5},{8,10},{9,11},{10,... | collective-permute-start | bytes 2359304 | tf_op jit(solution)/shard_map/ppermute | solution.py:285
  804.0 39.6 %collective-permute-start.96 = (bf16[2,4,128,384]{3,2,1,0:T(8,128)(2,1)}, bf16[2,4,128,384]{3,2,1,0:T(8,128)(2,1)}, u32[]{:S(2)}, u32[]{:S(2)}) collective-permute-start(bf16[2,4,128,384]{3,2,1,0:T(8,128)(2,1)} %get-tuple-element.597), channel_id=1, source_target_pairs={{0,1},{1,0},{2,3},{3,2},{4,5},{5,4},{6,7},{7,6},{8,9},{9,8},{10,11... | collective-permute-start | bytes 2359304 | tf_op jit(solution)/shard_map/ppermute | solution.py:285
  831.8 48.0 %collective-permute-start.106 = (bf16[256,2048]{1,0:T(8,128)(2,1)}, bf16[256,2048]{1,0:T(8,128)(2,1)}, u32[]{:S(2)}, u32[]{:S(2)}) collective-permute-start(bf16[256,2048]{1,0:T(8,128)(2,1)} %bitcast.116), channel_id=1, source_target_pairs={{0,16},{16,0},{1,17},{17,1},{2,18},{18,2},{3,19},{19,3},{4,20},{20... | collective-permute-start | bytes 3145736 | tf_op jit(solution)/shard_map/ppermute | solution.py:289
  845.9 29.8 %collective-permute-start.99 = (bf16[4,128,384]{2,1,0:T(8,128)(2,1)}, bf16[4,128,384]{2,1,0:T(8,128)(2,1)S(1)}, u32[]{:S(2)}, u32[]{:S(2)}) collective-permute-start(bf16[4,128,384]{2,1,0:T(8,128)(2,1)} %get-tuple-element.612), channel_id=1, source_target_pairs={{0,1},{1,0},{2,3},{3,2},{4,5},{5,4},{6,7},{7,6},{8,9},{9,8},{10,11... | collective-permute-start | bytes 1179656 | tf_op jit(solution)/shard_map/ppermute | solution.py:285
  846.5 29.2 %collective-permute-start.100 = (bf16[4,128,384]{2,1,0:T(8,128)(2,1)}, bf16[4,128,384]{2,1,0:T(8,128)(2,1)S(1)}, u32[]{:S(2)}, u32[]{:S(2)}) collective-permute-start(bf16[4,128,384]{2,1,0:T(8,128)(2,1)} %get-tuple-element.613), channel_id=1, source_target_pairs={{0,2},{1,3},{2,0},{3,1},{4,6},{5,7},{6,4},{7,5},{8,10},{9,11},{10,... | collective-permute-start | bytes 1179656 | tf_op jit(solution)/shard_map/ppermute | solution.py:285
  (174 other events, 1959.2 us)

commit v3 on v2

--- a/solution.py
+++ b/solution.py
@@ -345,6 +345,11 @@
     return [results[name] for name in range(len(tracks))]
 
 
+def one(value, move):
+    (came,) = yield [(value, move)]
+    return came
+
+
 def alone(track):
     return run(track)[0]
 
@@ -544,11 +549,16 @@
                 targets[2 * number + place][block] = low_sum(kept[place, block], came[place, block])
 
 
-def sum_second(split, came):
+def sum_later(split, came):
     shape = jax.ShapeDtypeStruct(came[0].shape[1:], jnp.bfloat16)
     arrays = [split[0], came[0], split[2], came[1]]
     first, to_first, second, to_second = whole_call(add_kernel, [shape] * 4, [], arrays)
-    return (first, second), (swap(to_first, X), swap(to_second, Y))
+    return (first, second), (to_first, to_second)
+
+
+def sum_second(split, came):
+    kept, sent = sum_later(split, came)
+    return kept, (swap(sent[0], X), swap(sent[1], Y))
 
 
 def end_kernel(first_ref, came_first, second_ref, came_second, out_ref):
@@ -648,17 +658,36 @@
     return lax.rem(place + 2, LINE), lax.rem(place + 1, LINE)
 
 
-def pack_kernel(core_ref, place_ref, q_ref, k_ref, v_ref, out_ref):
+def rotated(value, cosines, sines):
+    return value * cosines + pltpu.roll(value, HEAD // 2, 1) * sines
+
+
+def rotated_back(value, cosines, sines):
+    return value * cosines - pltpu.roll(value, HEAD // 2, 1) * sines
+
+
+def part_of(group, core):
+    return core if group == 0 else 1 - core
+
+
+def pack_kernel(core_ref, place_ref, raw_ref, scale_ref, gain_ref, cos_ref, sin_ref, out_ref):
     for group in range(2):
-        part = core_ref[0] if group == 0 else 1 - core_ref[0]
+        part = part_of(group, core_ref[0])
         for head in range(2):
-            lanes, target = head_lanes(head), 2 * group + head
+            target = 2 * group + head
             for slot in range(LINE):
-                for number, ref in enumerate((q_ref, k_ref, v_ref)):
-                    out_ref[target, LINE * number + slot] = ref[part, slot, :, lanes]
-            for number, slot in enumerate(halo_slots(place_ref[0])):
-                out_ref[target, 12 + number] = k_ref[core_ref[0], slot, :, lanes]
-                out_ref[target, 14 + number] = v_ref[core_ref[0], slot, :, lanes]
+                for number in range(2):
+                    lanes = slice((2 * number + head) * HEAD, (2 * number + head + 1) * HEAD)
+                    value = raw_ref[part, slot, :, lanes] * scale_ref[number, part, slot]
+                    value = value * gain_ref[number : number + 1, head_lanes(head)]
+                    value = rotated(value, cos_ref[part, slot], sin_ref[part, slot])
+                    out_ref[target, LINE * number + slot] = value.astype(jnp.bfloat16)
+                lanes = slice((4 + head) * HEAD, (5 + head) * HEAD)
+                out_ref[target, 2 * LINE + slot] = raw_ref[part, slot, :, lanes].astype(jnp.bfloat16)
+    for target in range(SQUARE):
+        for number, slot in enumerate(halo_slots(place_ref[0])):
+            out_ref[target, 12 + number] = out_ref[target % 2, LINE + slot]
+            out_ref[target, 14 + number] = out_ref[target % 2, 2 * LINE + slot]
 
 
 def unpack_kernel(core_ref, came_ref, out_ref):
@@ -677,23 +706,73 @@
                 out_ref[2 * group + head, slot] = grad_ref[part, slot, :, head_lanes(head)]
 
 
-def unpack_grad_kernel(core_ref, place_ref, came_ref, dq_ref, dk_ref, dv_ref):
+def unpack_grad_kernel(
+    core_ref,
+    place_ref,
+    came_ref,
+    raw_ref,
+    scale_ref,
+    gain_ref,
+    cos_ref,
+    sin_ref,
+    grad_ref,
+    value_ref,
+    sums_ref,
+    gain_grad_ref,
+    d_key,
+    d_value,
+):
     for group in range(2):
-        part = core_ref[0] if group == 0 else 1 - core_ref[0]
+        part = part_of(group, core_ref[0])
         for head in range(2):
             for slot in range(LINE):
-                for number, ref in enumerate((dq_ref, dk_ref, dv_ref)):
+                for number, ref in ((1, d_key), (2, d_value)):
                     ref[part, slot, :, head_lanes(head)] = came_ref[
                         2 * group + head, LINE * number + slot
                     ].astype(jnp.float32)
     for head in range(2):
         for number, slot in enumerate(halo_slots(place_ref[0])):
-            dk_ref[core_ref[0], slot, :, head_lanes(head)] += came_ref[2 + head, 12 + number].astype(
-                jnp.float32
-            )
-            dv_ref[core_ref[0], slot, :, head_lanes(head)] += came_ref[2 + head, 14 + number].astype(
-                jnp.float32
-            )
+            for first, ref in ((12, d_key), (14, d_value)):
+                ref[core_ref[0], slot, :, head_lanes(head)] += came_ref[2 + head, first + number].astype(
+                    jnp.float32
+                )
+    totals = [[jnp.zeros((1, HEAD), jnp.float32) for _ in range(2)] for _ in range(2)]
+    for group in range(2):
+        part = part_of(group, core_ref[0])
+        for slot in range(LINE):
+            sums = [jnp.zeros((ROWS, 1), jnp.float32) for _ in range(2)]
+            for head in range(2):
+                lanes = head_lanes(head)
+                d_query = came_ref[2 * group + head, slot].astype(jnp.float32)
+                for number, grad in ((0, d_query), (1, d_key[part, slot, :, lanes])):
+                    grad = rotated_back(grad, cos_ref[part, slot], sin_ref[part, slot])
+                    raw_lanes = slice((2 * number + head) * HEAD, (2 * number + head + 1) * HEAD)
+                    raw = raw_ref[part, slot, :, raw_lanes]
+                    totals[number][head] += jnp.sum(
+                        grad * raw * scale_ref[number, part, slot], axis=0, keepdims=True
+                    )
+                    grad = grad * gain_ref[number : number + 1, lanes]
+                    sums[number] += jnp.sum(grad * raw, axis=1, keepdims=True)
+                    grad_ref[number, part, slot, :, lanes] = grad
+            for number in range(2):
+                sums_ref[number, part, slot] = sums[number]
+    for number in range(2):
+        for head in range(2):
+            gain_grad_ref[number : number + 1, head_lanes(head)] = totals[number][head]
+    value_ref[...] = d_value[...].astype(jnp.bfloat16)
+
+
+def norm_grad_kernel(grad_ref, value_ref, raw_ref, scale_ref, mean_ref, out_ref):
+    for part in range(2):
+        for slot in range(LINE):
+            for number in range(2):
+                lanes = slice(2 * number * HEAD, 2 * (number + 1) * HEAD)
+                scale = scale_ref[number, part, slot]
+                grad = grad_ref[number, part, slot] * scale - raw_ref[part, slot, :, lanes] * (
+                    scale * scale * scale * mean_ref[number, part, slot]
+                )
+                out_ref[part, slot, :, lanes] = grad.astype(jnp.bfloat16)
+            out_ref[part, slot, :, 4 * HEAD :] = value_ref[part, slot]
 
 
 def visible_of(place):
@@ -809,6 +888,23 @@
 
 def turn_square(message):
     return lax.all_to_all(message, "shard", 0, 0, tiled=True, axis_index_groups=SQUARES)
+
+
+def turned_kernel(place_ref, block_ref, *refs):
+    came_refs, (whole_ref, first_ref, second_ref) = refs[: LINE - 1], refs[LINE - 1 :]
+    half = whole_ref.shape[-1] // 2
+    own_ref = block_ref.at[place_ref[0]]
+    for slot, ref in enumerate((own_ref, *came_refs)):
+        whole_ref[slot] = ref[...]
+        first_ref[slot] = ref[:, :half]
+        second_ref[slot] = ref[:, half:]
+
+
+def turned_line(place_ref, block, came):
+    half = jax.ShapeDtypeStruct(block.shape[:-1] + (block.shape[-1] // 2,), block.dtype)
+    whole = jax.ShapeDtypeStruct(block.shape, block.dtype)
+    whole, *parts = whole_call(turned_kernel, [whole, half, half], [place_ref], [block, *came])
+    return whole, parts
 
 
 def local_line(
@@ -893,26 +989,10 @@
         for part in (stream, stream_other)
     ]
     middle = HEAD // 2
-    frequency = jnp.power(500000.0, -2.0 * jnp.arange(middle).astype(f32) / HEAD)
-    angles = jnp.stack(held).astype(f32).reshape(tokens, 1) * frequency[None, :]
-    cosines, sines = together(jnp.cos(angles), jnp.sin(angles))
-    cosines = jnp.concatenate([cosines] * 4, axis=1)
-    sines = jnp.concatenate([-sines, sines] * 2, axis=1)
-
-    def halves_swapped(values):
-        return jnp.concatenate(
-            [jnp.roll(values[:, head_lanes(head)], middle, axis=1) for head in range(2)], axis=1
-        )
-
-    def rotated(values):
-        return values * cosines + halves_swapped(values) * sines
-
-    def rotated_back(values):
-        return values * cosines - halves_swapped(values) * sines
-
-    def row_sums(first, second):
-        sums = jnp.stack([jnp.sum(first, axis=-1), jnp.sum(second, axis=-1)])
-        return to_slots(sums.reshape(2, 2, LINE, ROWS).transpose(2, 0, 1, 3))
+    frequency = jnp.power(500000.0, -2.0 * (jnp.arange(HEAD) % middle).astype(f32) / HEAD)
+    angles = jnp.stack(held).astype(f32)[..., None] * frequency
+    sign = jnp.where(jnp.arange(HEAD) < middle, -1.0, 1.0)
+    cosines, sines = together(jnp.cos(angles), jnp.sin(angles) * sign)
 
     def sums_track(value):
         for bit in (Z, FAR):
@@ -922,13 +1002,21 @@
         return value + jnp.flip(came, 2)
 
     def row_means(sums):
-        return to_slots(sums).transpose(1, 2, 0, 3).reshape(2, tokens, 1) / width
+        sums = to_slots(sums.transpose(2, 0, 1, 3))
+
+        def finish(sums):
+            return to_slots(sums).transpose(1, 2, 0, 3)[..., None] / width
+
+        return sums, finish
 
     raw = dot(x_all, qkv_w)
-    q_raw, k_raw, v_raw = raw[:, :heads], raw[:, heads : 2 * heads], raw[:, 2 * heads :]
-    sums = region(lambda sums: alone(sums_track(sums)), row_sums(q_raw * q_raw, k_raw * k_raw))
-    sums, out_later, down_later = together(sums, out_later, down_later)
-    down_w = square_join(from_corner, down_own, down_came, down_later).reshape(-1, width)
+    raw = raw.reshape(2, LINE, ROWS, 3 * heads)
+    squares = raw[..., : 2 * heads] * raw[..., : 2 * heads]
+    sums = jnp.stack([jnp.sum(squares[..., :heads], axis=-1), jnp.sum(squares[..., heads:], axis=-1)])
+    sums, finish = row_means(sums)
+    sums = region(lambda sums: alone(sums_track(sums)), sums)
+    sums, out_later = together(sums, out_later)
+    scales = lax.rsqrt(finish(sums) + 1e-06)
     out_w = square_join(from_corner, out_own, out_came, out_later)
     out_w = lax.dynamic_slice_in_dim(out_w, core_index * 2, 2, 0).reshape(heads, width)
 
@@ -937,31 +1025,32 @@
         line_turn(k)(lax.dynamic_index_in_dim(hidden_block, (place + k) % LINE, 0, keepdims=False))
         for k in range(1, LINE)
     ]
-    means = row_means(sums)
-    q_scale, k_scale = lax.rsqrt(means[0] + 1e-06), lax.rsqrt(means[1] + 1e-06)
     shape = (2, LINE, ROWS, heads)
-    query = rotated(q_raw * q_scale * head_gain[0]).astype(bf16).reshape(shape)
-    key = rotated(k_raw * k_scale * head_gain[1]).astype(bf16).reshape(shape)
-    value = v_raw.astype(bf16).reshape(shape)
     message_shape = jax.ShapeDtypeStruct((SQUARE, 16, ROWS, HEAD), bf16)
     heads_shape = jax.ShapeDtypeStruct((SQUARE, LINE, ROWS, HEAD), bf16)
     tokens_shape = jax.ShapeDtypeStruct(shape, bf16)
 
-    def attended(query, key, value):
-        message = turn_square(
-            whole_call(pack_kernel, [message_shape], [core_ref, place_ref], [query, key, value])
+    tables = [head_gain, cosines, sines]
+
+    def attended(raw, scales, *tables):
+        message = whole_call(
+            pack_kernel, [message_shape], [core_ref, place_ref], [raw, scales, *tables]
         )
+        message = turn_square(message)
         mixed, lse = attend(place_ref, message, query_places)
         mixed = whole_call(unpack_kernel, [tokens_shape], [core_ref], [turn_square(mixed)])
         return message, lse, mixed.reshape(tokens, heads)
 
-    message, lse, mixed = region(attended, query, key, value)
-    mixed, line_came = together(mixed, line_came)
-    hidden_own = jnp.stack(
-        [lax.dynamic_index_in_dim(hidden_block, place, 0, keepdims=False), *line_came]
-    )
-    hidden_came = square_first(hidden_own)
-    branch = region(lambda mixed: alone(scatter_line(across_cores(mixed, out_w, dot))), mixed)
+    message, lse, mixed = region(attended, raw, scales, *tables)
+    mixed, line_came, down_later = together(mixed, line_came, down_later)
+    hidden_own, parts = turned_line(place_ref, hidden_block, line_came)
+    hidden_came = swap(parts[0], X), swap(parts[1], Y)
+
+    def branch_of(mixed, out_w, *down):
+        down_w = square_join(from_corner, down[0], down[1:3], down[3:]).reshape(-1, width)
+        return alone(scatter_line(across_cores(mixed, out_w, dot))), down_w
+
+    branch, down_w = region(branch_of, mixed, out_w, down_own, *down_came, *down_later)
     branch, hidden_came = together(branch, hidden_came)
     hidden_later = square_second(hidden_own, hidden_came)
 
@@ -994,70 +1083,72 @@
     d_both = jnp.concatenate([d_gate, d_up], axis=1)
 
     total = across_cores(d_both, hidden_w, along_last)
-    hidden_split = sum_split(
-        from_order, along_first(state, d_both).astype(bf16).reshape(BLOCKS, ROWS, -1)
-    )
-    down_split = sum_split(
-        from_corner, along_first(active, d_mlp).astype(bf16).reshape(SQUARE, -1, width)
-    )
-    split = [
-        jnp.concatenate([first, second.reshape(2, -1, ROWS, second.shape[-1])], axis=1)
-        for first, second in zip(hidden_split, down_split)
-    ]
-    total, split = together(total, split)
-    grads_came = sum_first(split)
-    d_resid = region(lambda total: cot + alone(scatter_line(total)), total)
-    def d_branch_begun(d_resid):
+
+    def d_state_begun(total, state, d_both, active, d_mlp):
+        carried = alone(scatter_first(total))
+        hidden_grad = along_first(state, d_both).astype(bf16).reshape(BLOCKS, ROWS, -1)
+        down_grad = along_first(active, d_mlp).astype(bf16).reshape(SQUARE, -1, width)
+        return carried, sum_split(from_order, hidden_grad), sum_split(from_corner, down_grad)
+
+    carried, hidden_split, down_split = region(d_state_begun, total, state, d_both, active, d_mlp)
+    hidden_came = sum_first(hidden_split)
+
+    def d_branch_begun(total, *carried):
+        d_resid = cot + alone(scatter_second(total, *carried))
         scaled = d_resid * gains[2]
         d_branch = branch_scale * scaled - branch * branch_scale**3 * jnp.mean(
             branch * scaled, axis=-1, keepdims=True
         )
         attn_gain_part = jnp.sum(d_resid * branch * branch_scale, axis=0)
-        return alone(gather_first(d_branch.astype(bf16))), jnp.stack([attn_gain_part, mlp_gain_part])
+        norms = jnp.stack([attn_gain_part, mlp_gain_part])
+        return d_resid, alone(gather_first(d_branch.astype(bf16))), norms
 
     def d_branch_of(*came):
         d_branch = both_cores(alone(gather_second(*came)))
         return d_branch, along_last(d_branch, out_w).astype(bf16)
 
-    d_branch, norms = region(d_branch_begun, d_resid)
-    d_branch, grads_came = together(d_branch, grads_came)
-    grads_kept, grads_came = sum_second(split, grads_came)
+    d_resid, d_branch, norms = region(d_branch_begun, total, *carried)
+    d_branch, hidden_came = together(d_branch, hidden_came)
+    hidden_kept, hidden_came = sum_second(hidden_split, hidden_came)
     d_branch, d_mixed = region(d_branch_of, *d_branch)
-    d_mixed, grads_came = together(d_mixed, grads_came)
-    grads = sum_end(grads_kept, grads_came)
-    hidden_grad, down_grad = grads[:LINE], grads[LINE:].reshape(-1, width)
+    d_mixed, hidden_came = together(d_mixed, hidden_came)
+    hidden_grad = sum_end(hidden_kept, hidden_came)
+    down_came = sum_first(hold(down_split, hidden_came))
     line_came = [
         line_turn(k)(lax.dynamic_index_in_dim(hidden_grad, (place + k) % LINE, 0, keepdims=False))
         for k in range(1, LINE)
     ]
 
-    def attended_back(d_mixed, message, lse, d_branch, mixed):
+    def attended_back(d_mixed, message, lse, d_branch, mixed, raw, scales, *tables):
         grad = whole_call(pack_grad_kernel, [heads_shape], [core_ref], [d_mixed.reshape(shape)])
         grads = attend_back(place_ref, message, query_places, lse, turn_square(grad))
         grads = turn_square(grads)
-        wide = jax.ShapeDtypeStruct(shape, f32)
         out_grad = along_first(mixed, d_branch).reshape(1, 2, ROWS, width)
         out_grad = jnp.where(core == jnp.arange(2).reshape(2, 1, 1, 1), out_grad, 0.0).astype(bf16)
+        shapes = [
+            jax.ShapeDtypeStruct((2,) + shape, f32),
+            tokens_shape,
+            jax.ShapeDtypeStruct((2, 2, LINE, ROWS, 1), f32),
+            jax.ShapeDtypeStruct((2, heads), f32),
+        ]
         return (
-            whole_call(unpack_grad_kernel, [wide] * 3, [core_ref, place_ref], [grads]),
+            whole_call(
+                unpack_grad_kernel,
+                shapes,
+                [core_ref, place_ref],
+                [grads, raw, scales, *tables],
+                [pltpu.VMEM(shape, f32)] * 2,
+            ),
             sum_split(from_corner, out_grad.reshape(SQUARE, ROWS, width)),
         )
 
-    (d_query, d_key, d_value), out_split = region(attended_back, d_mixed, message, lse, d_branch, mixed)
-    d_query, line_came = together(d_query, line_came)
-    hidden_grad = jnp.stack(
-        [lax.dynamic_index_in_dim(hidden_grad, place, 0, keepdims=False), *line_came]
-    )
+    (d_head, d_value, sums, head_part), out_split = region(
+        attended_back, d_mixed, message, lse, d_branch, mixed, raw, scales, *tables
+    )
+    d_head, sums, line_came, down_came = together(d_head, sums, line_came, down_came)
+    hidden_grad, _ = turned_line(place_ref, hidden_grad, line_came)
     hidden_other = swap_core(hidden_grad)
-    down_other = swap_core(down_grad)
     out_came = sum_first(out_split)
-    d_query = rotated_back(d_query.reshape(tokens, heads))
-    d_key = rotated_back(d_key.reshape(tokens, heads))
-    d_value = d_value.reshape(tokens, heads).astype(bf16)
-    query_gain_part = jnp.sum(d_query * q_raw * q_scale, axis=0)
-    key_gain_part = jnp.sum(d_key * k_raw * k_scale, axis=0)
-    d_query = d_query * head_gain[0]
-    d_key = d_key * head_gain[1]
 
     def head_gains(value):
         for move in (along(X), along(Y), swap_core):
@@ -1066,51 +1157,73 @@
         return value
 
     def all_norms(value):
-        for move in (along(Z), along(FAR), swap_core, along(X), along(Y)):
+        for move in (along(Z), along(FAR), swap_core):
             (came,) = yield [(value, move)]
             value = value + came
         return value
 
-    head_part = jnp.stack([query_gain_part, key_gain_part]).reshape(2, 1, 2, HEAD)
+    def norms_over(bit, value):
+        (came,) = yield [(value, along(bit))]
+        return value + came
+
+    head_part = head_part.reshape(2, 1, 2, HEAD)
     head_part = jnp.where(core == jnp.arange(2).reshape(1, 2, 1, 1), head_part, 0.0)
+    sums, finish = row_means(sums.reshape(2, 2, LINE, ROWS))
     sums, head_grads, norms = region(
         lambda *given: run(sums_track(given[0]), head_gains(given[1]), all_norms(given[2])),
-        row_sums(d_query * q_raw, d_key * k_raw),
+        sums,
         head_part,
         norms,
     )
     sums, out_came = together(sums, out_came)
-    out_kept, out_came = sum_second(out_split, out_came)
     head_grads = lax.dynamic_index_in_dim(head_grads.reshape(2, SQUARE, HEAD), corner, 1, keepdims=False)
-    norms = lax.dynamic_index_in_dim(norms.reshape(2, BLOCKS, ROWS), shard_index, 1, keepdims=False)
-    means = row_means(sums)
-    d_query = (d_query * q_scale - q_raw * q_scale**3 * means[0]).astype(bf16)
-    d_key = (d_key * k_scale - k_raw * k_scale**3 * means[1]).astype(bf16)
-    d_qkv = jnp.concatenate([d_query, d_key, d_value], axis=1)
+    qkv_shape = jax.ShapeDtypeStruct(raw.shape, bf16)
+    d_qkv = whole_call(norm_grad_kernel, [qkv_shape], [], [d_head, d_value, raw, scales, finish(sums)])
+    d_qkv = d_qkv.reshape(tokens, -1)
     total = across_cores(d_qkv, qkv_w, along_last)
     qkv_split = sum_split(
         from_order, along_first(x_all, d_qkv).astype(bf16).reshape(BLOCKS, ROWS, -1)
     )
-    total, qkv_split = together(total, qkv_split)
-    qkv_came = sum_first(qkv_split)
-
-    def inputs_begun(total, hidden_grad, hidden_other):
+
+    def first_track(split):
+        return (yield [(split[1], along(Y)), (split[3], along(X))])
+
+    def later_track(split, came):
+        kept, (first, second) = sum_later(split, came)
+        came = yield [(first, along(X)), (second, along(Y))]
+        return sum_end(kept, came)
+
+    def inputs_begun(total, split, hidden_grad, hidden_other):
         hidden_grads = spread_columns(core_ref, slot_places, hidden_grad, hidden_other, 2, SQUARE)
-        return alone(scatter_first(total)), hidden_grads
-
-    carried, (gate_grad, up_grad) = region(inputs_begun, total, hidden_grad, hidden_other)
-    total, carried, qkv_came, out_came = together(total, carried, qkv_came, out_came)
-    qkv_kept, qkv_came = sum_second(qkv_split, qkv_came)
-    out_grad = sum_end(out_kept, out_came)[0]
-    out_other = swap_core(out_grad)
-    input_grad = region(
-        lambda total, carried: d_resid + alone(scatter_second(total, *carried)), total, carried
-    )
-    input_grad, qkv_came = together(input_grad, qkv_came)
-    qkv_grad = alone(turn_line(sum_end(qkv_kept, qkv_came)))
-    query_grad, key_grad, value_grad = spread_columns(
-        core_ref, slot_places, qkv_grad, swap_core(qkv_grad), 3, 1
-    )
+        return run(scatter_first(total), first_track(split)), hidden_grads
+
+    (carried, qkv_came), (gate_grad, up_grad) = region(
+        inputs_begun, total, qkv_split, hidden_grad, hidden_other
+    )
+    total, out_came = together(total, out_came)
+    d_inputs, qkv_grad, norms = region(
+        lambda total, carried, split, came, norms: run(
+            scatter_second(total, *carried), later_track(split, came), norms_over(X, norms)
+        ),
+        total,
+        carried,
+        qkv_split,
+        qkv_came,
+        norms,
+    )
+    input_grad = d_resid + d_inputs
+    qkv_grad, out_grad, down_grad = run(
+        turn_line(qkv_grad), later_track(out_split, out_came), later_track(down_split, down_came)
+    )
+    out_grad, down_grad = out_grad[0], down_grad[0]
+    qkv_other, out_other, down_other, norms = run(
+        one(qkv_grad, swap_core),
+        one(out_grad, swap_core),
+        one(down_grad, swap_core),
+        norms_over(Y, norms),
+    )
+    norms = lax.dynamic_index_in_dim(norms.reshape(2, BLOCKS, ROWS), shard_index, 1, keepdims=False)
+    query_grad, key_grad, value_grad = spread_columns(core_ref, slot_places, qkv_grad, qkv_other, 3, 1)
     down_grad = jnp.concatenate(
         [jnp.where(core, down_other, down_grad), jnp.where(core, down_grad, down_other)]
     )

time: 913 us -> 867 us (0.950)
  Pallas kernels: 97.6 us -> 125 us
  waiting for transfers between devices: 378 us -> 353 us
  local copies, waits for them, and re-layouts: 78.2 us -> 56.3 us
  other arithmetic: 66.8 us -> 50.7 us
    pallas_call x36 -> x41, Pallas kernels: 97.6 us -> 125 us  [whole_call(): pl.pallas_call(kernel, out_shape=shapes[0] if single else shapes, in_spec...]
    ppermute x40, waiting for transfers between devices: 228 us -> 203 us  [line_move(): return lambda value: lax.ppermute(value, 'shard', pairs)]
    ppermute x38 -> x42, waiting for transfers between devices: 47.1 us -> 36 us  [swap(): lax.ppermute(value, 'shard', [(source, source ^ bit) for source in range(...]
    cond x31 -> x34, local copies, waits for them, and re-layouts: 18.9 us -> 8.89 us  [the longest x6 12.3 us: region(): return lax.cond(positions[0] >= 0, function, empty, *given)]
    unnamed x155 -> x163, local copies, waits for them, and re-layouts: 33.4 us -> 26 us
    ppermute x38 -> x42, starting transfers between devices: 39.2 us -> 41.9 us  [swap(): lax.ppermute(value, 'shard', [(source, source ^ bit) for source in range(...]
  transfers between devices with their start and end apart: 110 -> 114, of which waited for: 58 -> 53; matrix products, arithmetic and copies ran while one was open for 14% -> 10% of each run, Pallas kernels for 8% -> 10%
where the time goes in v3:
time: 867 us; the launch traced here: 857 us
  waiting for transfers between devices  353 us (41%)
  starting transfers between devices  165 us (19%)
  Pallas kernels  125 us (14%)
  matrix products  92.5 us (11%)
  local copies, waits for them, and re-layouts  56.3 us (6%)
  other arithmetic  50.7 us (6%)
  blocking collectives  10.4 us (1%)
    ppermute x40, waiting for transfers between devices, line_move(): return lambda value: lax.ppermute(value, 'shard', pairs)  203 us
    pallas_call x41, Pallas kernels, whole_call(): pl.pallas_call(kernel, out_shape=shapes[0] if single else shapes, in_spec...  125 us
    ppermute x40, starting transfers between devices, line_move(): return lambda value: lax.ppermute(value, 'shard', pairs)  92.3 us
    all_to_all x3, waiting for transfers between devices, turn_square(): lax.all_to_all(message, 'shard', 0, 0, tiled=True, axis_index_groups=SQUA...  56.4 us
    ppermute x42, starting transfers between devices, swap(): lax.ppermute(value, 'shard', [(source, source ^ bit) for source in range(...  41.9 us
    ppermute x42, waiting for transfers between devices, swap(): lax.ppermute(value, 'shard', [(source, source ^ bit) for source in range(...  36 us
    dot_general x6, matrix products, along_last(): lax.dot_general(left, right, (((1,), (1,)), ((), ())), preferred_element_...  34.6 us
    ppermute x12, waiting for transfers between devices, line_turn(): return lambda value: lax.ppermute(value, 'shard', pairs)  33.8 us
  transfers between devices with their start and end apart: 114, of which 53 were waited for; matrix products, arithmetic and copies ran while one was open for 10% of the time, Pallas kernels for 10%

profile of v3, /device:TPU:0, one launch (start us, length us, event | category | flops | bytes accessed | tf_op | source)
XLA Modules:
  0.0 856.6 jit_solution(12998244591500778447)
XLA Ops:
  63.0 15.8 %collective-permute-done.57.lefts_ref = bf16[128,2048]{1,0:T(8,128)(2,1)S(1)} collective-permute-done((bf16[128,2048]{1,0:T(8,128)(2,1)}, bf16[128,2048]{1,0:T(8,128)(2,1)S(1)}, u32[]{:S(2)}, u32[]{:S(2)}) %collective-permute-start.57) | collective-permute-done | bytes 524320 | tf_op jit(solution)/shard_map/ppermute | solution.py:306
  130.9 65.7 %conditional.12 = (bf16[4,16,128,128]{3,2,1,0:T(8,128)(2,1)}, f32[16,128,1]{2,1,0:T(8,128)}, bf16[1024,256]{1,0:T(8,128)(2,1)}) conditional(s32[]{:T(128)} %bitcast.18, () %tuple.156, (s32[1]{0:T(128)}, s32[1]{0:T(128)}, f32[2,4,128,768]{3,2,1,0:T(8,128)}, f32[2,2,4,128,1]{3,2,1,0,4:T(4,128)}, f32[2,256]{1,0:T(2,128)S(1)}, ...), branch_computations={%region_4.5_spmd, %region_5.6_spmd} | conditional | bytes 29495436 | solution.py:947
  146.4 23.6 %all-to-all-done.message_ref = bf16[4,16,128,128]{3,2,1,0:T(8,128)(2,1)} async-done(((bf16[4,16,128,128]{3,2,1,0:T(8,128)(2,1)}), bf16[4,16,128,128]{3,2,1,0:T(8,128)(2,1)}, u32[]{:S(2)}, u32[]{:S(2)}) %all-to-all-start) | async-done | bytes 2097184 | tf_op jit(solution)/shard_map/cond/branch_1_fun/all_to_all | solution.py:890
  171.3 13.8 %branch_1_fun.18 = (bf16[4,4,128,128]{3,2,1,0:T(8,128)(2,1)S(1)}, f32[16,128,1]{2,1,0:T(8,128)}) custom-call(s32[1]{0:T(128)} %get-tuple-element.172.place_ref, bf16[4,16,128,128]{3,2,1,0:T(8,128)(2,1)} %all-to-all-done.message_ref, s32[16,128,1]{2,1,0:T(8,128)S(1)} %copy-done.10), custom_call_target="tpu_custom_call" | custom-call | bytes 4210688 | tf_op jit(solution)/shard_map/cond/branch_1_fun/pallas_call | solution.py:587
  204.8 64.2 %conditional.13 = (f32[128,2048]{1,0:T(8,128)S(1)}, bf16[1024,2048]{1,0:T(8,128)(2,1)}) conditional(s32[]{:T(128)} %bitcast.18, () %tuple.155, (bf16[1024,256]{1,0:T(8,128)(2,1)}, bf16[256,2048]{1,0:T(8,128)(2,1)S(1)}, s32[4]{0:T(128)S(1)}, bf16[1,256,2048]{2,1,0:T(8,128)(2,1)}, bf16[1,256,1024]{2,1,0:T(8,128)(2,1)}, ...), branch_computations={%region_6.7_spmd, %region_7.8_spmd} | conditional | flops 1083179008 | bytes 66060884 | solution.py:947
  233.4 10.5 %collective-permute-done.26 = bf16[128,2048]{1,0:T(8,128)(2,1)} collective-permute-done((bf16[128,2048]{1,0:T(8,128)(2,1)}, bf16[128,2048]{1,0:T(8,128)(2,1)}, u32[]{:S(2)}, u32[]{:S(2)}) %collective-permute-start.26) | collective-permute-done | bytes 524320 | tf_op jit(solution)/shard_map/cond/branch_1_fun/ppermute | solution.py:306
  275.7 49.5 %conditional.14 = (f32[128,1]{0,1:T(1,128)S(1)}, f32[128,2048]{1,0:T(8,128)}, bf16[1024,2048]{1,0:T(8,128)(2,1)}) conditional(s32[]{:T(128)} %bitcast.18, () %tuple.154, (f32[128,2048]{1,0:T(8,128)S(1)}, bf16[128,2048]{1,0:T(8,128)(2,1)S(1)}, f32[4,2048]{1,0:T(4,128)S(1)}) %tuple.310), branch_computations={%region_8.9_spmd, %region_9.11_spmd} | conditional | flops 2097298 | bytes 39349180 | solution.py:947
  295.5 12.8 %collective-permute-done.16.lefts_ref = bf16[128,2048]{1,0:T(8,128)(2,1)S(1)} collective-permute-done((bf16[128,2048]{1,0:T(8,128)(2,1)S(1)}, bf16[128,2048]{1,0:T(8,128)(2,1)S(1)}, u32[]{:S(2)}, u32[]{:S(2)}) %collective-permute-start.16) | collective-permute-done | bytes 524320 | tf_op jit(solution)/shard_map/cond/branch_1_fun/ppermute | solution.py:306
  331.9 12.5 %fusion.60 = f32[1024,2048]{1,0:T(8,128)S(1)} fusion(bf16[1024,2048]{1,0:T(8,128)(2,1)} %get-tuple-element.621, bf16[2048,2048]{1,0:T(8,128)(2,1)} %bitcast.195), kind=kOutput, calls=%fused_computation.205 | convolution fusion | flops 8589934592 | bytes 20971520 | tf_op jit(solution)/shard_map/dot_general | solution.py:955
  379.1 10.7 %collective-permute-done.77 = bf16[128,2048]{1,0:T(8,128)(2,1)} collective-permute-done((bf16[128,2048]{1,0:T(8,128)(2,1)}, bf16[128,2048]{1,0:T(8,128)(2,1)}, u32[]{:S(2)}, u32[]{:S(2)}) %collective-permute-start.77) | collective-permute-done | bytes 524320 | tf_op jit(solution)/shard_map/ppermute | solution.py:306
  435.6 13.8 %collective-permute-done.83.lefts_ref = bf16[128,2048]{1,0:T(8,128)(2,1)S(1)} collective-permute-done((bf16[128,2048]{1,0:T(8,128)(2,1)S(1)}, bf16[128,2048]{1,0:T(8,128)(2,1)S(1)}, u32[]{:S(2)}, u32[]{:S(2)}) %collective-permute-start.83) | collective-permute-done | bytes 524320 | tf_op jit(solution)/shard_map/ppermute | solution.py:306
  466.3 10.9 %multiply_convert_fusion = (bf16[1024,1024]{1,0:T(8,128)(2,1)S(1)}, bf16[1024,1024]{1,0:T(8,128)(2,1)}) fusion(f32[1024,2048]{1,0:T(8,128)S(1)} %bitcast.201, bf16[1024,2048]{1,0:T(8,128)(2,1)} %shard_map.250, bf16[1024,2048]{1,0:T(8,128)(2,1)} %get-tuple-element.624), kind=kOutput, calls=%fused_computation.47 | convolution fusion | flops 4308598784 | bytes 20971520 | tf_op jit(solution)/shard_map/dot_general | solution.py:44
  499.6 32.8 %conditional.15 = (bf16[128,2048]{1,0:T(8,128)(2,1)}, bf16[128,2048]{1,0:T(8,128)(2,1)}, bf16[128,2048]{1,0:T(8,128)(2,1)}, bf16[2,4,128,1024]{3,2,1,0:T(8,128)(...) conditional(s32[]{:T(128)} %bitcast.18, () %tuple.183, ...), branch_computations={%region_13.14_spmd, %region_14.15_spmd} | conditional | flops 12891455488 | bytes 86507960 | solution.py:947
  507.8 12.0 %convolution_convert_fusion.1 = bf16[2048,2048]{1,0:T(8,128)(2,1)S(1)} fusion(bf16[1024,2048]{1,0:T(8,128)(2,1)} %get-tuple-element.220, bf16[1024,2048]{1,0:T(8,128)(2,1)} %get-tuple-element.221), kind=kOutput, calls=%fused_computation.14 | convolution fusion | flops 8594128896 | bytes 16777216 | tf_op jit(solution)/shard_map/cond/branch_1_fun/dot_general | solution.py:50
  537.2 40.2 %conditional.16 = (f32[128,2048]{1,0:T(8,128)}, bf16[128,2048]{1,0:T(8,128)(2,1)}, bf16[128,2048]{1,0:T(8,128)(2,1)}, bf16[128,2048]{1,0:T(8,128)(2,1)}, f32[2,2048]{1,0:T(2,128)S(1)}) conditional(s32[]{:T(128)} %bitcast.18, () %tuple.178, (bf16[512,2048]{1,0:T(8,128)(2,1)}, bf16[128,2048]{1,0:T(8,128)(2,1)}, bf16[128,2048]{1,0:T(8,128)(2,1)}, ...), branch_computations={%region_15.16_spmd, %region_16.20_spmd} | conditional | flops 9175315 | bytes 34165720 | solution.py:947
  588.0 38.3 %conditional.17 = (bf16[1024,2048]{1,0:T(8,128)(2,1)}, bf16[1024,256]{1,0:T(8,128)(2,1)S(1)}) conditional(s32[]{:T(128)} %bitcast.18, () %tuple.188, (bf16[128,2048]{1,0:T(8,128)(2,1)}, bf16[128,2048]{1,0:T(8,128)(2,1)}, bf16[128,2048]{1,0:T(8,128)(2,1)}, bf16[256,2048]{1,0:T(8,128)(2,1)}) %tuple.304), branch_computations={%region_20.21_spmd, %region_21.22_spmd} | conditional | flops 1074266112 | bytes 40894848 | solution.py:947
  592.4 14.2 %collective-permute-done.33.lefts_ref = bf16[128,2048]{1,0:T(8,128)(2,1)S(1)} collective-permute-done((bf16[128,2048]{1,0:T(8,128)(2,1)}, bf16[128,2048]{1,0:T(8,128)(2,1)S(1)}, u32[]{:S(2)}, u32[]{:S(2)}) %collective-permute-start.33) | collective-permute-done | bytes 524320 | tf_op jit(solution)/shard_map/cond/branch_1_fun/ppermute | solution.py:306
  636.7 76.1 %conditional.18 = (f32[2,2,4,128,256]{4,3,2,1,0:T(8,128)}, bf16[2,4,128,256]{3,2,1,0:T(8,128)(2,1)}, f32[2,2,4,128,1]{4,3,2,1,0:T(8,128)}, f32[2,256]{1,0:T(2,12...) conditional(s32[]{:T(128)} %bitcast.18, () %tuple.187, ...), branch_computations={%region_22.23_spmd, %region_23.24_spmd} | conditional | flops 1074790400 | bytes 48320700 | solution.py:947
  642.1 15.7 %all-to-all-done.2.do_ref = bf16[4,4,128,128]{3,2,1,0:T(8,128)(2,1)} async-done(((bf16[4,4,128,128]{3,2,1,0:T(8,128)(2,1)}), bf16[4,4,128,128]{3,2,1,0:T(8,128)(2,1)}, u32[]{:S(2)}, u32[]{:S(2)}) %all-to-all-start.2) | async-done | bytes 524320 | tf_op jit(solution)/shard_map/cond/branch_1_fun/all_to_all | solution.py:890
  657.8 15.8 %branch_1_fun.28 = bf16[4,16,128,128]{3,2,1,0:T(8,128)(2,1)S(1)} custom-call(s32[1]{0:T(128)} %get-tuple-element.262.place_ref, bf16[4,16,128,128]{3,2,1,0:T(8,128)(2,1)} %get-tuple-element.263.message_ref, s32[16,128,1]{2,1,0:T(8,128)S(1)} %copy.74.pos_ref, f32[16,128,1]{2,1,0:T(8,128)} %get-tuple-element.265.lse_ref, ...), custom_call_target="tpu_custom_call" | custom-call | bytes 5275648 | tf_op jit(solution)/shard_map/cond/branch_1_fun/pallas_call | solution.py:587
  687.3 17.1 %all-to-all-done.3.came_ref = bf16[4,16,128,128]{3,2,1,0:T(8,128)(2,1)} async-done(((bf16[4,16,128,128]{3,2,1,0:T(8,128)(2,1)}), bf16[4,16,128,128]{3,2,1,0:T(8,128)(2,1)}, u32[]{:S(2)}, u32[]{:S(2)}) %all-to-all-start.3) | async-done | bytes 2097184 | tf_op jit(solution)/shard_map/cond/branch_1_fun/all_to_all | solution.py:890
  717.6 17.1 %conditional.19 = (f32[4,2,2,128]{3,2,1,0:T(2,128)S(1)}, f32[2,2048]{1,0:T(2,128)S(1)}, f32[2,4,128]{2,1,0:T(4,128)S(1)}) conditional(s32[]{:T(128)} %bitcast.18, () %tuple.195, (s32[]{:T(128)}, s32[1,2,1,1]{1,3,2,0:T(1,128)S(1)}, f32[2,256]{1,0:T(2,128)S(1)}, f32[4,2,2,128]{3,2,1,0:T(2,128)S(1)}, f32[2,2048]{1,0:T(2,128)S(1)}) %tuple.196), branch_computations={%region_24.25_spmd, %region_25.26_spmd} | conditional | flops 25602 | bytes 629140 | solution.py:947
  758.7 25.9 %conditional.20 = (bf16[128,2048]{1,0:T(8,128)(2,1)}, bf16[128,2048]{1,0:T(8,128)(2,1)}, bf16[128,2048]{1,0:T(8,128)(2,1)}, bf16[2,4,128,384]{3,2,1,0:T(8,128)(2...) conditional(s32[]{:T(128)} %bitcast.18, () %tuple.199, ...), branch_computations={%region_26.27_spmd, %region_27.28_spmd} | conditional | flops 262162 | bytes 23593396 | solution.py:947
  784.7 29.4 %conditional.21 = (f32[128,2048]{1,0:T(8,128)}, bf16[4,128,768]{2,1,0:T(8,128)(2,1)}, f32[2,2048]{1,0:T(2,128)S(1)}) conditional(s32[]{:T(128)} %bitcast.18, () %tuple.186, (bf16[512,2048]{1,0:T(8,128)(2,1)S(1)}, bf16[128,2048]{1,0:T(8,128)(2,1)}, bf16[128,2048]{1,0:T(8,128)(2,1)}, bf16[128,2048]{1,0:T(8,128)(2,1)}, ...), branch_computations={%region_28.29_spmd, %region_29.30_spmd} | conditional | flops 4984851 | bytes 39961040 | solution.py:947
  (586 shorter events, 662.3 us)
Async XLA Ops:
  7.8 29.8 %collective-permute-start.50 = (bf16[1,256,1024]{2,1,0:T(8,128)(2,1)S(1)}, bf16[1,256,1024]{2,1,0:T(8,128)(2,1)S(1)}, u32[]{:S(2)}, u32[]{:S(2)}) collective-permute-start(bf16[1,256,1024]{2,1,0:T(8,128)(2,1)S(1)} %copy-done.83), channel_id=1, source_target_pairs={{0,1},{1,0},{2,3},{3,2},{4,5},{5,4},{6,7},{7,6},{8,9},{9,8},{10,11... | collective-permute-start | bytes 1572872 | tf_op jit(solution)/shard_map/ppermute | solution.py:285
  102.0 94.6 %collective-permute-start.68 = (bf16[2,1,256,1024]{3,2,1,0:T(8,128)(2,1)}, bf16[2,1,256,1024]{3,2,1,0:T(8,128)(2,1)}, u32[]{:S(2)}, u32[]{:S(2)}) collective-permute-start(bf16[2,1,256,1024]{3,2,1,0:T(8,128)(2,1)} %get-tuple-element.600), channel_id=1, source_target_pairs={{0,2},{1,3},{2,0},{3,1},{4,6},{5,7},{6,4},{7,5},{8,10},{9,11},{10,... | collective-permute-start | bytes 3145736 | tf_op jit(solution)/shard_map/ppermute | solution.py:285
  103.5 93.2 %collective-permute-start.69 = (bf16[2,1,256,1024]{3,2,1,0:T(8,128)(2,1)}, bf16[2,1,256,1024]{3,2,1,0:T(8,128)(2,1)}, u32[]{:S(2)}, u32[]{:S(2)}) collective-permute-start(bf16[2,1,256,1024]{3,2,1,0:T(8,128)(2,1)} %get-tuple-element.601), channel_id=1, source_target_pairs={{0,1},{1,0},{2,3},{3,2},{4,5},{5,4},{6,7},{7,6},{8,9},{9,8},{10,11... | collective-permute-start | bytes 3145736 | tf_op jit(solution)/shard_map/ppermute | solution.py:285
  123.4 73.3 %collective-permute-start.65 = (bf16[128,2048]{1,0:T(8,128)(2,1)}, bf16[128,2048]{1,0:T(8,128)(2,1)}, u32[]{:S(2)}, u32[]{:S(2)}) collective-permute-start(bf16[128,2048]{1,0:T(8,128)(2,1)} %get-tuple-element.889), channel_id=1, source_target_pairs={{0,4},{1,5},{2,6},{3,7},{4,8},{5,9},{6,10},{7,11},{8,12},{9,13},{1... | collective-permute-start | bytes 1572872 | tf_op jit(solution)/shard_map/ppermute | solution.py:314
  123.4 73.3 %collective-permute-start.66 = (bf16[128,2048]{1,0:T(8,128)(2,1)}, bf16[128,2048]{1,0:T(8,128)(2,1)}, u32[]{:S(2)}, u32[]{:S(2)}) collective-permute-start(bf16[128,2048]{1,0:T(8,128)(2,1)} %get-tuple-element.888), channel_id=1, source_target_pairs={{0,8},{1,9},{2,10},{3,11},{4,12},{5,13},{6,14},{7,15},{8,0},{9,1},... | collective-permute-start | bytes 1572872 | tf_op jit(solution)/shard_map/ppermute | solution.py:314
  123.4 73.3 %collective-permute-start.67 = (bf16[128,2048]{1,0:T(8,128)(2,1)}, bf16[128,2048]{1,0:T(8,128)(2,1)}, u32[]{:S(2)}, u32[]{:S(2)}) collective-permute-start(bf16[128,2048]{1,0:T(8,128)(2,1)} %get-tuple-element.887), channel_id=1, source_target_pairs={{0,12},{1,13},{2,14},{3,15},{4,0},{5,1},{6,2},{7,3},{8,4},{9,5},{1... | collective-permute-start | bytes 1572872 | tf_op jit(solution)/shard_map/ppermute | solution.py:314
  140.6 29.4 %all-to-all-start = ((bf16[4,16,128,128]{3,2,1,0:T(8,128)(2,1)}), bf16[4,16,128,128]{3,2,1,0:T(8,128)(2,1)}, u32[]{:S(2)}, u32[]{:S(2)}) async-start(bf16[4,16,128,128]{3,2,1,0:T(8,128)(2,1)} %copy-done.4), calls=%async_computation | async-start | bytes 4194304 | tf_op jit(solution)/shard_map/cond/branch_1_fun/all_to_all | solution.py:890
  200.9 68.1 %collective-permute-start.70 = (bf16[4,128,1024]{2,1,0:T(8,128)(2,1)}, bf16[4,128,1024]{2,1,0:T(8,128)(2,1)}, u32[]{:S(2)}, u32[]{:S(2)}) collective-permute-start(bf16[4,128,1024]{2,1,0:T(8,128)(2,1)} %get-tuple-element.611), channel_id=1, source_target_pairs={{0,1},{1,0},{2,3},{3,2},{4,5},{5,4},{6,7},{7,6},{8,9},{9,8},{10,11... | collective-permute-start | bytes 3145736 | tf_op jit(solution)/shard_map/ppermute | solution.py:285
  201.8 67.2 %collective-permute-start.71 = (bf16[4,128,1024]{2,1,0:T(8,128)(2,1)}, bf16[4,128,1024]{2,1,0:T(8,128)(2,1)}, u32[]{:S(2)}, u32[]{:S(2)}) collective-permute-start(bf16[4,128,1024]{2,1,0:T(8,128)(2,1)} %get-tuple-element.612), channel_id=1, source_target_pairs={{0,2},{1,3},{2,0},{3,1},{4,6},{5,7},{6,4},{7,5},{8,10},{9,11},{10,... | collective-permute-start | bytes 3145736 | tf_op jit(solution)/shard_map/ppermute | solution.py:285
  273.1 52.1 %collective-permute-start.72 = (bf16[2,4,128,1024]{3,2,1,0:T(8,128)(2,1)}, bf16[2,4,128,1024]{3,2,1,0:T(8,128)(2,1)}, u32[]{:S(2)}, u32[]{:S(2)}) collective-permute-start(bf16[2,4,128,1024]{3,2,1,0:T(8,128)(2,1)} %get-tuple-element.619), channel_id=1, source_target_pairs={{0,2},{1,3},{2,0},{3,1},{4,6},{5,7},{6,4},{7,5},{8,10},{9,11},{10,... | collective-permute-start | bytes 6291464 | tf_op jit(solution)/shard_map/ppermute | solution.py:285
  274.6 50.6 %collective-permute-start.73 = (bf16[2,4,128,1024]{3,2,1,0:T(8,128)(2,1)}, bf16[2,4,128,1024]{3,2,1,0:T(8,128)(2,1)}, u32[]{:S(2)}, u32[]{:S(2)}) collective-permute-start(bf16[2,4,128,1024]{3,2,1,0:T(8,128)(2,1)} %get-tuple-element.620), channel_id=1, source_target_pairs={{0,1},{1,0},{2,3},{3,2},{4,5},{5,4},{6,7},{7,6},{8,9},{9,8},{10,11... | collective-permute-start | bytes 6291464 | tf_op jit(solution)/shard_map/ppermute | solution.py:285
  499.7 32.5 %collective-permute-start.29 = (bf16[128,2048]{1,0:T(8,128)(2,1)S(1)}, bf16[128,2048]{1,0:T(8,128)(2,1)}, u32[]{:S(2)}, u32[]{:S(2)}) collective-permute-start(bf16[128,2048]{1,0:T(8,128)(2,1)S(1)} %get-tuple-element.214), channel_id=1, source_target_pairs={{0,4},{1,5},{2,6},{3,7},{4,8},{5,9},{6,10},{7,11},{16,20},{17,21},... | collective-permute-start | bytes 1572872 | tf_op jit(solution)/shard_map/cond/branch_1_fun/ppermute | solution.py:306
  501.8 30.4 %collective-permute-start.30 = (bf16[128,2048]{1,0:T(8,128)(2,1)S(1)}, bf16[128,2048]{1,0:T(8,128)(2,1)}, u32[]{:S(2)}, u32[]{:S(2)}) collective-permute-start(bf16[128,2048]{1,0:T(8,128)(2,1)S(1)} %get-tuple-element.214), channel_id=1, source_target_pairs={{12,8},{13,9},{14,10},{15,11},{8,4},{9,5},{10,6},{11,7},{28,24},{2... | collective-permute-start | bytes 1572872 | tf_op jit(solution)/shard_map/cond/branch_1_fun/ppermute | solution.py:306
  503.3 28.9 %collective-permute-start.31 = (bf16[128,2048]{1,0:T(8,128)(2,1)S(1)}, bf16[128,2048]{1,0:T(8,128)(2,1)}, u32[]{:S(2)}, u32[]{:S(2)}) collective-permute-start(bf16[128,2048]{1,0:T(8,128)(2,1)S(1)} %get-tuple-element.215), channel_id=1, source_target_pairs={{0,8},{1,9},{2,10},{3,11},{12,4},{13,5},{14,6},{15,7},{16,24},{17,... | collective-permute-start | bytes 1572872 | tf_op jit(solution)/shard_map/cond/branch_1_fun/ppermute | solution.py:306
  532.4 47.3 %collective-permute-start.87 = (bf16[2,4,128,1024]{3,2,1,0:T(8,128)(2,1)}, bf16[2,4,128,1024]{3,2,1,0:T(8,128)(2,1)S(1)}, u32[]{:S(2)}, u32[]{:S(2)}) collective-permute-start(bf16[2,4,128,1024]{3,2,1,0:T(8,128)(2,1)} %get-tuple-element.653), channel_id=1, source_target_pairs={{0,2},{1,3},{2,0},{3,1},{4,6},{5,7},{6,4},{7,5},{8,10},{9,11},{10,... | collective-permute-start | bytes 6291464 | tf_op jit(solution)/shard_map/ppermute | solution.py:285
  533.4 47.0 %collective-permute-start.88 = (bf16[2,4,128,1024]{3,2,1,0:T(8,128)(2,1)}, bf16[2,4,128,1024]{3,2,1,0:T(8,128)(2,1)}, u32[]{:S(2)}, u32[]{:S(2)}) collective-permute-start(bf16[2,4,128,1024]{3,2,1,0:T(8,128)(2,1)} %get-tuple-element.654), channel_id=1, source_target_pairs={{0,1},{1,0},{2,3},{3,2},{4,5},{5,4},{6,7},{7,6},{8,9},{9,8},{10,11... | collective-permute-start | bytes 6291464 | tf_op jit(solution)/shard_map/ppermute | solution.py:285
  586.0 40.3 %collective-permute-start.89 = (bf16[4,128,1024]{2,1,0:T(8,128)(2,1)}, bf16[4,128,1024]{2,1,0:T(8,128)(2,1)}, u32[]{:S(2)}, u32[]{:S(2)}) collective-permute-start(bf16[4,128,1024]{2,1,0:T(8,128)(2,1)} %get-tuple-element.663), channel_id=1, source_target_pairs={{0,1},{1,0},{2,3},{3,2},{4,5},{5,4},{6,7},{7,6},{8,9},{9,8},{10,11... | collective-permute-start | bytes 3145736 | tf_op jit(solution)/shard_map/ppermute | solution.py:285
  586.5 39.8 %collective-permute-start.90 = (bf16[4,128,1024]{2,1,0:T(8,128)(2,1)}, bf16[4,128,1024]{2,1,0:T(8,128)(2,1)}, u32[]{:S(2)}, u32[]{:S(2)}) collective-permute-start(bf16[4,128,1024]{2,1,0:T(8,128)(2,1)} %get-tuple-element.664), channel_id=1, source_target_pairs={{0,2},{1,3},{2,0},{3,1},{4,6},{5,7},{6,4},{7,5},{8,10},{9,11},{10,... | collective-permute-start | bytes 3145736 | tf_op jit(solution)/shard_map/ppermute | solution.py:285
  626.3 89.7 %collective-permute-start.94 = (bf16[2,1,256,1024]{3,2,1,0:T(8,128)(2,1)}, bf16[2,1,256,1024]{3,2,1,0:T(8,128)(2,1)}, u32[]{:S(2)}, u32[]{:S(2)}) collective-permute-start(bf16[2,1,256,1024]{3,2,1,0:T(8,128)(2,1)} %get-tuple-element.679), channel_id=1, source_target_pairs={{0,2},{1,3},{2,0},{3,1},{4,6},{5,7},{6,4},{7,5},{8,10},{9,11},{10,... | collective-permute-start | bytes 3145736 | tf_op jit(solution)/shard_map/ppermute | solution.py:285
  627.0 89.1 %collective-permute-start.95 = (bf16[2,1,256,1024]{3,2,1,0:T(8,128)(2,1)}, bf16[2,1,256,1024]{3,2,1,0:T(8,128)(2,1)}, u32[]{:S(2)}, u32[]{:S(2)}) collective-permute-start(bf16[2,1,256,1024]{3,2,1,0:T(8,128)(2,1)} %get-tuple-element.680), channel_id=1, source_target_pairs={{0,1},{1,0},{2,3},{3,2},{4,5},{5,4},{6,7},{7,6},{8,9},{9,8},{10,11... | collective-permute-start | bytes 3145736 | tf_op jit(solution)/shard_map/ppermute | solution.py:285
  632.9 80.0 %collective-permute-start.91 = (bf16[128,2048]{1,0:T(8,128)(2,1)}, bf16[128,2048]{1,0:T(8,128)(2,1)}, u32[]{:S(2)}, u32[]{:S(2)}) collective-permute-start(bf16[128,2048]{1,0:T(8,128)(2,1)} %get-tuple-element.884), channel_id=1, source_target_pairs={{0,4},{1,5},{2,6},{3,7},{4,8},{5,9},{6,10},{7,11},{8,12},{9,13},{1... | collective-permute-start | bytes 1572872 | tf_op jit(solution)/shard_map/ppermute | solution.py:314
  632.9 81.2 %collective-permute-start.92 = (bf16[128,2048]{1,0:T(8,128)(2,1)}, bf16[128,2048]{1,0:T(8,128)(2,1)}, u32[]{:S(2)}, u32[]{:S(2)}) collective-permute-start(bf16[128,2048]{1,0:T(8,128)(2,1)} %get-tuple-element.883), channel_id=1, source_target_pairs={{0,8},{1,9},{2,10},{3,11},{4,12},{5,13},{6,14},{7,15},{8,0},{9,1},... | collective-permute-start | bytes 1572872 | tf_op jit(solution)/shard_map/ppermute | solution.py:314
  633.5 82.5 %collective-permute-start.93 = (bf16[128,2048]{1,0:T(8,128)(2,1)}, bf16[128,2048]{1,0:T(8,128)(2,1)}, u32[]{:S(2)}, u32[]{:S(2)}) collective-permute-start(bf16[128,2048]{1,0:T(8,128)(2,1)} %get-tuple-element.882), channel_id=1, source_target_pairs={{0,12},{1,13},{2,14},{3,15},{4,0},{5,1},{6,2},{7,3},{8,4},{9,5},{1... | collective-permute-start | bytes 1572872 | tf_op jit(solution)/shard_map/ppermute | solution.py:314
  674.9 29.5 %all-to-all-start.3 = ((bf16[4,16,128,128]{3,2,1,0:T(8,128)(2,1)}), bf16[4,16,128,128]{3,2,1,0:T(8,128)(2,1)}, u32[]{:S(2)}, u32[]{:S(2)}) async-start(bf16[4,16,128,128]{3,2,1,0:T(8,128)(2,1)} %copy-done.5), calls=%async_computation.3 | async-start | bytes 4194304 | tf_op jit(solution)/shard_map/cond/branch_1_fun/all_to_all | solution.py:890
  (188 other events, 1961.6 us)

commit v4 on v3

--- a/solution.py
+++ b/solution.py
@@ -5,6 +5,7 @@
 import jax.numpy as jnp
 from jax import lax
 from jax.experimental import pallas as pl
+from jax.experimental.layout import Layout, with_layout_constraint
 from jax.experimental.pallas import tpu as pltpu
 from jax.sharding import PartitionSpec as P
 
@@ -275,9 +276,11 @@
 X, Y, Z, FAR = 1, 2, 4, 8
 ROWS = 128
 BLOCKS = 16
-WINDOW = 1152
+QUERIES = 2 * ROWS
+WINDOW = DOC_LEN + QUERIES
 SHARE = 256
 SCALING = 1.0 / math.sqrt(HEAD)
+LINES = [[SQUARE * z + r for z in range(LINE)] for r in range(SQUARE)]
 SQUARES = [[SQUARE * z + r for r in range(SQUARE)] for z in range(LINE)]
 
 
@@ -309,7 +312,7 @@
 RIGHT, LEFT = ((0, 1), (1, 2), (2, 3)), ((3, 2), (2, 1), (1, 0))
 
 
-def line_turn(distance):
+def line_step(distance):
     pairs = [(s, (s + SQUARE * distance) % BLOCKS) for s in range(BLOCKS)]
     return lambda value: lax.ppermute(value, "shard", pairs)
 
@@ -401,9 +404,13 @@
     out_ref[rows:, :] = other_ref[...]
 
 
+def join(own, other):
+    shape = jax.ShapeDtypeStruct((2 * own.shape[0], own.shape[1]), own.dtype)
+    return whole_call(join_kernel, [shape], [], [own, other])
+
+
 def both_cores(own):
-    shape = jax.ShapeDtypeStruct((2 * own.shape[0], own.shape[1]), own.dtype)
-    return whole_call(join_kernel, [shape], [], [own, swap_core(own)])
+    return join(own, swap_core(own))
 
 
 def scatter_first(total):
@@ -442,13 +449,7 @@
 
 
 def turn_line(block):
-    place = line_place()
-    came = yield [
-        (lax.dynamic_index_in_dim(block, (place + k) % LINE, 0, keepdims=False), line_turn(k))
-        for k in range(1, LINE)
-    ]
-    own = lax.dynamic_index_in_dim(block, place, 0, keepdims=False)
-    return jnp.stack([own, *came])
+    return lax.all_to_all(block, "shard", 0, 0, tiled=True, axis_index_groups=LINES)
 
 
 def to_slots(value):
@@ -514,24 +515,28 @@
     return whole_call(square_kernel, [shape], [index], [value, *came, *later])
 
 
-def split_kernel(index_ref, grad_ref, kept_first, sent_first, kept_second, sent_second):
-    half, count = grad_ref.shape[-1] // 2, kept_first.shape[1]
+def split_kernel(index_ref, *refs):
+    *grad_refs, kept_first, sent_first, kept_second, sent_second = refs
+    half, count = kept_first.shape[-1], kept_first.shape[1]
     firsts = ((kept_first, 0), (kept_first, 1), (sent_first, 0), (sent_first, 1))
     seconds = ((kept_second, 0), (sent_second, 0), (kept_second, 1), (sent_second, 1))
     for corner in range(SQUARE):
         for number in range(count):
-            block = grad_ref[index_ref[corner * count + number]]
-            for (target, place), lanes in (
-                (firsts[corner], slice(0, half)),
-                (seconds[corner], slice(half, 2 * half)),
-            ):
-                target[place, number] = block[:, lanes]
-
-
-def sum_split(index, grad):
-    blocks, rows, width = grad.shape
-    shape = jax.ShapeDtypeStruct((2, blocks // SQUARE, rows, width // 2), grad.dtype)
-    return whole_call(split_kernel, [shape] * 4, [index], [grad])
+            row = 0
+            for grad_ref in grad_refs:
+                block = grad_ref[index_ref[corner * count + number]]
+                rows = slice(row, row + block.shape[0])
+                row += block.shape[0]
+                (target, place), (other, other_place) = firsts[corner], seconds[corner]
+                target[place, number, rows, :] = block[:, :half]
+                other[other_place, number, rows, :] = block[:, half:]
+
+
+def sum_split(index, *grads):
+    rows = sum(grad.shape[1] for grad in grads)
+    shape = (2, grads[0].shape[0] // SQUARE, rows, grads[0].shape[2] // 2)
+    shape = jax.ShapeDtypeStruct(shape, grads[0].dtype)
+    return whole_call(split_kernel, [shape] * 4, [index], list(grads))
 
 
 def sum_first(split):
@@ -648,6 +653,30 @@
     shape = jax.ShapeDtypeStruct((mine.shape[1], 8 * mine.shape[2] // count), jnp.float32)
     kernel = functools.partial(spread_scalars_kernel, parts)
     return whole_call(kernel, [shape] * count, [core_ref, place_ref], [mine, came])
+
+
+def gated_grad_kernel(grad_ref, both_ref, out_ref):
+    width = grad_ref.shape[1]
+    gate, up, grad = both_ref[:, :width], both_ref[:, width:], grad_ref[...]
+    sigma = 1.0 / (1.0 + jnp.exp(-gate))
+    out_ref[:, :width] = (grad * up * sigma * (1.0 + gate * (1.0 - sigma))).astype(jnp.bfloat16)
+    out_ref[:, width:] = (grad * gate * sigma).astype(jnp.bfloat16)
+
+
+def gated_grad(grad, both):
+    rows, width = grad.shape
+    narrow, wide = (pl.BlockSpec((ROWS, w), lambda i: (i, 0)) for w in (width, 2 * width))
+    return pl.pallas_call(
+        gated_grad_kernel,
+        out_shape=jax.ShapeDtypeStruct(both.shape, jnp.bfloat16),
+        grid=(rows // ROWS,),
+        in_specs=[narrow, wide],
+        out_specs=wide,
+        compiler_params=pltpu.CompilerParams(vmem_limit_bytes=32 * 2**20),
+        cost_estimate=pl.CostEstimate(
+            flops=20 * grad.size, bytes_accessed=16 * grad.size, transcendentals=grad.size
+        ),
+    )(grad, both)
 
 
 def head_lanes(head):
@@ -776,9 +805,9 @@
 
 
 def visible_of(place):
-    row = lax.broadcasted_iota(jnp.int32, (ROWS, WINDOW), 0)
-    column = lax.broadcasted_iota(jnp.int32, (ROWS, WINDOW), 1)
-    distance = row - column + (WINDOW - ROWS)
+    row = lax.broadcasted_iota(jnp.int32, (QUERIES, WINDOW), 0)
+    column = lax.broadcasted_iota(jnp.int32, (QUERIES, WINDOW), 1)
+    distance = row - column + DOC_LEN
     return (distance >= 0) & (distance <= place)
 
 
@@ -814,21 +843,23 @@
     fill(place, message_ref, keys, values)
 
     def step(number, carry):
-        source, slot = number // LINE, number % LINE
-        block, start = stream_row(place, source, slot)
+        sources, slot = pl.ds(2 * (number // LINE), 2), number % LINE
+        block, start = stream_row(place, 2 * (number // LINE), slot)
         rows = pl.ds(start, WINDOW)
-        scores = dot_last(message_ref[source, slot], keys[rows, :]) * SCALING
-        masked = jnp.where(visible_of(pos_ref[block]), scores, -jnp.inf)
+        query = message_ref[sources, slot].reshape(QUERIES, HEAD)
+        scores = dot_last(query, keys[rows, :]) * SCALING
+        seen = pos_ref[pl.ds(block, 2)].reshape(QUERIES, 1)
+        masked = jnp.where(visible_of(seen), scores, -jnp.inf)
         top = jnp.max(masked, axis=-1, keepdims=True)
         expo = jnp.exp(masked - top)
         total = jnp.sum(expo, axis=-1, keepdims=True)
         probs = (expo / total).astype(jnp.bfloat16)
         mixed = jnp.dot(probs, values[rows, :], preferred_element_type=jnp.float32)
-        o_ref[source, slot] = mixed.astype(jnp.bfloat16)
-        lse_ref[number] = top + jnp.log(total)
+        o_ref[sources, slot] = mixed.astype(jnp.bfloat16).reshape(2, ROWS, HEAD)
+        lse_ref[pl.ds(2 * number, 2)] = (top + jnp.log(total)).reshape(2, ROWS, 1)
         return carry
 
-    lax.fori_loop(0, BLOCKS, step, 0)
+    lax.fori_loop(0, BLOCKS // 2, step, 0)
 
 
 def attend_back_kernel(
@@ -840,23 +871,26 @@
     d_values[...] = jnp.zeros_like(d_values)
 
     def step(number, carry):
-        source, slot = number // LINE, number % LINE
-        block, start = stream_row(place, source, slot)
+        sources, slot = pl.ds(2 * (number // LINE), 2), number % LINE
+        block, start = stream_row(place, 2 * (number // LINE), slot)
         rows = pl.ds(start, WINDOW)
-        query, grad = message_ref[source, slot], do_ref[source, slot]
+        query = message_ref[sources, slot].reshape(QUERIES, HEAD)
+        grad = do_ref[sources, slot].reshape(QUERIES, HEAD)
         key, value = keys[rows, :], values[rows, :]
         scores = dot_last(query, key) * SCALING
-        probs = jnp.where(visible_of(pos_ref[block]), jnp.exp(scores - lse_ref[number]), 0.0)
+        seen = pos_ref[pl.ds(block, 2)].reshape(QUERIES, 1)
+        lse = lse_ref[pl.ds(2 * number, 2)].reshape(QUERIES, 1)
+        probs = jnp.where(visible_of(seen), jnp.exp(scores - lse), 0.0)
         d_probs = dot_last(grad, value)
         inner = jnp.sum(probs * d_probs, axis=-1, keepdims=True)
         d_scores = (probs * (d_probs - inner) * SCALING).astype(jnp.bfloat16)
         d_query = jnp.dot(d_scores, key, preferred_element_type=jnp.float32)
-        out_ref[source, slot] = d_query.astype(jnp.bfloat16)
+        out_ref[sources, slot] = d_query.astype(jnp.bfloat16).reshape(2, ROWS, HEAD)
         d_keys[rows, :] += along_first(d_scores, query)
         d_values[rows, :] += along_first(probs.astype(jnp.bfloat16), grad)
         return carry
 
-    lax.fori_loop(0, BLOCKS, step, 0)
+    lax.fori_loop(0, BLOCKS // 2, step, 0)
     for source in range(SQUARE):
         for slot in range(LINE):
             _, start = stream_row(place, source, slot)
@@ -947,9 +981,12 @@
         return lax.cond(positions[0] >= 0, function, empty, *given)
 
     def across_cores(left, right, product):
-        other = product(left[part_tokens:], right).astype(bf16)
-        own = product(left[:part_tokens], right)
-        return add_low(own, swap_core(other))
+        other = swap_core(product(left[1], right).astype(bf16))
+        own = together(product(left[0], right).astype(bf16))[0]
+        return add_low(own, other)
+
+    def parts_of(value):
+        return value[:part_tokens], value[part_tokens:]
 
     def dot(left, right):
         return jnp.dot(left, right, preferred_element_type=f32)
@@ -962,19 +999,19 @@
         ]
     )
     down_own = lax.dynamic_index_in_dim(w_down.reshape(2, 1, hidden // SQUARE, width), core_index, 0, keepdims=False)
-    out_own = w_out[None]
-    head_block, out_came, down_came = run(
-        turn_line(pick_columns(core_ref, (w_query, w_key, w_value), 1, small)),
-        square_track(out_own),
-        square_track(down_own),
+    rows_own = jnp.concatenate([w_out[None], down_own], axis=1)
+    head_block, rows_came = run(
+        one(pick_columns(core_ref, (w_query, w_key, w_value), 1, small), turn_line),
+        square_track(rows_own),
     )
     x_came, head_came = run(gather_first(inputs), square_track(head_block))
-    x_own, head_later = run(gather_second(*x_came), second_track(head_block, head_came))
-    out_own, down_own = hold((out_own, down_own), x_own)
-    out_later = square_second(out_own, out_came)
-    down_later = square_second(down_own, down_came)
-    x_all = both_cores(x_own)
-    head_block = square_join(from_slots, head_block, head_came, head_later)
+    x_own, head_later, rows_parts = run(
+        gather_second(*x_came),
+        second_track(head_block, head_came),
+        one((rows_own, rows_came), lambda given: second_parts(*given)),
+    )
+    rows_later = swap(rows_parts[0], Y), swap(rows_parts[1], X)
+    head_block = square_join(from_order, head_block, head_came, head_later)
     qkv_w = head_block[:, :ROWS].reshape(width, 3 * heads)
     gains = head_block[:, ROWS : ROWS + 4, :HEAD].astype(f32)
     first_head = place * SQUARE + core_index * 2
@@ -990,10 +1027,6 @@
     ]
     middle = HEAD // 2
     frequency = jnp.power(500000.0, -2.0 * (jnp.arange(HEAD) % middle).astype(f32) / HEAD)
-    angles = jnp.stack(held).astype(f32)[..., None] * frequency
-    sign = jnp.where(jnp.arange(HEAD) < middle, -1.0, 1.0)
-    cosines, sines = together(jnp.cos(angles), jnp.sin(angles) * sign)
-
     def sums_track(value):
         for bit in (Z, FAR):
             (came,) = yield [(value, along(bit))]
@@ -1001,28 +1034,28 @@
         (came,) = yield [(value, swap_core)]
         return value + jnp.flip(came, 2)
 
+    def row_sums(sums):
+        return to_slots(sums.transpose(2, 0, 1, 3))
+
     def row_means(sums):
-        sums = to_slots(sums.transpose(2, 0, 1, 3))
-
-        def finish(sums):
-            return to_slots(sums).transpose(1, 2, 0, 3)[..., None] / width
-
-        return sums, finish
-
-    raw = dot(x_all, qkv_w)
-    raw = raw.reshape(2, LINE, ROWS, 3 * heads)
-    squares = raw[..., : 2 * heads] * raw[..., : 2 * heads]
-    sums = jnp.stack([jnp.sum(squares[..., :heads], axis=-1), jnp.sum(squares[..., heads:], axis=-1)])
-    sums, finish = row_means(sums)
-    sums = region(lambda sums: alone(sums_track(sums)), sums)
-    sums, out_later = together(sums, out_later)
-    scales = lax.rsqrt(finish(sums) + 1e-06)
-    out_w = square_join(from_corner, out_own, out_came, out_later)
-    out_w = lax.dynamic_slice_in_dim(out_w, core_index * 2, 2, 0).reshape(heads, width)
+        return to_slots(sums).transpose(1, 2, 0, 3)[..., None] / width
+
+    def projected(x_own, qkv_w, *held):
+        x_other = swap_core(x_own)
+        raw = jnp.stack([dot(x_own, qkv_w), dot(x_other, qkv_w)]).reshape(2, LINE, ROWS, 3 * heads)
+        squares = raw[..., : 2 * heads] * raw[..., : 2 * heads]
+        sums = jnp.stack([jnp.sum(squares[..., :heads], axis=-1), jnp.sum(squares[..., heads:], axis=-1)])
+        angles = jnp.stack(held).astype(f32)[..., None] * frequency
+        sign = jnp.where(jnp.arange(HEAD) < middle, -1.0, 1.0)
+        return x_other, raw, alone(sums_track(row_sums(sums))), jnp.cos(angles), jnp.sin(angles) * sign
+
+    x_other, raw, sums, cosines, sines = region(projected, x_own, qkv_w, *held)
+    raw, rows_later = together(raw, rows_later)
+    scales = lax.rsqrt(row_means(sums) + 1e-06)
 
     hidden_block = hold(pick_columns(core_ref, (w_gate, w_up), SQUARE), sums)
     line_came = [
-        line_turn(k)(lax.dynamic_index_in_dim(hidden_block, (place + k) % LINE, 0, keepdims=False))
+        line_step(k)(lax.dynamic_index_in_dim(hidden_block, (place + k) % LINE, 0, keepdims=False))
         for k in range(1, LINE)
     ]
     shape = (2, LINE, ROWS, heads)
@@ -1039,35 +1072,39 @@
         message = turn_square(message)
         mixed, lse = attend(place_ref, message, query_places)
         mixed = whole_call(unpack_kernel, [tokens_shape], [core_ref], [turn_square(mixed)])
-        return message, lse, mixed.reshape(tokens, heads)
-
-    message, lse, mixed = region(attended, raw, scales, *tables)
-    mixed, line_came, down_later = together(mixed, line_came, down_later)
+        rows_w = square_join(from_corner, rows_own, rows_came, rows_later)
+        return message, lse, mixed.reshape(tokens, heads), rows_w
+
+    message, lse, mixed, rows_w = region(attended, raw, scales, *tables)
+    mixed, line_came = together(mixed, line_came)
+    out_w = lax.dynamic_slice(rows_w, (core_index * 2, 0, 0), (2, ROWS, width)).reshape(heads, width)
     hidden_own, parts = turned_line(place_ref, hidden_block, line_came)
     hidden_came = swap(parts[0], X), swap(parts[1], Y)
 
-    def branch_of(mixed, out_w, *down):
-        down_w = square_join(from_corner, down[0], down[1:3], down[3:]).reshape(-1, width)
-        return alone(scatter_line(across_cores(mixed, out_w, dot))), down_w
-
-    branch, down_w = region(branch_of, mixed, out_w, down_own, *down_came, *down_later)
+    branch = across_cores(parts_of(mixed), out_w, dot)
+    branch, down_w = region(
+        lambda total, rows: (alone(scatter_line(total)), rows[:, ROWS:].reshape(-1, width)), branch, rows_w
+    )
     branch, hidden_came = together(branch, hidden_came)
     hidden_later = square_second(hidden_own, hidden_came)
 
     def state_of(branch):
         branch_scale = lax.rsqrt(jnp.mean(branch * branch, axis=-1, keepdims=True) + 1e-06)
         hidden_state = inputs.astype(f32) + branch * branch_scale * gains[2]
-        state = both_cores(alone(gather_line(hidden_state.astype(bf16))))
+        state = alone(gather_line(hidden_state.astype(bf16)))
         return branch_scale, hidden_state, state
 
     branch_scale, hidden_state, state = region(state_of, branch)
     state, hidden_later = together(state, hidden_later)
     hidden_w = square_join(from_slots, hidden_own, hidden_came, hidden_later).reshape(width, -1)
 
-    both = dot(state, hidden_w)
-    gate, up = in_two(both)
-    active = (jax.nn.silu(gate) * up).astype(bf16)
-    mlp = alone(scatter_line(across_cores(active, down_w, dot)))
+    state = (state, swap_core(state))
+    both = [dot(part, hidden_w) for part in state]
+    active = [(jax.nn.silu(in_two(part)[0]) * in_two(part)[1]).astype(bf16) for part in both]
+    mlp, (state, both, active) = run(
+        scatter_line(across_cores(active, down_w, dot)),
+        one((state, both, active), lambda pairs: [join(*pair) for pair in pairs]),
+    )
     mlp_scale = lax.rsqrt(jnp.mean(mlp * mlp, axis=-1, keepdims=True) + 1e-06)
     cot = cotangent.astype(f32)
     scaled = cot * gains[3]
@@ -1076,54 +1113,50 @@
     output = (hidden_state + mlp * mlp_scale * gains[3]).astype(bf16)
     mlp_gain_part = jnp.sum(cot * mlp * mlp_scale, axis=0)
 
-    d_active = along_last(d_mlp, down_w)
-    sigma = jax.nn.sigmoid(gate)
-    d_gate = (d_active * up * sigma * (1.0 + gate * (1.0 - sigma))).astype(bf16)
-    d_up = (d_active * gate * sigma).astype(bf16)
-    d_both = jnp.concatenate([d_gate, d_up], axis=1)
-
-    total = across_cores(d_both, hidden_w, along_last)
-
-    def d_state_begun(total, state, d_both, active, d_mlp):
+    d_both = gated_grad(along_last(d_mlp, down_w), both)
+
+    total = across_cores(parts_of(d_both), hidden_w, along_last)
+
+    def d_state_begun(total, state, d_both):
         carried = alone(scatter_first(total))
         hidden_grad = along_first(state, d_both).astype(bf16).reshape(BLOCKS, ROWS, -1)
-        down_grad = along_first(active, d_mlp).astype(bf16).reshape(SQUARE, -1, width)
-        return carried, sum_split(from_order, hidden_grad), sum_split(from_corner, down_grad)
-
-    carried, hidden_split, down_split = region(d_state_begun, total, state, d_both, active, d_mlp)
+        return carried, sum_split(from_order, hidden_grad)
+
+    carried, hidden_split = region(d_state_begun, total, state, d_both)
     hidden_came = sum_first(hidden_split)
 
-    def d_branch_begun(total, *carried):
-        d_resid = cot + alone(scatter_second(total, *carried))
+    def d_branch_begun(total, carried, active, d_mlp):
+        d_resid = cotangent.astype(f32) + alone(scatter_second(total, *carried))
         scaled = d_resid * gains[2]
         d_branch = branch_scale * scaled - branch * branch_scale**3 * jnp.mean(
             branch * scaled, axis=-1, keepdims=True
         )
         attn_gain_part = jnp.sum(d_resid * branch * branch_scale, axis=0)
         norms = jnp.stack([attn_gain_part, mlp_gain_part])
-        return d_resid, alone(gather_first(d_branch.astype(bf16))), norms
-
-    def d_branch_of(*came):
-        d_branch = both_cores(alone(gather_second(*came)))
-        return d_branch, along_last(d_branch, out_w).astype(bf16)
-
-    d_resid, d_branch, norms = region(d_branch_begun, total, *carried)
+        down_grad = along_first(active, d_mlp).astype(bf16).reshape(SQUARE, -1, width)
+        return d_resid, alone(gather_first(d_branch.astype(bf16))), norms, down_grad
+
+    def d_branch_of(d_branch):
+        d_branch = (d_branch, swap_core(d_branch))
+        return d_branch, jnp.stack([along_last(part, out_w).astype(bf16) for part in d_branch])
+
+    d_resid, d_branch, norms, down_grad = region(d_branch_begun, total, carried, active, d_mlp)
     d_branch, hidden_came = together(d_branch, hidden_came)
     hidden_kept, hidden_came = sum_second(hidden_split, hidden_came)
-    d_branch, d_mixed = region(d_branch_of, *d_branch)
+    d_branch, d_mixed = region(d_branch_of, alone(gather_second(*d_branch)))
     d_mixed, hidden_came = together(d_mixed, hidden_came)
     hidden_grad = sum_end(hidden_kept, hidden_came)
-    down_came = sum_first(hold(down_split, hidden_came))
     line_came = [
-        line_turn(k)(lax.dynamic_index_in_dim(hidden_grad, (place + k) % LINE, 0, keepdims=False))
+        line_step(k)(lax.dynamic_index_in_dim(hidden_grad, (place + k) % LINE, 0, keepdims=False))
         for k in range(1, LINE)
     ]
 
-    def attended_back(d_mixed, message, lse, d_branch, mixed, raw, scales, *tables):
+    def attended_back(d_mixed, message, lse, d_branch, mixed, down_grad, raw, scales, *tables):
         grad = whole_call(pack_grad_kernel, [heads_shape], [core_ref], [d_mixed.reshape(shape)])
         grads = attend_back(place_ref, message, query_places, lse, turn_square(grad))
         grads = turn_square(grads)
-        out_grad = along_first(mixed, d_branch).reshape(1, 2, ROWS, width)
+        out_grad = sum(along_first(*pair) for pair in zip(parts_of(mixed), d_branch))
+        out_grad = out_grad.reshape(1, 2, ROWS, width)
         out_grad = jnp.where(core == jnp.arange(2).reshape(2, 1, 1, 1), out_grad, 0.0).astype(bf16)
         shapes = [
             jax.ShapeDtypeStruct((2,) + shape, f32),
@@ -1139,52 +1172,50 @@
                 [grads, raw, scales, *tables],
                 [pltpu.VMEM(shape, f32)] * 2,
             ),
-            sum_split(from_corner, out_grad.reshape(SQUARE, ROWS, width)),
+            sum_split(from_corner, out_grad.reshape(SQUARE, ROWS, width), down_grad),
         )
 
-    (d_head, d_value, sums, head_part), out_split = region(
-        attended_back, d_mixed, message, lse, d_branch, mixed, raw, scales, *tables
-    )
-    d_head, sums, line_came, down_came = together(d_head, sums, line_came, down_came)
+    (d_head, d_value, sums, head_part), rows_split = region(
+        attended_back, d_mixed, message, lse, d_branch, mixed, down_grad, raw, scales, *tables
+    )
+    d_head, sums, line_came = together(d_head, sums, line_came)
     hidden_grad, _ = turned_line(place_ref, hidden_grad, line_came)
     hidden_other = swap_core(hidden_grad)
-    out_came = sum_first(out_split)
-
-    def head_gains(value):
-        for move in (along(X), along(Y), swap_core):
-            (came,) = yield [(value, move)]
-            value = value + came
-        return value
-
-    def all_norms(value):
-        for move in (along(Z), along(FAR), swap_core):
-            (came,) = yield [(value, move)]
-            value = value + came
-        return value
-
-    def norms_over(bit, value):
+    rows_grads_came = sum_first(rows_split)
+
+    head_part = head_part.reshape(2, 1, 2, HEAD)
+    head_part = jnp.where(core == jnp.arange(2).reshape(1, 2, 1, 1), head_part, 0.0)
+
+    def gain_sums(norms, heads):
+        for bit in (Z, FAR):
+            (came,) = yield [(norms, along(bit))]
+            norms = norms + came
+        both = jnp.concatenate([norms.reshape(-1, ROWS), heads.reshape(-1, ROWS)])
+        (came,) = yield [(both, swap_core)]
+        return both + came
+
+    def gains_over(bit, value):
         (came,) = yield [(value, along(bit))]
         return value + came
 
-    head_part = head_part.reshape(2, 1, 2, HEAD)
-    head_part = jnp.where(core == jnp.arange(2).reshape(1, 2, 1, 1), head_part, 0.0)
-    sums, finish = row_means(sums.reshape(2, 2, LINE, ROWS))
-    sums, head_grads, norms = region(
-        lambda *given: run(sums_track(given[0]), head_gains(given[1]), all_norms(given[2])),
-        sums,
-        head_part,
-        norms,
-    )
-    sums, out_came = together(sums, out_came)
-    head_grads = lax.dynamic_index_in_dim(head_grads.reshape(2, SQUARE, HEAD), corner, 1, keepdims=False)
-    qkv_shape = jax.ShapeDtypeStruct(raw.shape, bf16)
-    d_qkv = whole_call(norm_grad_kernel, [qkv_shape], [], [d_head, d_value, raw, scales, finish(sums)])
-    d_qkv = d_qkv.reshape(tokens, -1)
-    total = across_cores(d_qkv, qkv_w, along_last)
-    qkv_split = sum_split(
-        from_order, along_first(x_all, d_qkv).astype(bf16).reshape(BLOCKS, ROWS, -1)
-    )
-
+    def d_qkv_of(sums, head_part, norms, d_head, d_value, raw, scales, *x_parts):
+        sums, gain_grads, x_all = run(
+            sums_track(row_sums(sums.reshape(2, 2, LINE, ROWS))),
+            gain_sums(norms, head_part),
+            one(x_parts, lambda parts: join(*parts)),
+        )
+        qkv_shape = jax.ShapeDtypeStruct(raw.shape, bf16)
+        arrays = [d_head, d_value, raw, scales, row_means(sums)]
+        d_qkv = whole_call(norm_grad_kernel, [qkv_shape], [], arrays).reshape(tokens, -1)
+        total = across_cores(parts_of(d_qkv), qkv_w, along_last)
+        qkv_grad = along_first(x_all, d_qkv).astype(bf16)
+        qkv_grad = with_layout_constraint(qkv_grad, Layout(major_to_minor=(0, 1)))
+        return total, sum_split(from_order, qkv_grad.reshape(BLOCKS, ROWS, -1)), gain_grads
+
+    total, qkv_split, gain_grads = region(
+        d_qkv_of, sums, head_part, norms, d_head, d_value, raw, scales, x_own, x_other
+    )
+    total, rows_grads_came = together(total, rows_grads_came)
     def first_track(split):
         return (yield [(split[1], along(Y)), (split[3], along(X))])
 
@@ -1200,30 +1231,30 @@
     (carried, qkv_came), (gate_grad, up_grad) = region(
         inputs_begun, total, qkv_split, hidden_grad, hidden_other
     )
-    total, out_came = together(total, out_came)
-    d_inputs, qkv_grad, norms = region(
+    def inputs_ended(total, *carried):
+        return d_resid + (yield from scatter_second(total, *carried))
+
+    input_grad, qkv_grad, gain_grads = region(
         lambda total, carried, split, came, norms: run(
-            scatter_second(total, *carried), later_track(split, came), norms_over(X, norms)
+            inputs_ended(total, *carried), later_track(split, came), gains_over(X, norms)
         ),
         total,
         carried,
         qkv_split,
         qkv_came,
-        norms,
-    )
-    input_grad = d_resid + d_inputs
-    qkv_grad, out_grad, down_grad = run(
-        turn_line(qkv_grad), later_track(out_split, out_came), later_track(down_split, down_came)
-    )
-    out_grad, down_grad = out_grad[0], down_grad[0]
-    qkv_other, out_other, down_other, norms = run(
-        one(qkv_grad, swap_core),
-        one(out_grad, swap_core),
-        one(down_grad, swap_core),
-        norms_over(Y, norms),
-    )
-    norms = lax.dynamic_index_in_dim(norms.reshape(2, BLOCKS, ROWS), shard_index, 1, keepdims=False)
-    query_grad, key_grad, value_grad = spread_columns(core_ref, slot_places, qkv_grad, qkv_other, 3, 1)
+        gain_grads,
+    )
+    qkv_grad, rows_grad = run(one(qkv_grad, turn_line), later_track(rows_split, rows_grads_came))
+    qkv_other, rows_other, gain_grads = run(
+        one(qkv_grad, swap_core), one(rows_grad[0], swap_core), gains_over(Y, gain_grads)
+    )
+    out_grad, down_grad = rows_grad[0, :ROWS], rows_grad[0, ROWS:]
+    out_other, down_other = rows_other[:ROWS], rows_other[ROWS:]
+    norms, head_grads = (
+        lax.dynamic_index_in_dim(part.reshape(2, -1, ROWS), number, 1, keepdims=False)
+        for part, number in ((gain_grads[: 2 * BLOCKS], shard_index), (gain_grads[2 * BLOCKS :], corner))
+    )
+    query_grad, key_grad, value_grad = spread_columns(core_ref, slots, qkv_grad, qkv_other, 3, 1)
     down_grad = jnp.concatenate(
         [jnp.where(core, down_other, down_grad), jnp.where(core, down_grad, down_other)]
     )

time: 867 us -> 820 us (0.946)
  waiting for transfers between devices: 353 us -> 288 us
  other arithmetic: 50.7 us -> 61.9 us
  blocking collectives: 10.4 us -> 0 us
    ppermute x12 -> x6, waiting for transfers between devices: 33.8 us -> 0.02 us  [line_step(): return lambda value: lax.ppermute(value, 'shard', pairs)]
    ppermute x40, waiting for transfers between devices: 203 us -> 173 us  [line_move(): return lambda value: lax.ppermute(value, 'shard', pairs)]
    ppermute x42 -> x32, waiting for transfers between devices: 36 us -> 57.4 us  [swap(): lax.ppermute(value, 'shard', [(source, source ^ bit) for source in range(...]
    ppermute x17 -> x15, waiting for transfers between devices: 23.7 us -> 8.28 us  [swap_core(): return lax.ppermute(value, 'grp', [(0, 1), (1, 0)])]
    all_to_all x1 -> x0, blocking collectives: 10.4 us -> none  [turn_square(): lax.all_to_all(message, 'shard', 0, 0, tiled=True, axis_index_groups=SQUA...]
    all_to_all x0 -> x2, starting transfers between devices: none -> 9.94 us  [turn_line(): lax.all_to_all(block, 'shard', 0, 0, tiled=True, axis_index_groups=LINES)]
    all_to_all x3 -> x4, waiting for transfers between devices: 56.4 us -> 47 us  [turn_square(): lax.all_to_all(message, 'shard', 0, 0, tiled=True, axis_index_groups=SQUA...]
    ppermute x42 -> x32, starting transfers between devices: 41.9 us -> 33.8 us  [swap(): lax.ppermute(value, 'shard', [(source, source ^ bit) for source in range(...]
  transfers between devices with their start and end apart: 114 -> 99, of which waited for: 53 -> 49; matrix products, arithmetic and copies ran while one was open for 10% -> 14% of each run, Pallas kernels for 10% -> 13%
where the time goes in v4:
time: 820 us; the launch traced here: 809 us
  waiting for transfers between devices  288 us (35%)
  starting transfers between devices  172 us (21%)
  Pallas kernels  133 us (16%)
  matrix products  89 us (11%)
  other arithmetic  61.9 us (8%)
  local copies, waits for them, and re-layouts  61.7 us (8%)
    ppermute x40, waiting for transfers between devices, line_move(): return lambda value: lax.ppermute(value, 'shard', pairs)  173 us
    pallas_call x37, Pallas kernels, whole_call(): pl.pallas_call(kernel, out_shape=shapes[0] if single else shapes, in_spec...  128 us
    ppermute x40, starting transfers between devices, line_move(): return lambda value: lax.ppermute(value, 'shard', pairs)  100 us
    ppermute x32, waiting for transfers between devices, swap(): lax.ppermute(value, 'shard', [(source, source ^ bit) for source in range(...  57.4 us
    all_to_all x4, waiting for transfers between devices, turn_square(): lax.all_to_all(message, 'shard', 0, 0, tiled=True, axis_index_groups=SQUA...  47 us
    dot_general x8, matrix products, dot(): return jnp.dot(left, right, preferred_element_type=f32)  34.7 us
    ppermute x32, starting transfers between devices, swap(): lax.ppermute(value, 'shard', [(source, source ^ bit) for source in range(...  33.8 us
    unnamed x138, local copies, waits for them, and re-layouts  30 us
  transfers between devices with their start and end apart: 99, of which 49 were waited for; matrix products, arithmetic and copies ran while one was open for 14% of the time, Pallas kernels for 13%

profile of v4, /device:TPU:0, one launch (start us, length us, event | category | flops | bytes accessed | tf_op | source)
XLA Modules:
  0.0 808.9 jit_solution(2471882352000932503)
XLA Ops:
  15.2 16.2 %collective-permute-done.39.first_ref = bf16[1,384,1024]{2,1,0:T(8,128)(2,1)S(1)} collective-permute-done((bf16[1,384,1024]{2,1,0:T(8,128)(2,1)}, bf16[1,384,1024]{2,1,0:T(8,128)(2,1)S(1)}, u32[]{:S(2)}, u32[]{:S(2)}) %collective-permute-start.39) | collective-permute-done | bytes 786464 | tf_op jit(solution)/shard_map/ppermute | solution.py:288
  79.4 9.2 %collective-permute-done.47.further_ref = bf16[128,2048]{1,0:T(8,128)(2,1)} collective-permute-done((bf16[128,2048]{1,0:T(8,128)(2,1)}, bf16[128,2048]{1,0:T(8,128)(2,1)}, u32[]{:S(2)}, u32[]{:S(2)}) %collective-permute-start.47) | collective-permute-done | bytes 524320 | tf_op jit(solution)/shard_map/ppermute | solution.py:309
  97.3 20.3 %conditional.11 = (bf16[512,2048]{1,0:T(8,128)(2,1)}, f32[2,4,128,768]{3,2,1,0:T(8,128)}, f32[4,2,2,128]{3,2,1,0:T(2,128)S(1)}, f32[2,4,128,128]{3,2,1,0:T(8,128)S(1)}, f32[2,4,128,128]{3,2,1,0:T(8,128)S(1)}) conditional(s32[]{:T(128)} %bitcast.39, () %tuple.157, (bf16[512,2048]{1,0:T(8,128)(2,1)}, bf16[2048,768]{1,0:T(8,128)(2,1)}, ...), branch_computations={%region_0.1_spmd, %region_1.4_spmd} | conditional | flops 3223876096 | bytes 49536476 | solution.py:981
  124.1 62.0 %conditional.12 = (bf16[4,16,128,128]{3,2,1,0:T(8,128)(2,1)}, f32[16,128,1]{2,1,0:T(8,128)}, bf16[1024,256]{1,0:T(8,128)(2,1)}, bf16[4,384,2048]{2,1,0:T(8,128)(2,1)}) conditional(s32[]{:T(128)} %bitcast.39, () %tuple.156, (s32[1]{0:T(128)}, s32[1]{0:T(128)}, f32[2,4,128,768]{3,2,1,0:T(8,128)}, f32[2,2,4,128,1]{3,2,1,0,4:T(4,128)S(1)}, ...), branch_computations={%region_4.5_spmd, %region_5.6_spmd} | conditional | bytes 48828624 | solution.py:981
  137.4 24.9 %all-to-all-done.message_ref = bf16[4,16,128,128]{3,2,1,0:T(8,128)(2,1)} async-done(((bf16[4,16,128,128]{3,2,1,0:T(8,128)(2,1)}), bf16[4,16,128,128]{3,2,1,0:T(8,128)(2,1)}, u32[]{:S(2)}, u32[]{:S(2)}) %all-to-all-start) | async-done | bytes 2097184 | tf_op jit(solution)/shard_map/cond/branch_1_fun/all_to_all | solution.py:924
  162.3 11.1 %branch_1_fun.17 = (bf16[4,4,128,128]{3,2,1,0:T(8,128)(2,1)S(1)}, f32[16,128,1]{2,1,0:T(8,128)}) custom-call(s32[1]{0:T(128)} %get-tuple-element.210.place_ref, bf16[4,16,128,128]{3,2,1,0:T(8,128)(2,1)} %all-to-all-done.message_ref, s32[16,128,1]{2,1,0:T(8,128)S(1)} %copy.48.pos_ref), custom_call_target="tpu_custom_call" | custom-call | bytes 4210688 | tf_op jit(solution)/shard_map/cond/branch_1_fun/pallas_call | solution.py:592
  198.2 53.6 %conditional.13 = (f32[128,2048]{1,0:T(8,128)}, bf16[1024,2048]{1,0:T(8,128)(2,1)}) conditional(s32[]{:T(128)} %bitcast.39, () %tuple.155, (bf16[512,2048]{1,0:T(8,128)(2,1)}, bf16[4,384,2048]{2,1,0:T(8,128)(2,1)}) %tuple.169), branch_computations={%region_6.7_spmd, %region_7.8_spmd} | conditional | flops 5242900 | bytes 27787680 | solution.py:981
  215.8 10.2 %collective-permute-done.2 = bf16[128,2048]{1,0:T(8,128)(2,1)} collective-permute-done((bf16[128,2048]{1,0:T(8,128)(2,1)}, bf16[128,2048]{1,0:T(8,128)(2,1)}, u32[]{:S(2)}, u32[]{:S(2)}) %collective-permute-start.2) | collective-permute-done | bytes 524320 | tf_op jit(solution)/shard_map/cond/branch_1_fun/ppermute | solution.py:309
  257.4 47.5 %conditional.14 = (f32[128,1]{0,1:T(1,128)S(1)}, f32[128,2048]{1,0:T(8,128)}, bf16[512,2048]{1,0:T(8,128)(2,1)}) conditional(s32[]{:T(128)} %bitcast.39, () %tuple.154, (f32[128,2048]{1,0:T(8,128)}, bf16[128,2048]{1,0:T(8,128)(2,1)S(1)}, f32[4,2048]{1,0:T(4,128)S(1)}) %tuple.300), branch_computations={%region_8.9_spmd, %region_9.11_spmd} | conditional | flops 2097298 | bytes 22571924 | solution.py:981
  281.2 13.5 %collective-permute-done.18.lefts_ref = bf16[128,2048]{1,0:T(8,128)(2,1)S(1)} collective-permute-done((bf16[128,2048]{1,0:T(8,128)(2,1)}, bf16[128,2048]{1,0:T(8,128)(2,1)S(1)}, u32[]{:S(2)}, u32[]{:S(2)}) %collective-permute-start.18) | collective-permute-done | bytes 524320 | tf_op jit(solution)/shard_map/cond/branch_1_fun/ppermute | solution.py:309
  411.3 13.8 %collective-permute-done.71.lefts_ref = bf16[128,2048]{1,0:T(8,128)(2,1)S(1)} collective-permute-done((bf16[128,2048]{1,0:T(8,128)(2,1)S(1)}, bf16[128,2048]{1,0:T(8,128)(2,1)S(1)}, u32[]{:S(2)}, u32[]{:S(2)}) %collective-permute-start.71) | collective-permute-done | bytes 524320 | tf_op jit(solution)/shard_map/ppermute | solution.py:309
  425.1 9.8 %collective-permute-done.72.further_ref = bf16[128,2048]{1,0:T(8,128)(2,1)S(1)} collective-permute-done((bf16[128,2048]{1,0:T(8,128)(2,1)S(1)}, bf16[128,2048]{1,0:T(8,128)(2,1)S(1)}, u32[]{:S(2)}, u32[]{:S(2)}) %collective-permute-start.72) | collective-permute-done | bytes 524320 | tf_op jit(solution)/shard_map/ppermute | solution.py:309
  467.3 24.8 %conditional.15 = (bf16[128,2048]{1,0:T(8,128)(2,1)}, bf16[128,2048]{1,0:T(8,128)(2,1)}, bf16[128,2048]{1,0:T(8,128)(2,1)}, bf16[2,4,128,1024]{3,2,1,0:T(8,128)(...) conditional(s32[]{:T(128)} %bitcast.39, () %tuple.186, ...), branch_computations={%region_13.14_spmd, %region_14.15_spmd} | conditional | flops 8594391040 | bytes 42467684 | solution.py:981
  475.7 12.0 %convolution_convert_fusion = bf16[2048,2048]{1,0:T(8,128)(2,1)S(1)} fusion(bf16[1024,2048]{1,0:T(8,128)(2,1)} %get-tuple-element.258, bf16[1024,2048]{1,0:T(8,128)(2,1)} %get-tuple-element.259), kind=kOutput, calls=%fused_computation.35 | convolution fusion | flops 8594128896 | bytes 16777216 | tf_op jit(solution)/shard_map/cond/branch_1_fun/dot_general | solution.py:51
  497.3 45.4 %conditional.16 = (f32[128,2048]{1,0:T(8,128)}, bf16[128,2048]{1,0:T(8,128)(2,1)}, bf16[128,2048]{1,0:T(8,128)(2,1)}, bf16[128,2048]{1,0:T(8,128)(2,1)}, f32[2,2...) conditional(s32[]{:T(128)} %bitcast.39, () %tuple.181, (bf16[128,2048]{1,0:T(8,128)(2,1)}, ...), branch_computations={%region_16.17_spmd, %region_17.20_spmd} | conditional | flops 4306502144 | bytes 68244512 | solution.py:981
  553.8 14.8 %collective-permute-done.78.lefts_ref = bf16[128,2048]{1,0:T(8,128)(2,1)S(1)} collective-permute-done((bf16[128,2048]{1,0:T(8,128)(2,1)}, bf16[128,2048]{1,0:T(8,128)(2,1)S(1)}, u32[]{:S(2)}, u32[]{:S(2)}) %collective-permute-start.78) | collective-permute-done | bytes 524320 | tf_op jit(solution)/shard_map/ppermute | solution.py:309
  568.6 10.2 %collective-permute-done.79.further_ref = bf16[128,2048]{1,0:T(8,128)(2,1)S(1)} collective-permute-done((bf16[128,2048]{1,0:T(8,128)(2,1)S(1)}, bf16[128,2048]{1,0:T(8,128)(2,1)S(1)}, u32[]{:S(2)}, u32[]{:S(2)}) %collective-permute-start.79) | collective-permute-done | bytes 524320 | tf_op jit(solution)/shard_map/ppermute | solution.py:309
  596.8 65.7 %conditional.18 = (f32[2,2,4,128,256]{4,3,2,1,0:T(8,128)}, bf16[2,4,128,256]{3,2,1,0:T(8,128)(2,1)}, f32[2,2,4,128,1]{4,3,2,1,0:T(8,128)}, f32[2,256]{1,0:T(2,12...) conditional(s32[]{:T(128)} %bitcast.39, () %tuple.179, ...), branch_computations={%region_22.23_spmd, %region_23.24_spmd} | conditional | flops 1075838976 | bytes 60903612 | solution.py:981
  609.9 14.2 %branch_1_fun.23 = bf16[4,16,128,128]{3,2,1,0:T(8,128)(2,1)S(1)} custom-call(s32[1]{0:T(128)} %get-tuple-element.286.place_ref, bf16[4,16,128,128]{3,2,1,0:T(8,128)(2,1)} %get-tuple-element.287.message_ref, s32[16,128,1]{2,1,0:T(8,128)S(1)} %copy.49.pos_ref, f32[16,128,1]{2,1,0:T(8,128)} %get-tuple-element.289.lse_ref, ...), custom_call_target="tpu_custom_call" | custom-call | bytes 5275648 | tf_op jit(solution)/shard_map/cond/branch_1_fun/pallas_call | solution.py:592
  641.3 12.7 %all-to-all-done.3.came_ref = bf16[4,16,128,128]{3,2,1,0:T(8,128)(2,1)} async-done(((bf16[4,16,128,128]{3,2,1,0:T(8,128)(2,1)}), bf16[4,16,128,128]{3,2,1,0:T(8,128)(2,1)}, u32[]{:S(2)}, u32[]{:S(2)}) %all-to-all-start.3) | async-done | bytes 2097184 | tf_op jit(solution)/shard_map/cond/branch_1_fun/all_to_all | solution.py:924
  667.9 35.5 %conditional.19 = (bf16[512,2048]{1,0:T(8,128)(2,1)S(1)}, bf16[2,4,128,384]{3,2,1,0:T(8,128)(2,1)}, bf16[2,4,128,384]{3,2,1,0:T(8,128)(2,1)}, bf16[2,4,128,384]{...) conditional(s32[]{:T(128)} %bitcast.39, () %tuple.178, ...), branch_computations={%region_24.25_spmd, %region_25.26_spmd} | conditional | flops 6450374656 | bytes 111975696 | solution.py:981
  710.0 27.8 %conditional.20 = (bf16[128,2048]{1,0:T(8,128)(2,1)}, bf16[128,2048]{1,0:T(8,128)(2,1)}, bf16[128,2048]{1,0:T(8,128)(2,1)}, bf16[2,4,128,384]{3,2,1,0:T(8,128)(2...) conditional(s32[]{:T(128)} %bitcast.39, () %tuple.198, ...), branch_computations={%region_26.27_spmd, %region_27.28_spmd} | conditional | flops 262182 | bytes 23593444 | solution.py:981
  737.8 28.4 %conditional.21 = (f32[128,2048]{1,0:T(8,128)}, bf16[4,128,768]{2,1,0:T(8,128)(2,1)S(1)}, f32[40,128]{1,0:T(8,128)S(1)}) conditional(s32[]{:T(128)} %bitcast.39, () %tuple.177, (bf16[512,2048]{1,0:T(8,128)(2,1)}, bf16[128,2048]{1,0:T(8,128)(2,1)}, bf16[128,2048]{1,0:T(8,128)(2,1)}, bf16[128,2048]{1,0:T(8,128)(2,1)}, ...), branch_computations={%region_28.29_spmd, %region_29.30_spmd} | conditional | flops 5248019 | bytes 32649658 | solution.py:981
  772.6 14.2 %collective-permute-done.88.came_first = bf16[1,384,1024]{2,1,0:T(8,128)(2,1)S(1)} collective-permute-done((bf16[1,384,1024]{2,1,0:T(8,128)(2,1)}, bf16[1,384,1024]{2,1,0:T(8,128)(2,1)S(1)}, u32[]{:S(2)}, u32[]{:S(2)}) %collective-permute-start.88) | collective-permute-done | bytes 786464 | tf_op jit(solution)/shard_map/ppermute | solution.py:288
  (544 shorter events, 624.7 us)
Async XLA Ops:
  5.7 28.7 %all-to-all-start.4 = ((bf16[4,144,768]{2,1,0:T(8,128)(2,1)}), bf16[4,144,768]{2,1,0:T(8,128)(2,1)S(1)}, u32[]{:S(2)}, u32[]{:S(2)}) async-start(bf16[4,144,768]{2,1,0:T(8,128)(2,1)} %shard_map.237), calls=%async_computation.4 | async-start | bytes 1769472 | tf_op jit(solution)/shard_map/all_to_all | solution.py:452
  57.1 31.5 %collective-permute-start.48 = (bf16[2,4,144,384]{3,2,1,0:T(8,128)(2,1)}, bf16[2,4,144,384]{3,2,1,0:T(8,128)(2,1)}, u32[]{:S(2)}, u32[]{:S(2)}) collective-permute-start(bf16[2,4,144,384]{3,2,1,0:T(8,128)(2,1)} %get-tuple-element.599), channel_id=1, source_target_pairs={{0,2},{1,3},{2,0},{3,1},{4,6},{5,7},{6,4},{7,5},{8,10},{9,11},{10,... | collective-permute-start | bytes 2654216 | tf_op jit(solution)/shard_map/ppermute | solution.py:288
  58.6 30.0 %collective-permute-start.49 = (bf16[2,4,144,384]{3,2,1,0:T(8,128)(2,1)}, bf16[2,4,144,384]{3,2,1,0:T(8,128)(2,1)}, u32[]{:S(2)}, u32[]{:S(2)}) collective-permute-start(bf16[2,4,144,384]{3,2,1,0:T(8,128)(2,1)} %get-tuple-element.600), channel_id=1, source_target_pairs={{0,1},{1,0},{2,3},{3,2},{4,5},{5,4},{6,7},{7,6},{8,9},{9,8},{10,11... | collective-permute-start | bytes 2654216 | tf_op jit(solution)/shard_map/ppermute | solution.py:288
  90.4 33.2 %collective-permute-start.51 = (bf16[2,1,384,1024]{3,2,1,0:T(8,128)(2,1)}, bf16[2,1,384,1024]{3,2,1,0:T(8,128)(2,1)}, u32[]{:S(2)}, u32[]{:S(2)}) collective-permute-start(bf16[2,1,384,1024]{3,2,1,0:T(8,128)(2,1)} %get-tuple-element.612), channel_id=1, source_target_pairs={{0,2},{1,3},{2,0},{3,1},{4,6},{5,7},{6,4},{7,5},{8,10},{9,11},{10,... | collective-permute-start | bytes 4718600 | tf_op jit(solution)/shard_map/ppermute | solution.py:288
  91.0 32.6 %collective-permute-start.52 = (bf16[2,1,384,1024]{3,2,1,0:T(8,128)(2,1)}, bf16[2,1,384,1024]{3,2,1,0:T(8,128)(2,1)}, u32[]{:S(2)}, u32[]{:S(2)}) collective-permute-start(bf16[2,1,384,1024]{3,2,1,0:T(8,128)(2,1)} %get-tuple-element.613), channel_id=1, source_target_pairs={{0,1},{1,0},{2,3},{3,2},{4,5},{5,4},{6,7},{7,6},{8,9},{9,8},{10,11... | collective-permute-start | bytes 4718600 | tf_op jit(solution)/shard_map/ppermute | solution.py:288
  119.0 67.2 %collective-permute-start.53 = (bf16[128,2048]{1,0:T(8,128)(2,1)}, bf16[128,2048]{1,0:T(8,128)(2,1)}, u32[]{:S(2)}, u32[]{:S(2)}) collective-permute-start(bf16[128,2048]{1,0:T(8,128)(2,1)} %get-tuple-element.954), channel_id=1, source_target_pairs={{0,4},{1,5},{2,6},{3,7},{4,8},{5,9},{6,10},{7,11},{8,12},{9,13},{1... | collective-permute-start | bytes 1572872 | tf_op jit(solution)/shard_map/ppermute | solution.py:317
  119.0 67.2 %collective-permute-start.54 = (bf16[128,2048]{1,0:T(8,128)(2,1)}, bf16[128,2048]{1,0:T(8,128)(2,1)}, u32[]{:S(2)}, u32[]{:S(2)}) collective-permute-start(bf16[128,2048]{1,0:T(8,128)(2,1)} %get-tuple-element.953), channel_id=1, source_target_pairs={{0,8},{1,9},{2,10},{3,11},{4,12},{5,13},{6,14},{7,15},{8,0},{9,1},... | collective-permute-start | bytes 1572872 | tf_op jit(solution)/shard_map/ppermute | solution.py:317
  119.3 66.9 %collective-permute-start.55 = (bf16[128,2048]{1,0:T(8,128)(2,1)}, bf16[128,2048]{1,0:T(8,128)(2,1)}, u32[]{:S(2)}, u32[]{:S(2)}) collective-permute-start(bf16[128,2048]{1,0:T(8,128)(2,1)} %get-tuple-element.952), channel_id=1, source_target_pairs={{0,12},{1,13},{2,14},{3,15},{4,0},{5,1},{6,2},{7,3},{8,4},{9,5},{1... | collective-permute-start | bytes 1572872 | tf_op jit(solution)/shard_map/ppermute | solution.py:317
  132.6 29.8 %all-to-all-start = ((bf16[4,16,128,128]{3,2,1,0:T(8,128)(2,1)}), bf16[4,16,128,128]{3,2,1,0:T(8,128)(2,1)}, u32[]{:S(2)}, u32[]{:S(2)}) async-start(bf16[4,16,128,128]{3,2,1,0:T(8,128)(2,1)} %copy-done.8), calls=%async_computation | async-start | bytes 4194304 | tf_op jit(solution)/shard_map/cond/branch_1_fun/all_to_all | solution.py:924
  192.3 59.5 %collective-permute-start.57 = (bf16[4,128,1024]{2,1,0:T(8,128)(2,1)}, bf16[4,128,1024]{2,1,0:T(8,128)(2,1)S(1)}, u32[]{:S(2)}, u32[]{:S(2)}) collective-permute-start(bf16[4,128,1024]{2,1,0:T(8,128)(2,1)} %get-tuple-element.628), channel_id=1, source_target_pairs={{0,1},{1,0},{2,3},{3,2},{4,5},{5,4},{6,7},{7,6},{8,9},{9,8},{10,11... | collective-permute-start | bytes 3145736 | tf_op jit(solution)/shard_map/ppermute | solution.py:288
  193.7 58.1 %collective-permute-start.58 = (bf16[4,128,1024]{2,1,0:T(8,128)(2,1)}, bf16[4,128,1024]{2,1,0:T(8,128)(2,1)}, u32[]{:S(2)}, u32[]{:S(2)}) collective-permute-start(bf16[4,128,1024]{2,1,0:T(8,128)(2,1)} %get-tuple-element.629), channel_id=1, source_target_pairs={{0,2},{1,3},{2,0},{3,1},{4,6},{5,7},{6,4},{7,5},{8,10},{9,11},{10,... | collective-permute-start | bytes 3145736 | tf_op jit(solution)/shard_map/ppermute | solution.py:288
  255.3 49.6 %collective-permute-start.59 = (bf16[2,4,128,1024]{3,2,1,0:T(8,128)(2,1)}, bf16[2,4,128,1024]{3,2,1,0:T(8,128)(2,1)}, u32[]{:S(2)}, u32[]{:S(2)}) collective-permute-start(bf16[2,4,128,1024]{3,2,1,0:T(8,128)(2,1)} %get-tuple-element.636), channel_id=1, source_target_pairs={{0,2},{1,3},{2,0},{3,1},{4,6},{5,7},{6,4},{7,5},{8,10},{9,11},{10,... | collective-permute-start | bytes 6291464 | tf_op jit(solution)/shard_map/ppermute | solution.py:288
  256.8 48.1 %collective-permute-start.60 = (bf16[2,4,128,1024]{3,2,1,0:T(8,128)(2,1)}, bf16[2,4,128,1024]{3,2,1,0:T(8,128)(2,1)}, u32[]{:S(2)}, u32[]{:S(2)}) collective-permute-start(bf16[2,4,128,1024]{3,2,1,0:T(8,128)(2,1)} %get-tuple-element.637), channel_id=1, source_target_pairs={{0,1},{1,0},{2,3},{3,2},{4,5},{5,4},{6,7},{7,6},{8,9},{9,8},{10,11... | collective-permute-start | bytes 6291464 | tf_op jit(solution)/shard_map/ppermute | solution.py:288
  492.1 50.6 %collective-permute-start.75 = (bf16[2,4,128,1024]{3,2,1,0:T(8,128)(2,1)}, bf16[2,4,128,1024]{3,2,1,0:T(8,128)(2,1)S(1)}, u32[]{:S(2)}, u32[]{:S(2)}) collective-permute-start(bf16[2,4,128,1024]{3,2,1,0:T(8,128)(2,1)} %get-tuple-element.678), channel_id=1, source_target_pairs={{0,2},{1,3},{2,0},{3,1},{4,6},{5,7},{6,4},{7,5},{8,10},{9,11},{10,... | collective-permute-start | bytes 6291464 | tf_op jit(solution)/shard_map/ppermute | solution.py:288
  493.6 49.2 %collective-permute-start.76 = (bf16[2,4,128,1024]{3,2,1,0:T(8,128)(2,1)}, bf16[2,4,128,1024]{3,2,1,0:T(8,128)(2,1)}, u32[]{:S(2)}, u32[]{:S(2)}) collective-permute-start(bf16[2,4,128,1024]{3,2,1,0:T(8,128)(2,1)} %get-tuple-element.679), channel_id=1, source_target_pairs={{0,1},{1,0},{2,3},{3,2},{4,5},{5,4},{6,7},{7,6},{8,9},{9,8},{10,11... | collective-permute-start | bytes 6291464 | tf_op jit(solution)/shard_map/ppermute | solution.py:288
  547.3 39.9 %collective-permute-start.80 = (bf16[4,128,1024]{2,1,0:T(8,128)(2,1)}, bf16[4,128,1024]{2,1,0:T(8,128)(2,1)}, u32[]{:S(2)}, u32[]{:S(2)}) collective-permute-start(bf16[4,128,1024]{2,1,0:T(8,128)(2,1)} %get-tuple-element.694), channel_id=1, source_target_pairs={{0,1},{1,0},{2,3},{3,2},{4,5},{5,4},{6,7},{7,6},{8,9},{9,8},{10,11... | collective-permute-start | bytes 3145736 | tf_op jit(solution)/shard_map/ppermute | solution.py:288
  548.8 38.4 %collective-permute-start.81 = (bf16[4,128,1024]{2,1,0:T(8,128)(2,1)}, bf16[4,128,1024]{2,1,0:T(8,128)(2,1)}, u32[]{:S(2)}, u32[]{:S(2)}) collective-permute-start(bf16[4,128,1024]{2,1,0:T(8,128)(2,1)} %get-tuple-element.695), channel_id=1, source_target_pairs={{0,2},{1,3},{2,0},{3,1},{4,6},{5,7},{6,4},{7,5},{8,10},{9,11},{10,... | collective-permute-start | bytes 3145736 | tf_op jit(solution)/shard_map/ppermute | solution.py:288
  592.9 69.5 %collective-permute-start.82 = (bf16[128,2048]{1,0:T(8,128)(2,1)}, bf16[128,2048]{1,0:T(8,128)(2,1)}, u32[]{:S(2)}, u32[]{:S(2)}) collective-permute-start(bf16[128,2048]{1,0:T(8,128)(2,1)} %get-tuple-element.949), channel_id=1, source_target_pairs={{0,4},{1,5},{2,6},{3,7},{4,8},{5,9},{6,10},{7,11},{8,12},{9,13},{1... | collective-permute-start | bytes 1572872 | tf_op jit(solution)/shard_map/ppermute | solution.py:317
  592.9 69.5 %collective-permute-start.83 = (bf16[128,2048]{1,0:T(8,128)(2,1)}, bf16[128,2048]{1,0:T(8,128)(2,1)}, u32[]{:S(2)}, u32[]{:S(2)}) collective-permute-start(bf16[128,2048]{1,0:T(8,128)(2,1)} %get-tuple-element.948), channel_id=1, source_target_pairs={{0,8},{1,9},{2,10},{3,11},{4,12},{5,13},{6,14},{7,15},{8,0},{9,1},... | collective-permute-start | bytes 1572872 | tf_op jit(solution)/shard_map/ppermute | solution.py:317
  592.9 69.5 %collective-permute-start.84 = (bf16[128,2048]{1,0:T(8,128)(2,1)}, bf16[128,2048]{1,0:T(8,128)(2,1)}, u32[]{:S(2)}, u32[]{:S(2)}) collective-permute-start(bf16[128,2048]{1,0:T(8,128)(2,1)} %get-tuple-element.947), channel_id=1, source_target_pairs={{0,12},{1,13},{2,14},{3,15},{4,0},{5,1},{6,2},{7,3},{8,4},{9,5},{1... | collective-permute-start | bytes 1572872 | tf_op jit(solution)/shard_map/ppermute | solution.py:317
  625.4 28.5 %all-to-all-start.3 = ((bf16[4,16,128,128]{3,2,1,0:T(8,128)(2,1)}), bf16[4,16,128,128]{3,2,1,0:T(8,128)(2,1)}, u32[]{:S(2)}, u32[]{:S(2)}) async-start(bf16[4,16,128,128]{3,2,1,0:T(8,128)(2,1)} %copy-done.9), calls=%async_computation.3 | async-start | bytes 4194304 | tf_op jit(solution)/shard_map/cond/branch_1_fun/all_to_all | solution.py:924
  665.9 42.4 %collective-permute-start.87 = (bf16[4,128,2048]{2,1,0:T(8,128)(2,1)}, bf16[4,128,2048]{2,1,0:T(8,128)(2,1)}, u32[]{:S(2)}, u32[]{:S(2)}) collective-permute-start(bf16[4,128,2048]{2,1,0:T(8,128)(2,1)} %get-tuple-element.723), channel_id=1, source_target_pairs={{0,16},{16,0},{1,17},{17,1},{2,18},{18,2},{3,19},{19,3},{4,20},{20... | collective-permute-start | bytes 6291464 | tf_op jit(solution)/shard_map/ppermute | solution.py:292
  665.9 37.5 %collective-permute-start.85 = (bf16[2,1,384,1024]{3,2,1,0:T(8,128)(2,1)}, bf16[2,1,384,1024]{3,2,1,0:T(8,128)(2,1)}, u32[]{:S(2)}, u32[]{:S(2)}) collective-permute-start(bf16[2,1,384,1024]{3,2,1,0:T(8,128)(2,1)} %get-tuple-element.715), channel_id=1, source_target_pairs={{0,2},{1,3},{2,0},{3,1},{4,6},{5,7},{6,4},{7,5},{8,10},{9,11},{10,... | collective-permute-start | bytes 4718600 | tf_op jit(solution)/shard_map/ppermute | solution.py:288
  667.4 36.8 %collective-permute-start.86 = (bf16[2,1,384,1024]{3,2,1,0:T(8,128)(2,1)}, bf16[2,1,384,1024]{3,2,1,0:T(8,128)(2,1)}, u32[]{:S(2)}, u32[]{:S(2)}) collective-permute-start(bf16[2,1,384,1024]{3,2,1,0:T(8,128)(2,1)} %get-tuple-element.716), channel_id=1, source_target_pairs={{0,1},{1,0},{2,3},{3,2},{4,5},{5,4},{6,7},{7,6},{8,9},{9,8},{10,11... | collective-permute-start | bytes 4718600 | tf_op jit(solution)/shard_map/ppermute | solution.py:288
  (162 other events, 1578.0 us)

commit v5 on v4

--- a/solution.py
+++ b/solution.py
@@ -276,8 +276,6 @@
 X, Y, Z, FAR = 1, 2, 4, 8
 ROWS = 128
 BLOCKS = 16
-QUERIES = 2 * ROWS
-WINDOW = DOC_LEN + QUERIES
 SHARE = 256
 SCALING = 1.0 / math.sqrt(HEAD)
 LINES = [[SQUARE * z + r for z in range(LINE)] for r in range(SQUARE)]
@@ -748,32 +746,25 @@
     value_ref,
     sums_ref,
     gain_grad_ref,
-    d_key,
-    d_value,
 ):
-    for group in range(2):
-        part = part_of(group, core_ref[0])
-        for head in range(2):
-            for slot in range(LINE):
-                for number, ref in ((1, d_key), (2, d_value)):
-                    ref[part, slot, :, head_lanes(head)] = came_ref[
-                        2 * group + head, LINE * number + slot
-                    ].astype(jnp.float32)
-    for head in range(2):
-        for number, slot in enumerate(halo_slots(place_ref[0])):
-            for first, ref in ((12, d_key), (14, d_value)):
-                ref[core_ref[0], slot, :, head_lanes(head)] += came_ref[2 + head, first + number].astype(
-                    jnp.float32
-                )
+    core = core_ref[0]
+
+    def summed(first, part, slot, head):
+        total = came_ref[2 * part_of(part, core) + head, first + slot].astype(jnp.float32)
+        for number, end_slot in enumerate(halo_slots(place_ref[0])):
+            here = jnp.where((core == part) & (end_slot == slot), 1.0, 0.0)
+            total += here * came_ref[2 + head, 10 + first // 2 + number].astype(jnp.float32)
+        return total
+
     totals = [[jnp.zeros((1, HEAD), jnp.float32) for _ in range(2)] for _ in range(2)]
-    for group in range(2):
-        part = part_of(group, core_ref[0])
+    for part in range(2):
         for slot in range(LINE):
             sums = [jnp.zeros((ROWS, 1), jnp.float32) for _ in range(2)]
             for head in range(2):
                 lanes = head_lanes(head)
-                d_query = came_ref[2 * group + head, slot].astype(jnp.float32)
-                for number, grad in ((0, d_query), (1, d_key[part, slot, :, lanes])):
+                value_ref[part, slot, :, lanes] = summed(8, part, slot, head).astype(jnp.bfloat16)
+                d_query = came_ref[2 * part_of(part, core) + head, slot].astype(jnp.float32)
+                for number, grad in ((0, d_query), (1, summed(4, part, slot, head))):
                     grad = rotated_back(grad, cos_ref[part, slot], sin_ref[part, slot])
                     raw_lanes = slice((2 * number + head) * HEAD, (2 * number + head + 1) * HEAD)
                     raw = raw_ref[part, slot, :, raw_lanes]
@@ -788,7 +779,6 @@
     for number in range(2):
         for head in range(2):
             gain_grad_ref[number : number + 1, head_lanes(head)] = totals[number][head]
-    value_ref[...] = d_value[...].astype(jnp.bfloat16)
 
 
 def norm_grad_kernel(grad_ref, value_ref, raw_ref, scale_ref, mean_ref, out_ref):
@@ -804,11 +794,12 @@
             out_ref[part, slot, :, 4 * HEAD :] = value_ref[part, slot]
 
 
-def visible_of(place):
-    row = lax.broadcasted_iota(jnp.int32, (QUERIES, WINDOW), 0)
-    column = lax.broadcasted_iota(jnp.int32, (QUERIES, WINDOW), 1)
+def visible_of(seen):
+    shape = (seen.shape[0], DOC_LEN + seen.shape[0])
+    row = lax.broadcasted_iota(jnp.int32, shape, 0)
+    column = lax.broadcasted_iota(jnp.int32, shape, 1)
     distance = row - column + DOC_LEN
-    return (distance >= 0) & (distance <= place)
+    return (distance >= 0) & (distance <= seen)
 
 
 def dot_last(left, right):
@@ -843,20 +834,22 @@
     fill(place, message_ref, keys, values)
 
     def step(number, carry):
-        sources, slot = pl.ds(2 * (number // LINE), 2), number % LINE
-        block, start = stream_row(place, 2 * (number // LINE), slot)
-        rows = pl.ds(start, WINDOW)
-        query = message_ref[sources, slot].reshape(QUERIES, HEAD)
+        count, rows_of = 2, 2 * ROWS
+        first, slot = count * (number // LINE), number % LINE
+        sources = pl.ds(first, count)
+        block, start = stream_row(place, first, slot)
+        rows = pl.ds(start, DOC_LEN + rows_of)
+        query = message_ref[sources, slot].reshape(rows_of, HEAD)
         scores = dot_last(query, keys[rows, :]) * SCALING
-        seen = pos_ref[pl.ds(block, 2)].reshape(QUERIES, 1)
+        seen = pos_ref[pl.ds(block, count)].reshape(rows_of, 1)
         masked = jnp.where(visible_of(seen), scores, -jnp.inf)
         top = jnp.max(masked, axis=-1, keepdims=True)
         expo = jnp.exp(masked - top)
         total = jnp.sum(expo, axis=-1, keepdims=True)
-        probs = (expo / total).astype(jnp.bfloat16)
+        probs = (expo * (1.0 / total)).astype(jnp.bfloat16)
         mixed = jnp.dot(probs, values[rows, :], preferred_element_type=jnp.float32)
-        o_ref[sources, slot] = mixed.astype(jnp.bfloat16).reshape(2, ROWS, HEAD)
-        lse_ref[pl.ds(2 * number, 2)] = (top + jnp.log(total)).reshape(2, ROWS, 1)
+        o_ref[sources, slot] = mixed.astype(jnp.bfloat16).reshape(count, ROWS, HEAD)
+        lse_ref[pl.ds(block, count)] = (top + jnp.log(total)).reshape(count, ROWS, 1)
         return carry
 
     lax.fori_loop(0, BLOCKS // 2, step, 0)
@@ -871,26 +864,28 @@
     d_values[...] = jnp.zeros_like(d_values)
 
     def step(number, carry):
-        sources, slot = pl.ds(2 * (number // LINE), 2), number % LINE
-        block, start = stream_row(place, 2 * (number // LINE), slot)
-        rows = pl.ds(start, WINDOW)
-        query = message_ref[sources, slot].reshape(QUERIES, HEAD)
-        grad = do_ref[sources, slot].reshape(QUERIES, HEAD)
+        count, rows_of = 4, 4 * ROWS
+        first, slot = count * (number // LINE), number % LINE
+        sources = pl.ds(first, count)
+        block, start = stream_row(place, first, slot)
+        rows = pl.ds(start, DOC_LEN + rows_of)
+        query = message_ref[sources, slot].reshape(rows_of, HEAD)
+        grad = do_ref[sources, slot].reshape(rows_of, HEAD)
         key, value = keys[rows, :], values[rows, :]
         scores = dot_last(query, key) * SCALING
-        seen = pos_ref[pl.ds(block, 2)].reshape(QUERIES, 1)
-        lse = lse_ref[pl.ds(2 * number, 2)].reshape(QUERIES, 1)
+        seen = pos_ref[pl.ds(block, count)].reshape(rows_of, 1)
+        lse = lse_ref[pl.ds(block, count)].reshape(rows_of, 1)
         probs = jnp.where(visible_of(seen), jnp.exp(scores - lse), 0.0)
         d_probs = dot_last(grad, value)
         inner = jnp.sum(probs * d_probs, axis=-1, keepdims=True)
         d_scores = (probs * (d_probs - inner) * SCALING).astype(jnp.bfloat16)
         d_query = jnp.dot(d_scores, key, preferred_element_type=jnp.float32)
-        out_ref[sources, slot] = d_query.astype(jnp.bfloat16).reshape(2, ROWS, HEAD)
+        out_ref[sources, slot] = d_query.astype(jnp.bfloat16).reshape(count, ROWS, HEAD)
         d_keys[rows, :] += along_first(d_scores, query)
         d_values[rows, :] += along_first(probs.astype(jnp.bfloat16), grad)
         return carry
 
-    lax.fori_loop(0, BLOCKS // 2, step, 0)
+    lax.fori_loop(0, BLOCKS // 4, step, 0)
     for source in range(SQUARE):
         for slot in range(LINE):
             _, start = stream_row(place, source, slot)
@@ -1109,9 +1104,17 @@
     cot = cotangent.astype(f32)
     scaled = cot * gains[3]
     d_mlp = mlp_scale * scaled - mlp * mlp_scale**3 * jnp.mean(mlp * scaled, axis=-1, keepdims=True)
-    d_mlp = both_cores(alone(gather_line(d_mlp.astype(bf16))))
-    output = (hidden_state + mlp * mlp_scale * gains[3]).astype(bf16)
-    mlp_gain_part = jnp.sum(cot * mlp * mlp_scale, axis=0)
+
+    def finished(given):
+        cotangent, hidden_state, mlp, mlp_scale = given
+        normed = mlp * mlp_scale
+        output = (hidden_state + normed * gains[3]).astype(bf16)
+        return output, jnp.sum(cotangent.astype(f32) * normed, axis=0)
+
+    d_mlp, (output, mlp_gain_part) = run(
+        gather_line(d_mlp.astype(bf16)), one((cotangent, hidden_state, mlp, mlp_scale), finished)
+    )
+    d_mlp = both_cores(d_mlp)
 
     d_both = gated_grad(along_last(d_mlp, down_w), both)
 
@@ -1125,25 +1128,23 @@
     carried, hidden_split = region(d_state_begun, total, state, d_both)
     hidden_came = sum_first(hidden_split)
 
-    def d_branch_begun(total, carried, active, d_mlp):
+    def d_branch_begun(total, carried):
         d_resid = cotangent.astype(f32) + alone(scatter_second(total, *carried))
         scaled = d_resid * gains[2]
         d_branch = branch_scale * scaled - branch * branch_scale**3 * jnp.mean(
             branch * scaled, axis=-1, keepdims=True
         )
-        attn_gain_part = jnp.sum(d_resid * branch * branch_scale, axis=0)
-        norms = jnp.stack([attn_gain_part, mlp_gain_part])
-        down_grad = along_first(active, d_mlp).astype(bf16).reshape(SQUARE, -1, width)
-        return d_resid, alone(gather_first(d_branch.astype(bf16))), norms, down_grad
-
-    def d_branch_of(d_branch):
+        return d_resid, alone(gather_first(d_branch.astype(bf16)))
+
+    def d_branch_of(d_branch, d_resid):
         d_branch = (d_branch, swap_core(d_branch))
-        return d_branch, jnp.stack([along_last(part, out_w).astype(bf16) for part in d_branch])
-
-    d_resid, d_branch, norms, down_grad = region(d_branch_begun, total, carried, active, d_mlp)
+        norms = jnp.stack([jnp.sum(d_resid * branch * branch_scale, axis=0), mlp_gain_part])
+        return d_branch, jnp.stack([along_last(part, out_w).astype(bf16) for part in d_branch]), norms
+
+    d_resid, d_branch = region(d_branch_begun, total, carried)
     d_branch, hidden_came = together(d_branch, hidden_came)
     hidden_kept, hidden_came = sum_second(hidden_split, hidden_came)
-    d_branch, d_mixed = region(d_branch_of, alone(gather_second(*d_branch)))
+    d_branch, d_mixed, norms = region(d_branch_of, alone(gather_second(*d_branch)), d_resid)
     d_mixed, hidden_came = together(d_mixed, hidden_came)
     hidden_grad = sum_end(hidden_kept, hidden_came)
     line_came = [
@@ -1151,10 +1152,11 @@
         for k in range(1, LINE)
     ]
 
-    def attended_back(d_mixed, message, lse, d_branch, mixed, down_grad, raw, scales, *tables):
+    def attended_back(d_mixed, message, lse, d_branch, mixed, active, d_mlp, raw, scales, *tables):
         grad = whole_call(pack_grad_kernel, [heads_shape], [core_ref], [d_mixed.reshape(shape)])
         grads = attend_back(place_ref, message, query_places, lse, turn_square(grad))
         grads = turn_square(grads)
+        down_grad = along_first(active, d_mlp).astype(bf16).reshape(SQUARE, -1, width)
         out_grad = sum(along_first(*pair) for pair in zip(parts_of(mixed), d_branch))
         out_grad = out_grad.reshape(1, 2, ROWS, width)
         out_grad = jnp.where(core == jnp.arange(2).reshape(2, 1, 1, 1), out_grad, 0.0).astype(bf16)
@@ -1170,13 +1172,12 @@
                 shapes,
                 [core_ref, place_ref],
                 [grads, raw, scales, *tables],
-                [pltpu.VMEM(shape, f32)] * 2,
             ),
             sum_split(from_corner, out_grad.reshape(SQUARE, ROWS, width), down_grad),
         )
 
     (d_head, d_value, sums, head_part), rows_split = region(
-        attended_back, d_mixed, message, lse, d_branch, mixed, down_grad, raw, scales, *tables
+        attended_back, d_mixed, message, lse, d_branch, mixed, active, d_mlp, raw, scales, *tables
     )
     d_head, sums, line_came = together(d_head, sums, line_came)
     hidden_grad, _ = turned_line(place_ref, hidden_grad, line_came)
@@ -1194,9 +1195,8 @@
         (came,) = yield [(both, swap_core)]
         return both + came
 
-    def gains_over(bit, value):
-        (came,) = yield [(value, along(bit))]
-        return value + came
+    def gains_to(bit):
+        return lambda value: value + swap(value, bit)
 
     def d_qkv_of(sums, head_part, norms, d_head, d_value, raw, scales, *x_parts):
         sums, gain_grads, x_all = run(
@@ -1224,53 +1224,62 @@
         came = yield [(first, along(X)), (second, along(Y))]
         return sum_end(kept, came)
 
-    def inputs_begun(total, split, hidden_grad, hidden_other):
+    def inputs_begun(total, split, hidden_grad, hidden_other, rows_split, rows_came):
         hidden_grads = spread_columns(core_ref, slot_places, hidden_grad, hidden_other, 2, SQUARE)
-        return run(scatter_first(total), first_track(split)), hidden_grads
-
-    (carried, qkv_came), (gate_grad, up_grad) = region(
-        inputs_begun, total, qkv_split, hidden_grad, hidden_other
+        rows_grads = sum_later(rows_split, rows_came)
+        return run(scatter_first(total), first_track(split)), hidden_grads, rows_grads
+
+    (carried, qkv_came), (gate_grad, up_grad), rows_grads = region(
+        inputs_begun, total, qkv_split, hidden_grad, hidden_other, rows_split, rows_grads_came
     )
     def inputs_ended(total, *carried):
         return d_resid + (yield from scatter_second(total, *carried))
 
-    input_grad, qkv_grad, gain_grads = region(
-        lambda total, carried, split, came, norms: run(
-            inputs_ended(total, *carried), later_track(split, came), gains_over(X, norms)
+    input_grad, qkv_grad = region(
+        lambda total, carried, split, came: (
+            alone(inputs_ended(total, *carried)),
+            alone(later_track(split, came)),
         ),
         total,
         carried,
         qkv_split,
         qkv_came,
-        gain_grads,
-    )
-    qkv_grad, rows_grad = run(one(qkv_grad, turn_line), later_track(rows_split, rows_grads_came))
-    qkv_other, rows_other, gain_grads = run(
-        one(qkv_grad, swap_core), one(rows_grad[0], swap_core), gains_over(Y, gain_grads)
-    )
-    out_grad, down_grad = rows_grad[0, :ROWS], rows_grad[0, ROWS:]
-    out_other, down_other = rows_other[:ROWS], rows_other[ROWS:]
+    )
+    qkv_grad = turn_line(qkv_grad)
+
+    def rows_ended(kept, sent, gain_grads):
+        *came, gain_grads = yield [(sent[0], along(X)), (sent[1], along(Y)), (gain_grads, gains_to(X))]
+        mine = jnp.concatenate([add_low(*pair) for pair in zip(kept, came)], axis=-1)[0]
+        other, gain_grads = yield [(mine, swap_core), (gain_grads, gains_to(Y))]
+        out_grad = mine[:ROWS].astype(f32) + other[:ROWS].astype(f32)
+        mine, other = mine[ROWS:], other[ROWS:]
+        down_grad = jnp.concatenate([jnp.where(core, other, mine), jnp.where(core, mine, other)])
+        return out_grad, down_grad.astype(f32), gain_grads
+
+    rows_grads, gain_grads = hold((rows_grads, gain_grads), input_grad)
+    out_grad, down_grad, gain_grads = region(
+        lambda grads, gains: alone(rows_ended(*grads, gains)), rows_grads, gain_grads
+    )
+    qkv_grad, out_grad = together(qkv_grad, out_grad)
+    qkv_other = swap_core(qkv_grad)
     norms, head_grads = (
         lax.dynamic_index_in_dim(part.reshape(2, -1, ROWS), number, 1, keepdims=False)
         for part, number in ((gain_grads[: 2 * BLOCKS], shard_index), (gain_grads[2 * BLOCKS :], corner))
     )
     query_grad, key_grad, value_grad = spread_columns(core_ref, slots, qkv_grad, qkv_other, 3, 1)
-    down_grad = jnp.concatenate(
-        [jnp.where(core, down_other, down_grad), jnp.where(core, down_grad, down_other)]
-    )
     return (
         output,
         input_grad,
         query_grad,
         key_grad,
         value_grad,
-        out_grad.astype(f32) + out_other.astype(f32),
+        out_grad,
         head_grads[0],
         head_grads[1],
         norms[0],
         gate_grad,
         up_grad,
-        down_grad.astype(f32),
+        down_grad,
         norms[1],
     )
 

time: 820 us -> 809 us (0.987)
    ppermute x32, waiting for transfers between devices: 57.4 us -> 66.1 us  [swap(): lax.ppermute(value, 'shard', [(source, source ^ bit) for source in range(...]
    unnamed x138 -> x118, local copies, waits for them, and re-layouts: 30 us -> 21.6 us
    pallas_call x37 -> x36, Pallas kernels: 128 us -> 127 us  [whole_call(): pl.pallas_call(kernel, out_shape=shapes[0] if single else shapes, in_spec...]
  transfers between devices with their start and end apart: 99 -> 99, of which waited for: 49 -> 52; matrix products, arithmetic and copies ran while one was open for 14% -> 15% of each run, Pallas kernels for 13% -> 13%
where the time goes in v5:
time: 809 us; the launch traced here: 797 us
  waiting for transfers between devices  292 us (36%)
  starting transfers between devices  167 us (21%)
  Pallas kernels  131 us (16%)
  matrix products  87.8 us (11%)
  other arithmetic  59.1 us (7%)
  local copies, waits for them, and re-layouts  55.3 us (7%)
    ppermute x40, waiting for transfers between devices, line_move(): return lambda value: lax.ppermute(value, 'shard', pairs)  176 us
    pallas_call x36, Pallas kernels, whole_call(): pl.pallas_call(kernel, out_shape=shapes[0] if single else shapes, in_spec...  127 us
    ppermute x40, starting transfers between devices, line_move(): return lambda value: lax.ppermute(value, 'shard', pairs)  97.3 us
    ppermute x32, waiting for transfers between devices, swap(): lax.ppermute(value, 'shard', [(source, source ^ bit) for source in range(...  66.1 us
    all_to_all x4, waiting for transfers between devices, turn_square(): lax.all_to_all(message, 'shard', 0, 0, tiled=True, axis_index_groups=SQUA...  41.1 us
    dot_general x8, matrix products, dot(): return jnp.dot(left, right, preferred_element_type=f32)  34.7 us
    ppermute x32, starting transfers between devices, swap(): lax.ppermute(value, 'shard', [(source, source ^ bit) for source in range(...  33 us
    dot_general x7, matrix products, along_last(): lax.dot_general(left, right, (((1,), (1,)), ((), ())), preferred_element_...  27.4 us
  transfers between devices with their start and end apart: 99, of which 52 were waited for; matrix products, arithmetic and copies ran while one was open for 15% of the time, Pallas kernels for 13%

profile of v5, /device:TPU:0, one launch (start us, length us, event | category | flops | bytes accessed | tf_op | source)
XLA Modules:
  0.0 797.3 jit_solution(2638622715428448127)
XLA Ops:
  15.2 16.2 %collective-permute-done.43.first_ref = bf16[1,384,1024]{2,1,0:T(8,128)(2,1)S(1)} collective-permute-done((bf16[1,384,1024]{2,1,0:T(8,128)(2,1)}, bf16[1,384,1024]{2,1,0:T(8,128)(2,1)S(1)}, u32[]{:S(2)}, u32[]{:S(2)}) %collective-permute-start.43) | collective-permute-done | bytes 786464 | tf_op jit(solution)/shard_map/ppermute | solution.py:286
  79.4 9.2 %collective-permute-done.51.further_ref = bf16[128,2048]{1,0:T(8,128)(2,1)} collective-permute-done((bf16[128,2048]{1,0:T(8,128)(2,1)}, bf16[128,2048]{1,0:T(8,128)(2,1)}, u32[]{:S(2)}, u32[]{:S(2)}) %collective-permute-start.51) | collective-permute-done | bytes 524320 | tf_op jit(solution)/shard_map/ppermute | solution.py:307
  97.3 19.9 %conditional.12 = (bf16[512,2048]{1,0:T(8,128)(2,1)}, f32[2,4,128,768]{3,2,1,0:T(8,128)}, f32[4,2,2,128]{3,2,1,0:T(2,128)S(1)}, f32[2,4,128,128]{3,2,1,0:T(8,128)S(1)}, f32[2,4,128,128]{3,2,1,0:T(8,128)S(1)}) conditional(s32[]{:T(128)} %bitcast.43, () %tuple.169, (bf16[512,2048]{1,0:T(8,128)(2,1)}, bf16[2048,768]{1,0:T(8,128)(2,1)}, ...), branch_computations={%region_0.1_spmd, %region_1.4_spmd} | conditional | flops 3223876096 | bytes 49536476 | solution.py:976
  127.9 61.5 %conditional.13 = (bf16[4,16,128,128]{3,2,1,0:T(8,128)(2,1)}, f32[16,128,1]{2,1,0:T(8,128)}, bf16[1024,256]{1,0:T(8,128)(2,1)}, bf16[4,384,2048]{2,1,0:T(8,128)(2,1)}) conditional(s32[]{:T(128)} %bitcast.43, () %tuple.168, (s32[1]{0:T(128)}, s32[1]{0:T(128)}, f32[2,4,128,768]{3,2,1,0:T(8,128)}, f32[2,2,4,128,1]{3,2,1,0,4:T(4,128)S(1)}, ...), branch_computations={%region_4.5_spmd, %region_5.6_spmd} | conditional | bytes 48828624 | solution.py:976
  141.2 24.4 %all-to-all-done.message_ref = bf16[4,16,128,128]{3,2,1,0:T(8,128)(2,1)} async-done(((bf16[4,16,128,128]{3,2,1,0:T(8,128)(2,1)}), bf16[4,16,128,128]{3,2,1,0:T(8,128)(2,1)}, u32[]{:S(2)}, u32[]{:S(2)}) %all-to-all-start) | async-done | bytes 2097184 | tf_op jit(solution)/shard_map/cond/branch_1_fun/all_to_all | solution.py:919
  165.7 11.1 %branch_1_fun.18 = (bf16[4,4,128,128]{3,2,1,0:T(8,128)(2,1)S(1)}, f32[16,128,1]{2,1,0:T(8,128)}) custom-call(s32[1]{0:T(128)} %get-tuple-element.232.place_ref, bf16[4,16,128,128]{3,2,1,0:T(8,128)(2,1)} %all-to-all-done.message_ref, s32[16,128,1]{2,1,0:T(8,128)S(1)} %copy.48.pos_ref), custom_call_target="tpu_custom_call" | custom-call | bytes 4210688 | tf_op jit(solution)/shard_map/cond/branch_1_fun/pallas_call | solution.py:590
  201.4 51.4 %conditional.14 = (f32[128,2048]{1,0:T(8,128)}, bf16[1024,2048]{1,0:T(8,128)(2,1)}) conditional(s32[]{:T(128)} %bitcast.43, () %tuple.167, (bf16[512,2048]{1,0:T(8,128)(2,1)}, bf16[4,384,2048]{2,1,0:T(8,128)(2,1)}) %tuple.181), branch_computations={%region_6.7_spmd, %region_7.8_spmd} | conditional | flops 5242900 | bytes 27787680 | solution.py:976
  217.8 10.5 %collective-permute-done.2 = bf16[128,2048]{1,0:T(8,128)(2,1)} collective-permute-done((bf16[128,2048]{1,0:T(8,128)(2,1)}, bf16[128,2048]{1,0:T(8,128)(2,1)}, u32[]{:S(2)}, u32[]{:S(2)}) %collective-permute-start.2) | collective-permute-done | bytes 524320 | tf_op jit(solution)/shard_map/cond/branch_1_fun/ppermute | solution.py:307
  258.5 50.0 %conditional.15 = (f32[128,1]{0,1:T(1,128)S(1)}, f32[128,2048]{1,0:T(8,128)}, bf16[512,2048]{1,0:T(8,128)(2,1)}) conditional(s32[]{:T(128)} %bitcast.43, () %tuple.166, (f32[128,2048]{1,0:T(8,128)}, bf16[128,2048]{1,0:T(8,128)(2,1)S(1)}, f32[4,2048]{1,0:T(4,128)S(1)}) %tuple.313), branch_computations={%region_8.9_spmd, %region_9.11_spmd} | conditional | flops 2097298 | bytes 22571924 | solution.py:976
  282.9 13.2 %collective-permute-done.22.lefts_ref = bf16[128,2048]{1,0:T(8,128)(2,1)S(1)} collective-permute-done((bf16[128,2048]{1,0:T(8,128)(2,1)}, bf16[128,2048]{1,0:T(8,128)(2,1)S(1)}, u32[]{:S(2)}, u32[]{:S(2)}) %collective-permute-start.22) | collective-permute-done | bytes 524320 | tf_op jit(solution)/shard_map/cond/branch_1_fun/ppermute | solution.py:307
  412.8 13.8 %collective-permute-done.75.lefts_ref = bf16[128,2048]{1,0:T(8,128)(2,1)S(1)} collective-permute-done((bf16[128,2048]{1,0:T(8,128)(2,1)S(1)}, bf16[128,2048]{1,0:T(8,128)(2,1)S(1)}, u32[]{:S(2)}, u32[]{:S(2)}) %collective-permute-start.75) | collective-permute-done | bytes 524320 | tf_op jit(solution)/shard_map/ppermute | solution.py:307
  426.6 9.8 %collective-permute-done.76.further_ref = bf16[128,2048]{1,0:T(8,128)(2,1)S(1)} collective-permute-done((bf16[128,2048]{1,0:T(8,128)(2,1)S(1)}, bf16[128,2048]{1,0:T(8,128)(2,1)S(1)}, u32[]{:S(2)}, u32[]{:S(2)}) %collective-permute-start.76) | collective-permute-done | bytes 524320 | tf_op jit(solution)/shard_map/ppermute | solution.py:307
  468.8 25.0 %conditional.16 = (bf16[128,2048]{1,0:T(8,128)(2,1)}, bf16[128,2048]{1,0:T(8,128)(2,1)}, bf16[128,2048]{1,0:T(8,128)(2,1)}, bf16[2,4,128,1024]{3,2,1,0:T(8,128)(...) conditional(s32[]{:T(128)} %bitcast.43, () %tuple.198, ...), branch_computations={%region_14.15_spmd, %region_15.16_spmd} | conditional | flops 8594391040 | bytes 42467684 | solution.py:976
  477.4 12.0 %convolution_convert_fusion = bf16[2048,2048]{1,0:T(8,128)(2,1)S(1)} fusion(bf16[1024,2048]{1,0:T(8,128)(2,1)} %get-tuple-element.280, bf16[1024,2048]{1,0:T(8,128)(2,1)} %get-tuple-element.281), kind=kOutput, calls=%fused_computation.35 | convolution fusion | flops 8594128896 | bytes 16777216 | tf_op jit(solution)/shard_map/cond/branch_1_fun/dot_general | solution.py:51
  495.8 44.0 %conditional.17 = (f32[128,2048]{1,0:T(8,128)}, bf16[128,2048]{1,0:T(8,128)(2,1)}, bf16[128,2048]{1,0:T(8,128)(2,1)}, bf16[128,2048]{1,0:T(8,128)(2,1)}) conditional(s32[]{:T(128)} %bitcast.43, () %tuple.195, (bf16[128,2048]{1,0:T(8,128)(2,1)S(1)}, bf16[512,2048]{1,0:T(8,128)(2,1)}, bf16[128,2048]{1,0:T(8,128)(2,1)}, bf16[128,2048]{1,0:T(8,128)(2,1)}, ...), branch_computations={%region_16.17_spmd, %region_17.19_spmd} | conditional | flops 7864595 | bytes 18911614 | solution.py:976
  553.6 16.7 %collective-permute-done.82.lefts_ref = bf16[128,2048]{1,0:T(8,128)(2,1)S(1)} collective-permute-done((bf16[128,2048]{1,0:T(8,128)(2,1)}, bf16[128,2048]{1,0:T(8,128)(2,1)S(1)}, u32[]{:S(2)}, u32[]{:S(2)}) %collective-permute-start.82) | collective-permute-done | bytes 524320 | tf_op jit(solution)/shard_map/ppermute | solution.py:307
  570.3 10.2 %collective-permute-done.83.further_ref = bf16[128,2048]{1,0:T(8,128)(2,1)S(1)} collective-permute-done((bf16[128,2048]{1,0:T(8,128)(2,1)S(1)}, bf16[128,2048]{1,0:T(8,128)(2,1)S(1)}, u32[]{:S(2)}, u32[]{:S(2)}) %collective-permute-start.83) | collective-permute-done | bytes 524320 | tf_op jit(solution)/shard_map/ppermute | solution.py:307
  598.6 66.4 %conditional.19 = (f32[2,2,4,128,256]{4,3,2,1,0:T(8,128)}, bf16[2,4,128,256]{3,2,1,0:T(8,128)(2,1)}, f32[2,2,4,128,1]{4,3,2,1,0:T(8,128)}, f32[2,256]{1,0:T(2,12...) conditional(s32[]{:T(128)} %bitcast.43, () %tuple.193, ...), branch_computations={%region_22.23_spmd, %region_23.24_spmd} | conditional | flops 5372903424 | bytes 96588040 | solution.py:976
  613.0 13.7 %branch_1_fun.24 = bf16[4,16,128,128]{3,2,1,0:T(8,128)(2,1)S(1)} custom-call(s32[1]{0:T(128)} %get-tuple-element.309.place_ref, bf16[4,16,128,128]{3,2,1,0:T(8,128)(2,1)} %get-tuple-element.310.message_ref, s32[16,128,1]{2,1,0:T(8,128)S(1)} %copy-done.13, f32[16,128,1]{2,1,0:T(8,128)} %get-tuple-element.312.lse_ref, ...), custom_call_target="tpu_custom_call" | custom-call | bytes 5275648 | tf_op jit(solution)/shard_map/cond/branch_1_fun/pallas_call | solution.py:590
  670.6 35.5 %conditional.20 = (bf16[512,2048]{1,0:T(8,128)(2,1)S(1)}, bf16[2,4,128,384]{3,2,1,0:T(8,128)(2,1)}, bf16[2,4,128,384]{3,2,1,0:T(8,128)(2,1)}, bf16[2,4,128,384]{...) conditional(s32[]{:T(128)} %bitcast.43, () %tuple.192, ...), branch_computations={%region_24.25_spmd, %region_25.26_spmd} | conditional | flops 6450374656 | bytes 111975696 | solution.py:976
  707.4 26.4 %conditional.21 = (bf16[128,2048]{1,0:T(8,128)(2,1)}, bf16[128,2048]{1,0:T(8,128)(2,1)}, bf16[128,2048]{1,0:T(8,128)(2,1)}, bf16[2,4,128,384]{3,2,1,0:T(8,128)(2...) conditional(s32[]{:T(128)} %bitcast.43, () %tuple.210, ...), branch_computations={%region_26.27_spmd, %region_27.28_spmd} | conditional | flops 262182 | bytes 36176388 | solution.py:976
  733.9 25.7 %conditional.22 = (f32[128,2048]{1,0:T(8,128)S(1)}, bf16[4,128,768]{2,1,0:T(8,128)(2,1)S(1)}) conditional(s32[]{:T(128)} %bitcast.43, () %tuple.191, (bf16[512,2048]{1,0:T(8,128)(2,1)}, bf16[128,2048]{1,0:T(8,128)(2,1)}, bf16[128,2048]{1,0:T(8,128)(2,1)}, bf16[128,2048]{1,0:T(8,128)(2,1)}, f32[128,2048]{1,0:T(8,128)}, ...), branch_computations={%region_28.29_spmd, %region_29.30_spmd} | conditional | flops 5242899 | bytes 24117614 | solution.py:976
  764.1 27.4 %conditional.23 = (f32[128,2048]{1,0:T(8,128)}, f32[512,2048]{1,0:T(8,128)}, f32[40,128]{1,0:T(8,128)S(1)}) conditional(s32[]{:T(128)} %bitcast.43, () %tuple.213, (bf16[1,384,1024]{2,1,0:T(8,128)(2,1)}, bf16[1,384,1024]{2,1,0:T(8,128)(2,1)}, bf16[1,384,1024]{2,1,0:T(8,128)(2,1)}, f32[40,128]{1,0:T(8,128)S(1)}, bf16[1,384,1024]{2,1,0:T(8,128)(2,1)}, ...), branch_computations={%region_30.31_spmd, %region_31.32_spmd} | conditional | flops 17573888 | bytes 34889952 | solution.py:976
  767.3 13.2 %collective-permute-done.16 = f32[40,128]{1,0:T(8,128)S(1)} collective-permute-done((f32[40,128]{1,0:T(8,128)S(1)}, f32[40,128]{1,0:T(8,128)S(1)}, u32[]{:S(2)}, u32[]{:S(2)}) %collective-permute-start.16) | collective-permute-done | bytes 20512 | tf_op jit(solution)/shard_map/cond/branch_1_fun/ppermute | solution.py:286
  (518 shorter events, 625.2 us)
Async XLA Ops:
  5.7 28.7 %all-to-all-start.4 = ((bf16[4,144,768]{2,1,0:T(8,128)(2,1)}), bf16[4,144,768]{2,1,0:T(8,128)(2,1)S(1)}, u32[]{:S(2)}, u32[]{:S(2)}) async-start(bf16[4,144,768]{2,1,0:T(8,128)(2,1)} %shard_map.237), calls=%async_computation.4 | async-start | bytes 1769472 | tf_op jit(solution)/shard_map/all_to_all | solution.py:450
  57.1 31.5 %collective-permute-start.52 = (bf16[2,4,144,384]{3,2,1,0:T(8,128)(2,1)}, bf16[2,4,144,384]{3,2,1,0:T(8,128)(2,1)}, u32[]{:S(2)}, u32[]{:S(2)}) collective-permute-start(bf16[2,4,144,384]{3,2,1,0:T(8,128)(2,1)} %get-tuple-element.646), channel_id=1, source_target_pairs={{0,2},{1,3},{2,0},{3,1},{4,6},{5,7},{6,4},{7,5},{8,10},{9,11},{10,... | collective-permute-start | bytes 2654216 | tf_op jit(solution)/shard_map/ppermute | solution.py:286
  58.6 30.0 %collective-permute-start.53 = (bf16[2,4,144,384]{3,2,1,0:T(8,128)(2,1)}, bf16[2,4,144,384]{3,2,1,0:T(8,128)(2,1)}, u32[]{:S(2)}, u32[]{:S(2)}) collective-permute-start(bf16[2,4,144,384]{3,2,1,0:T(8,128)(2,1)} %get-tuple-element.647), channel_id=1, source_target_pairs={{0,1},{1,0},{2,3},{3,2},{4,5},{5,4},{6,7},{7,6},{8,9},{9,8},{10,11... | collective-permute-start | bytes 2654216 | tf_op jit(solution)/shard_map/ppermute | solution.py:286
  90.5 37.1 %collective-permute-start.55 = (bf16[2,1,384,1024]{3,2,1,0:T(8,128)(2,1)}, bf16[2,1,384,1024]{3,2,1,0:T(8,128)(2,1)}, u32[]{:S(2)}, u32[]{:S(2)}) collective-permute-start(bf16[2,1,384,1024]{3,2,1,0:T(8,128)(2,1)} %get-tuple-element.659), channel_id=1, source_target_pairs={{0,2},{1,3},{2,0},{3,1},{4,6},{5,7},{6,4},{7,5},{8,10},{9,11},{10,... | collective-permute-start | bytes 4718600 | tf_op jit(solution)/shard_map/ppermute | solution.py:286
  91.1 36.8 %collective-permute-start.56 = (bf16[2,1,384,1024]{3,2,1,0:T(8,128)(2,1)}, bf16[2,1,384,1024]{3,2,1,0:T(8,128)(2,1)}, u32[]{:S(2)}, u32[]{:S(2)}) collective-permute-start(bf16[2,1,384,1024]{3,2,1,0:T(8,128)(2,1)} %get-tuple-element.660), channel_id=1, source_target_pairs={{0,1},{1,0},{2,3},{3,2},{4,5},{5,4},{6,7},{7,6},{8,9},{9,8},{10,11... | collective-permute-start | bytes 4718600 | tf_op jit(solution)/shard_map/ppermute | solution.py:286
  118.6 70.8 %collective-permute-start.57 = (bf16[128,2048]{1,0:T(8,128)(2,1)}, bf16[128,2048]{1,0:T(8,128)(2,1)}, u32[]{:S(2)}, u32[]{:S(2)}) collective-permute-start(bf16[128,2048]{1,0:T(8,128)(2,1)} %get-tuple-element.1002), channel_id=1, source_target_pairs={{0,4},{1,5},{2,6},{3,7},{4,8},{5,9},{6,10},{7,11},{8,12},{9,13},{1... | collective-permute-start | bytes 1572872 | tf_op jit(solution)/shard_map/ppermute | solution.py:315
  118.7 70.8 %collective-permute-start.58 = (bf16[128,2048]{1,0:T(8,128)(2,1)}, bf16[128,2048]{1,0:T(8,128)(2,1)}, u32[]{:S(2)}, u32[]{:S(2)}) collective-permute-start(bf16[128,2048]{1,0:T(8,128)(2,1)} %get-tuple-element.1001), channel_id=1, source_target_pairs={{0,8},{1,9},{2,10},{3,11},{4,12},{5,13},{6,14},{7,15},{8,0},{9,1},... | collective-permute-start | bytes 1572872 | tf_op jit(solution)/shard_map/ppermute | solution.py:315
  118.9 70.5 %collective-permute-start.59 = (bf16[128,2048]{1,0:T(8,128)(2,1)}, bf16[128,2048]{1,0:T(8,128)(2,1)}, u32[]{:S(2)}, u32[]{:S(2)}) collective-permute-start(bf16[128,2048]{1,0:T(8,128)(2,1)} %get-tuple-element.1000), channel_id=1, source_target_pairs={{0,12},{1,13},{2,14},{3,15},{4,0},{5,1},{6,2},{7,3},{8,4},{9,5},{1... | collective-permute-start | bytes 1572872 | tf_op jit(solution)/shard_map/ppermute | solution.py:315
  136.4 29.3 %all-to-all-start = ((bf16[4,16,128,128]{3,2,1,0:T(8,128)(2,1)}), bf16[4,16,128,128]{3,2,1,0:T(8,128)(2,1)}, u32[]{:S(2)}, u32[]{:S(2)}) async-start(bf16[4,16,128,128]{3,2,1,0:T(8,128)(2,1)} %copy-done.8), calls=%async_computation | async-start | bytes 4194304 | tf_op jit(solution)/shard_map/cond/branch_1_fun/all_to_all | solution.py:919
  195.5 57.3 %collective-permute-start.61 = (bf16[4,128,1024]{2,1,0:T(8,128)(2,1)}, bf16[4,128,1024]{2,1,0:T(8,128)(2,1)S(1)}, u32[]{:S(2)}, u32[]{:S(2)}) collective-permute-start(bf16[4,128,1024]{2,1,0:T(8,128)(2,1)} %get-tuple-element.675), channel_id=1, source_target_pairs={{0,1},{1,0},{2,3},{3,2},{4,5},{5,4},{6,7},{7,6},{8,9},{9,8},{10,11... | collective-permute-start | bytes 3145736 | tf_op jit(solution)/shard_map/ppermute | solution.py:286
  196.9 55.9 %collective-permute-start.62 = (bf16[4,128,1024]{2,1,0:T(8,128)(2,1)}, bf16[4,128,1024]{2,1,0:T(8,128)(2,1)}, u32[]{:S(2)}, u32[]{:S(2)}) collective-permute-start(bf16[4,128,1024]{2,1,0:T(8,128)(2,1)} %get-tuple-element.676), channel_id=1, source_target_pairs={{0,2},{1,3},{2,0},{3,1},{4,6},{5,7},{6,4},{7,5},{8,10},{9,11},{10,... | collective-permute-start | bytes 3145736 | tf_op jit(solution)/shard_map/ppermute | solution.py:286
  256.4 52.1 %collective-permute-start.63 = (bf16[2,4,128,1024]{3,2,1,0:T(8,128)(2,1)}, bf16[2,4,128,1024]{3,2,1,0:T(8,128)(2,1)}, u32[]{:S(2)}, u32[]{:S(2)}) collective-permute-start(bf16[2,4,128,1024]{3,2,1,0:T(8,128)(2,1)} %get-tuple-element.682), channel_id=1, source_target_pairs={{0,2},{1,3},{2,0},{3,1},{4,6},{5,7},{6,4},{7,5},{8,10},{9,11},{10,... | collective-permute-start | bytes 6291464 | tf_op jit(solution)/shard_map/ppermute | solution.py:286
  257.8 50.6 %collective-permute-start.64 = (bf16[2,4,128,1024]{3,2,1,0:T(8,128)(2,1)}, bf16[2,4,128,1024]{3,2,1,0:T(8,128)(2,1)}, u32[]{:S(2)}, u32[]{:S(2)}) collective-permute-start(bf16[2,4,128,1024]{3,2,1,0:T(8,128)(2,1)} %get-tuple-element.683), channel_id=1, source_target_pairs={{0,1},{1,0},{2,3},{3,2},{4,5},{5,4},{6,7},{7,6},{8,9},{9,8},{10,11... | collective-permute-start | bytes 6291464 | tf_op jit(solution)/shard_map/ppermute | solution.py:286
  493.8 47.5 %collective-permute-start.79 = (bf16[2,4,128,1024]{3,2,1,0:T(8,128)(2,1)}, bf16[2,4,128,1024]{3,2,1,0:T(8,128)(2,1)S(1)}, u32[]{:S(2)}, u32[]{:S(2)}) collective-permute-start(bf16[2,4,128,1024]{3,2,1,0:T(8,128)(2,1)} %get-tuple-element.729), channel_id=1, source_target_pairs={{0,2},{1,3},{2,0},{3,1},{4,6},{5,7},{6,4},{7,5},{8,10},{9,11},{10,... | collective-permute-start | bytes 6291464 | tf_op jit(solution)/shard_map/ppermute | solution.py:286
  495.3 47.4 %collective-permute-start.80 = (bf16[2,4,128,1024]{3,2,1,0:T(8,128)(2,1)}, bf16[2,4,128,1024]{3,2,1,0:T(8,128)(2,1)}, u32[]{:S(2)}, u32[]{:S(2)}) collective-permute-start(bf16[2,4,128,1024]{3,2,1,0:T(8,128)(2,1)} %get-tuple-element.730), channel_id=1, source_target_pairs={{0,1},{1,0},{2,3},{3,2},{4,5},{5,4},{6,7},{7,6},{8,9},{9,8},{10,11... | collective-permute-start | bytes 6291464 | tf_op jit(solution)/shard_map/ppermute | solution.py:286
  547.2 41.9 %collective-permute-start.84 = (bf16[4,128,1024]{2,1,0:T(8,128)(2,1)}, bf16[4,128,1024]{2,1,0:T(8,128)(2,1)}, u32[]{:S(2)}, u32[]{:S(2)}) collective-permute-start(bf16[4,128,1024]{2,1,0:T(8,128)(2,1)} %get-tuple-element.747), channel_id=1, source_target_pairs={{0,1},{1,0},{2,3},{3,2},{4,5},{5,4},{6,7},{7,6},{8,9},{9,8},{10,11... | collective-permute-start | bytes 3145736 | tf_op jit(solution)/shard_map/ppermute | solution.py:286
  547.7 41.4 %collective-permute-start.85 = (bf16[4,128,1024]{2,1,0:T(8,128)(2,1)}, bf16[4,128,1024]{2,1,0:T(8,128)(2,1)}, u32[]{:S(2)}, u32[]{:S(2)}) collective-permute-start(bf16[4,128,1024]{2,1,0:T(8,128)(2,1)} %get-tuple-element.748), channel_id=1, source_target_pairs={{0,2},{1,3},{2,0},{3,1},{4,6},{5,7},{6,4},{7,5},{8,10},{9,11},{10,... | collective-permute-start | bytes 3145736 | tf_op jit(solution)/shard_map/ppermute | solution.py:286
  594.8 70.3 %collective-permute-start.86 = (bf16[128,2048]{1,0:T(8,128)(2,1)}, bf16[128,2048]{1,0:T(8,128)(2,1)}, u32[]{:S(2)}, u32[]{:S(2)}) collective-permute-start(bf16[128,2048]{1,0:T(8,128)(2,1)} %get-tuple-element.997), channel_id=1, source_target_pairs={{0,4},{1,5},{2,6},{3,7},{4,8},{5,9},{6,10},{7,11},{8,12},{9,13},{1... | collective-permute-start | bytes 1572872 | tf_op jit(solution)/shard_map/ppermute | solution.py:315
  594.8 70.3 %collective-permute-start.87 = (bf16[128,2048]{1,0:T(8,128)(2,1)}, bf16[128,2048]{1,0:T(8,128)(2,1)}, u32[]{:S(2)}, u32[]{:S(2)}) collective-permute-start(bf16[128,2048]{1,0:T(8,128)(2,1)} %get-tuple-element.996), channel_id=1, source_target_pairs={{0,8},{1,9},{2,10},{3,11},{4,12},{5,13},{6,14},{7,15},{8,0},{9,1},... | collective-permute-start | bytes 1572872 | tf_op jit(solution)/shard_map/ppermute | solution.py:315
  594.8 70.3 %collective-permute-start.88 = (bf16[128,2048]{1,0:T(8,128)(2,1)}, bf16[128,2048]{1,0:T(8,128)(2,1)}, u32[]{:S(2)}, u32[]{:S(2)}) collective-permute-start(bf16[128,2048]{1,0:T(8,128)(2,1)} %get-tuple-element.995), channel_id=1, source_target_pairs={{0,12},{1,13},{2,14},{3,15},{4,0},{5,1},{6,2},{7,3},{8,4},{9,5},{1... | collective-permute-start | bytes 1572872 | tf_op jit(solution)/shard_map/ppermute | solution.py:315
  668.6 38.3 %collective-permute-start.91 = (bf16[4,128,2048]{2,1,0:T(8,128)(2,1)}, bf16[4,128,2048]{2,1,0:T(8,128)(2,1)}, u32[]{:S(2)}, u32[]{:S(2)}) collective-permute-start(bf16[4,128,2048]{2,1,0:T(8,128)(2,1)} %get-tuple-element.776), channel_id=1, source_target_pairs={{0,16},{16,0},{1,17},{17,1},{2,18},{18,2},{3,19},{19,3},{4,20},{20... | collective-permute-start | bytes 6291464 | tf_op jit(solution)/shard_map/ppermute | solution.py:290
  668.6 37.5 %collective-permute-start.89 = (bf16[2,1,384,1024]{3,2,1,0:T(8,128)(2,1)}, bf16[2,1,384,1024]{3,2,1,0:T(8,128)(2,1)}, u32[]{:S(2)}, u32[]{:S(2)}) collective-permute-start(bf16[2,1,384,1024]{3,2,1,0:T(8,128)(2,1)} %get-tuple-element.768), channel_id=1, source_target_pairs={{0,2},{1,3},{2,0},{3,1},{4,6},{5,7},{6,4},{7,5},{8,10},{9,11},{10,... | collective-permute-start | bytes 4718600 | tf_op jit(solution)/shard_map/ppermute | solution.py:286
  670.1 36.8 %collective-permute-start.90 = (bf16[2,1,384,1024]{3,2,1,0:T(8,128)(2,1)}, bf16[2,1,384,1024]{3,2,1,0:T(8,128)(2,1)}, u32[]{:S(2)}, u32[]{:S(2)}) collective-permute-start(bf16[2,1,384,1024]{3,2,1,0:T(8,128)(2,1)} %get-tuple-element.769), channel_id=1, source_target_pairs={{0,1},{1,0},{2,3},{3,2},{4,5},{5,4},{6,7},{7,6},{8,9},{9,8},{10,11... | collective-permute-start | bytes 4718600 | tf_op jit(solution)/shard_map/ppermute | solution.py:286
  760.4 31.1 %all-to-all-start.5 = ((bf16[4,128,768]{2,1,0:T(8,128)(2,1)}), bf16[4,128,768]{2,1,0:T(8,128)(2,1)S(1)}, u32[]{:S(2)}, u32[]{:S(2)}) async-start(bf16[4,128,768]{2,1,0:T(8,128)(2,1)} %copy-done.47), calls=%async_computation.5 | async-start | bytes 1572864 | tf_op jit(solution)/shard_map/all_to_all | solution.py:450
  (147 other events, 1528.7 us)

commit v6 on v5

--- a/solution.py
+++ b/solution.py
@@ -1045,7 +1045,6 @@
         return x_other, raw, alone(sums_track(row_sums(sums))), jnp.cos(angles), jnp.sin(angles) * sign
 
     x_other, raw, sums, cosines, sines = region(projected, x_own, qkv_w, *held)
-    raw, rows_later = together(raw, rows_later)
     scales = lax.rsqrt(row_means(sums) + 1e-06)
 
     hidden_block = hold(pick_columns(core_ref, (w_gate, w_up), SQUARE), sums)
@@ -1060,17 +1059,16 @@
 
     tables = [head_gain, cosines, sines]
 
-    def attended(raw, scales, *tables):
-        message = whole_call(
-            pack_kernel, [message_shape], [core_ref, place_ref], [raw, scales, *tables]
-        )
+    def attended(message):
         message = turn_square(message)
         mixed, lse = attend(place_ref, message, query_places)
         mixed = whole_call(unpack_kernel, [tokens_shape], [core_ref], [turn_square(mixed)])
         rows_w = square_join(from_corner, rows_own, rows_came, rows_later)
         return message, lse, mixed.reshape(tokens, heads), rows_w
 
-    message, lse, mixed, rows_w = region(attended, raw, scales, *tables)
+    packed = whole_call(pack_kernel, [message_shape], [core_ref, place_ref], [raw, scales, *tables])
+    packed, rows_later = together(packed, rows_later)
+    message, lse, mixed, rows_w = region(attended, packed)
     mixed, line_came = together(mixed, line_came)
     out_w = lax.dynamic_slice(rows_w, (core_index * 2, 0, 0), (2, ROWS, width)).reshape(heads, width)
     hidden_own, parts = turned_line(place_ref, hidden_block, line_came)

time: 809 us -> 804 us (level)
    unnamed x118 -> x116, local copies, waits for them, and re-layouts: 21.6 us -> 20.2 us
  transfers between devices with their start and end apart: 99 -> 99, of which waited for: 52 -> 49; matrix products, arithmetic and copies ran while one was open for 15% -> 15% of each run, Pallas kernels for 13% -> 13%
where the time goes in v6:
time: 804 us; the launch traced here: 793 us
  waiting for transfers between devices  285 us (35%)
  starting transfers between devices  170 us (21%)
  Pallas kernels  132 us (16%)
  matrix products  87.8 us (11%)
  other arithmetic  61.9 us (8%)
  local copies, waits for them, and re-layouts  51 us (6%)
    ppermute x40, waiting for transfers between devices, line_move(): return lambda value: lax.ppermute(value, 'shard', pairs)  173 us
    pallas_call x36, Pallas kernels, whole_call(): pl.pallas_call(kernel, out_shape=shapes[0] if single else shapes, in_spec...  128 us
    ppermute x40, starting transfers between devices, line_move(): return lambda value: lax.ppermute(value, 'shard', pairs)  100 us
    ppermute x32, waiting for transfers between devices, swap(): lax.ppermute(value, 'shard', [(source, source ^ bit) for source in range(...  61.6 us
    all_to_all x4, waiting for transfers between devices, turn_square(): lax.all_to_all(message, 'shard', 0, 0, tiled=True, axis_index_groups=SQUA...  41.8 us
    dot_general x8, matrix products, dot(): return jnp.dot(left, right, preferred_element_type=f32)  34.7 us
    ppermute x32, starting transfers between devices, swap(): lax.ppermute(value, 'shard', [(source, source ^ bit) for source in range(...  33 us
    dot_general x7, matrix products, along_last(): lax.dot_general(left, right, (((1,), (1,)), ((), ())), preferred_element_...  27.4 us
  transfers between devices with their start and end apart: 99, of which 49 were waited for; matrix products, arithmetic and copies ran while one was open for 15% of the time, Pallas kernels for 13%

profile of v6, /device:TPU:0, one launch (start us, length us, event | category | flops | bytes accessed | tf_op | source)
XLA Modules:
  0.0 792.9 jit_solution(2792689894630047546)
XLA Ops:
  15.2 16.2 %collective-permute-done.43.first_ref = bf16[1,384,1024]{2,1,0:T(8,128)(2,1)S(1)} collective-permute-done((bf16[1,384,1024]{2,1,0:T(8,128)(2,1)}, bf16[1,384,1024]{2,1,0:T(8,128)(2,1)S(1)}, u32[]{:S(2)}, u32[]{:S(2)}) %collective-permute-start.43) | collective-permute-done | bytes 786464 | tf_op jit(solution)/shard_map/ppermute | solution.py:286
  79.4 9.2 %collective-permute-done.51.further_ref = bf16[128,2048]{1,0:T(8,128)(2,1)} collective-permute-done((bf16[128,2048]{1,0:T(8,128)(2,1)}, bf16[128,2048]{1,0:T(8,128)(2,1)}, u32[]{:S(2)}, u32[]{:S(2)}) %collective-permute-start.51) | collective-permute-done | bytes 524320 | tf_op jit(solution)/shard_map/ppermute | solution.py:307
  97.3 20.0 %conditional.12 = (bf16[512,2048]{1,0:T(8,128)(2,1)}, f32[2,4,128,768]{3,2,1,0:T(8,128)}, f32[4,2,2,128]{3,2,1,0:T(2,128)S(1)}, f32[2,4,128,128]{3,2,1,0:T(8,128)S(1)}, f32[2,4,128,128]{3,2,1,0:T(8,128)S(1)}) conditional(s32[]{:T(128)} %bitcast.43, () %tuple.169, (bf16[512,2048]{1,0:T(8,128)(2,1)}, bf16[2048,768]{1,0:T(8,128)(2,1)}, ...), branch_computations={%region_0.1_spmd, %region_1.4_spmd} | conditional | flops 3223876096 | bytes 49536476 | solution.py:976
  130.1 53.6 %conditional.13 = (bf16[4,16,128,128]{3,2,1,0:T(8,128)(2,1)}, f32[16,128,1]{2,1,0:T(8,128)}, bf16[1024,256]{1,0:T(8,128)(2,1)}, bf16[4,384,2048]{2,1,0:T(8,128)(2,1)}) conditional(s32[]{:T(128)} %bitcast.43, () %tuple.168, (bf16[4,16,128,128]{3,2,1,0:T(8,128)(2,1)}, s32[1]{0:T(128)}, s32[16,128,1]{1,0,2:T(8,128)S(1)}, s32[1]{0:T(128)}, ...), branch_computations={%region_4.5_spmd, %region_5.6_spmd} | conditional | bytes 27820156 | solution.py:976
  135.0 24.9 %all-to-all-done.message_ref = bf16[4,16,128,128]{3,2,1,0:T(8,128)(2,1)} async-done(((bf16[4,16,128,128]{3,2,1,0:T(8,128)(2,1)}), bf16[4,16,128,128]{3,2,1,0:T(8,128)(2,1)}, u32[]{:S(2)}, u32[]{:S(2)}) %all-to-all-start) | async-done | bytes 2097184 | tf_op jit(solution)/shard_map/cond/branch_1_fun/all_to_all | solution.py:919
  159.9 11.1 %branch_1_fun.16 = (bf16[4,4,128,128]{3,2,1,0:T(8,128)(2,1)S(1)}, f32[16,128,1]{2,1,0:T(8,128)}) custom-call(s32[1]{0:T(128)} %get-tuple-element.224.place_ref, bf16[4,16,128,128]{3,2,1,0:T(8,128)(2,1)} %all-to-all-done.message_ref, s32[16,128,1]{2,1,0:T(8,128)S(1)} %copy.48.pos_ref), custom_call_target="tpu_custom_call" | custom-call | bytes 4210688 | tf_op jit(solution)/shard_map/cond/branch_1_fun/pallas_call | solution.py:590
  195.8 53.5 %conditional.14 = (f32[128,2048]{1,0:T(8,128)}, bf16[1024,2048]{1,0:T(8,128)(2,1)}) conditional(s32[]{:T(128)} %bitcast.43, () %tuple.167, (bf16[512,2048]{1,0:T(8,128)(2,1)}, bf16[4,384,2048]{2,1,0:T(8,128)(2,1)}) %tuple.181), branch_computations={%region_6.7_spmd, %region_7.8_spmd} | conditional | flops 5242900 | bytes 27787680 | solution.py:976
  213.4 10.2 %collective-permute-done.2 = bf16[128,2048]{1,0:T(8,128)(2,1)} collective-permute-done((bf16[128,2048]{1,0:T(8,128)(2,1)}, bf16[128,2048]{1,0:T(8,128)(2,1)}, u32[]{:S(2)}, u32[]{:S(2)}) %collective-permute-start.2) | collective-permute-done | bytes 524320 | tf_op jit(solution)/shard_map/cond/branch_1_fun/ppermute | solution.py:307
  254.9 47.7 %conditional.15 = (f32[128,1]{0,1:T(1,128)S(1)}, f32[128,2048]{1,0:T(8,128)}, bf16[512,2048]{1,0:T(8,128)(2,1)}) conditional(s32[]{:T(128)} %bitcast.43, () %tuple.166, (f32[128,2048]{1,0:T(8,128)}, bf16[128,2048]{1,0:T(8,128)(2,1)S(1)}, f32[4,2048]{1,0:T(4,128)S(1)}) %tuple.312), branch_computations={%region_8.9_spmd, %region_9.11_spmd} | conditional | flops 2097298 | bytes 22571924 | solution.py:976
  278.8 13.5 %collective-permute-done.22.lefts_ref = bf16[128,2048]{1,0:T(8,128)(2,1)S(1)} collective-permute-done((bf16[128,2048]{1,0:T(8,128)(2,1)}, bf16[128,2048]{1,0:T(8,128)(2,1)S(1)}, u32[]{:S(2)}, u32[]{:S(2)}) %collective-permute-start.22) | collective-permute-done | bytes 524320 | tf_op jit(solution)/shard_map/cond/branch_1_fun/ppermute | solution.py:307
  406.9 13.8 %collective-permute-done.75.lefts_ref = bf16[128,2048]{1,0:T(8,128)(2,1)S(1)} collective-permute-done((bf16[128,2048]{1,0:T(8,128)(2,1)S(1)}, bf16[128,2048]{1,0:T(8,128)(2,1)S(1)}, u32[]{:S(2)}, u32[]{:S(2)}) %collective-permute-start.75) | collective-permute-done | bytes 524320 | tf_op jit(solution)/shard_map/ppermute | solution.py:307
  420.7 9.8 %collective-permute-done.76.further_ref = bf16[128,2048]{1,0:T(8,128)(2,1)S(1)} collective-permute-done((bf16[128,2048]{1,0:T(8,128)(2,1)S(1)}, bf16[128,2048]{1,0:T(8,128)(2,1)S(1)}, u32[]{:S(2)}, u32[]{:S(2)}) %collective-permute-start.76) | collective-permute-done | bytes 524320 | tf_op jit(solution)/shard_map/ppermute | solution.py:307
  462.9 26.4 %conditional.16 = (bf16[128,2048]{1,0:T(8,128)(2,1)}, bf16[128,2048]{1,0:T(8,128)(2,1)}, bf16[128,2048]{1,0:T(8,128)(2,1)}, bf16[2,4,128,1024]{3,2,1,0:T(8,128)(...) conditional(s32[]{:T(128)} %bitcast.43, () %tuple.198, ...), branch_computations={%region_14.15_spmd, %region_15.16_spmd} | conditional | flops 8594391040 | bytes 42467684 | solution.py:976
  472.9 12.0 %convolution_convert_fusion = bf16[2048,2048]{1,0:T(8,128)(2,1)S(1)} fusion(bf16[1024,2048]{1,0:T(8,128)(2,1)} %get-tuple-element.268, bf16[1024,2048]{1,0:T(8,128)(2,1)} %get-tuple-element.269), kind=kOutput, calls=%fused_computation.35 | convolution fusion | flops 8594128896 | bytes 16777216 | tf_op jit(solution)/shard_map/cond/branch_1_fun/dot_general | solution.py:51
  491.3 44.0 %conditional.17 = (f32[128,2048]{1,0:T(8,128)}, bf16[128,2048]{1,0:T(8,128)(2,1)}, bf16[128,2048]{1,0:T(8,128)(2,1)}, bf16[128,2048]{1,0:T(8,128)(2,1)}) conditional(s32[]{:T(128)} %bitcast.43, () %tuple.195, (bf16[128,2048]{1,0:T(8,128)(2,1)S(1)}, bf16[512,2048]{1,0:T(8,128)(2,1)}, bf16[128,2048]{1,0:T(8,128)(2,1)}, bf16[128,2048]{1,0:T(8,128)(2,1)}, ...), branch_computations={%region_16.17_spmd, %region_17.19_spmd} | conditional | flops 7864595 | bytes 18911614 | solution.py:976
  549.1 16.7 %collective-permute-done.82.lefts_ref = bf16[128,2048]{1,0:T(8,128)(2,1)S(1)} collective-permute-done((bf16[128,2048]{1,0:T(8,128)(2,1)}, bf16[128,2048]{1,0:T(8,128)(2,1)S(1)}, u32[]{:S(2)}, u32[]{:S(2)}) %collective-permute-start.82) | collective-permute-done | bytes 524320 | tf_op jit(solution)/shard_map/ppermute | solution.py:307
  565.8 10.2 %collective-permute-done.83.further_ref = bf16[128,2048]{1,0:T(8,128)(2,1)S(1)} collective-permute-done((bf16[128,2048]{1,0:T(8,128)(2,1)S(1)}, bf16[128,2048]{1,0:T(8,128)(2,1)S(1)}, u32[]{:S(2)}, u32[]{:S(2)}) %collective-permute-start.83) | collective-permute-done | bytes 524320 | tf_op jit(solution)/shard_map/ppermute | solution.py:307
  594.2 66.5 %conditional.19 = (f32[2,2,4,128,256]{4,3,2,1,0:T(8,128)}, bf16[2,4,128,256]{3,2,1,0:T(8,128)(2,1)}, f32[2,2,4,128,1]{4,3,2,1,0:T(8,128)}, f32[2,256]{1,0:T(2,12...) conditional(s32[]{:T(128)} %bitcast.43, () %tuple.193, ...), branch_computations={%region_22.23_spmd, %region_23.24_spmd} | conditional | flops 5372903424 | bytes 96588040 | solution.py:976
  608.5 13.7 %branch_1_fun.22 = bf16[4,16,128,128]{3,2,1,0:T(8,128)(2,1)S(1)} custom-call(s32[1]{0:T(128)} %get-tuple-element.297.place_ref, bf16[4,16,128,128]{3,2,1,0:T(8,128)(2,1)} %get-tuple-element.298.message_ref, s32[16,128,1]{2,1,0:T(8,128)S(1)} %copy-done.12, f32[16,128,1]{2,1,0:T(8,128)} %get-tuple-element.300.lse_ref, ...), custom_call_target="tpu_custom_call" | custom-call | bytes 5275648 | tf_op jit(solution)/shard_map/cond/branch_1_fun/pallas_call | solution.py:590
  666.1 35.5 %conditional.20 = (bf16[512,2048]{1,0:T(8,128)(2,1)S(1)}, bf16[2,4,128,384]{3,2,1,0:T(8,128)(2,1)}, bf16[2,4,128,384]{3,2,1,0:T(8,128)(2,1)}, bf16[2,4,128,384]{...) conditional(s32[]{:T(128)} %bitcast.43, () %tuple.192, ...), branch_computations={%region_24.25_spmd, %region_25.26_spmd} | conditional | flops 6450374656 | bytes 111975696 | solution.py:976
  703.0 26.4 %conditional.21 = (bf16[128,2048]{1,0:T(8,128)(2,1)}, bf16[128,2048]{1,0:T(8,128)(2,1)}, bf16[128,2048]{1,0:T(8,128)(2,1)}, bf16[2,4,128,384]{3,2,1,0:T(8,128)(2...) conditional(s32[]{:T(128)} %bitcast.43, () %tuple.210, ...), branch_computations={%region_26.27_spmd, %region_27.28_spmd} | conditional | flops 262182 | bytes 36176388 | solution.py:976
  729.4 25.7 %conditional.22 = (f32[128,2048]{1,0:T(8,128)S(1)}, bf16[4,128,768]{2,1,0:T(8,128)(2,1)S(1)}) conditional(s32[]{:T(128)} %bitcast.43, () %tuple.191, (bf16[512,2048]{1,0:T(8,128)(2,1)}, bf16[128,2048]{1,0:T(8,128)(2,1)}, bf16[128,2048]{1,0:T(8,128)(2,1)}, bf16[128,2048]{1,0:T(8,128)(2,1)}, f32[128,2048]{1,0:T(8,128)}, ...), branch_computations={%region_28.29_spmd, %region_29.30_spmd} | conditional | flops 5242899 | bytes 24117614 | solution.py:976
  759.6 27.4 %conditional.23 = (f32[128,2048]{1,0:T(8,128)}, f32[512,2048]{1,0:T(8,128)}, f32[40,128]{1,0:T(8,128)S(1)}) conditional(s32[]{:T(128)} %bitcast.43, () %tuple.213, (bf16[1,384,1024]{2,1,0:T(8,128)(2,1)}, bf16[1,384,1024]{2,1,0:T(8,128)(2,1)}, bf16[1,384,1024]{2,1,0:T(8,128)(2,1)}, f32[40,128]{1,0:T(8,128)S(1)}, bf16[1,384,1024]{2,1,0:T(8,128)(2,1)}, ...), branch_computations={%region_30.31_spmd, %region_31.32_spmd} | conditional | flops 17573888 | bytes 34889952 | solution.py:976
  762.8 13.2 %collective-permute-done.16 = f32[40,128]{1,0:T(8,128)S(1)} collective-permute-done((f32[40,128]{1,0:T(8,128)S(1)}, f32[40,128]{1,0:T(8,128)S(1)}, u32[]{:S(2)}, u32[]{:S(2)}) %collective-permute-start.16) | collective-permute-done | bytes 20512 | tf_op jit(solution)/shard_map/cond/branch_1_fun/ppermute | solution.py:286
  (510 shorter events, 620.6 us)
Async XLA Ops:
  5.7 28.7 %all-to-all-start.4 = ((bf16[4,144,768]{2,1,0:T(8,128)(2,1)}), bf16[4,144,768]{2,1,0:T(8,128)(2,1)S(1)}, u32[]{:S(2)}, u32[]{:S(2)}) async-start(bf16[4,144,768]{2,1,0:T(8,128)(2,1)} %shard_map.237), calls=%async_computation.4 | async-start | bytes 1769472 | tf_op jit(solution)/shard_map/all_to_all | solution.py:450
  57.1 31.5 %collective-permute-start.52 = (bf16[2,4,144,384]{3,2,1,0:T(8,128)(2,1)}, bf16[2,4,144,384]{3,2,1,0:T(8,128)(2,1)}, u32[]{:S(2)}, u32[]{:S(2)}) collective-permute-start(bf16[2,4,144,384]{3,2,1,0:T(8,128)(2,1)} %get-tuple-element.634), channel_id=1, source_target_pairs={{0,2},{1,3},{2,0},{3,1},{4,6},{5,7},{6,4},{7,5},{8,10},{9,11},{10,... | collective-permute-start | bytes 2654216 | tf_op jit(solution)/shard_map/ppermute | solution.py:286
  58.6 30.0 %collective-permute-start.53 = (bf16[2,4,144,384]{3,2,1,0:T(8,128)(2,1)}, bf16[2,4,144,384]{3,2,1,0:T(8,128)(2,1)}, u32[]{:S(2)}, u32[]{:S(2)}) collective-permute-start(bf16[2,4,144,384]{3,2,1,0:T(8,128)(2,1)} %get-tuple-element.635), channel_id=1, source_target_pairs={{0,1},{1,0},{2,3},{3,2},{4,5},{5,4},{6,7},{7,6},{8,9},{9,8},{10,11... | collective-permute-start | bytes 2654216 | tf_op jit(solution)/shard_map/ppermute | solution.py:286
  90.5 39.6 %collective-permute-start.55 = (bf16[2,1,384,1024]{3,2,1,0:T(8,128)(2,1)}, bf16[2,1,384,1024]{3,2,1,0:T(8,128)(2,1)}, u32[]{:S(2)}, u32[]{:S(2)}) collective-permute-start(bf16[2,1,384,1024]{3,2,1,0:T(8,128)(2,1)} %get-tuple-element.650), channel_id=1, source_target_pairs={{0,2},{1,3},{2,0},{3,1},{4,6},{5,7},{6,4},{7,5},{8,10},{9,11},{10,... | collective-permute-start | bytes 4718600 | tf_op jit(solution)/shard_map/ppermute | solution.py:286
  91.1 39.0 %collective-permute-start.56 = (bf16[2,1,384,1024]{3,2,1,0:T(8,128)(2,1)}, bf16[2,1,384,1024]{3,2,1,0:T(8,128)(2,1)}, u32[]{:S(2)}, u32[]{:S(2)}) collective-permute-start(bf16[2,1,384,1024]{3,2,1,0:T(8,128)(2,1)} %get-tuple-element.651), channel_id=1, source_target_pairs={{0,1},{1,0},{2,3},{3,2},{4,5},{5,4},{6,7},{7,6},{8,9},{9,8},{10,11... | collective-permute-start | bytes 4718600 | tf_op jit(solution)/shard_map/ppermute | solution.py:286
  118.7 65.1 %collective-permute-start.57 = (bf16[128,2048]{1,0:T(8,128)(2,1)}, bf16[128,2048]{1,0:T(8,128)(2,1)}, u32[]{:S(2)}, u32[]{:S(2)}) collective-permute-start(bf16[128,2048]{1,0:T(8,128)(2,1)} %get-tuple-element.978), channel_id=1, source_target_pairs={{0,4},{1,5},{2,6},{3,7},{4,8},{5,9},{6,10},{7,11},{8,12},{9,13},{1... | collective-permute-start | bytes 1572872 | tf_op jit(solution)/shard_map/ppermute | solution.py:315
  118.7 65.1 %collective-permute-start.58 = (bf16[128,2048]{1,0:T(8,128)(2,1)}, bf16[128,2048]{1,0:T(8,128)(2,1)}, u32[]{:S(2)}, u32[]{:S(2)}) collective-permute-start(bf16[128,2048]{1,0:T(8,128)(2,1)} %get-tuple-element.977), channel_id=1, source_target_pairs={{0,8},{1,9},{2,10},{3,11},{4,12},{5,13},{6,14},{7,15},{8,0},{9,1},... | collective-permute-start | bytes 1572872 | tf_op jit(solution)/shard_map/ppermute | solution.py:315
  118.9 64.8 %collective-permute-start.59 = (bf16[128,2048]{1,0:T(8,128)(2,1)}, bf16[128,2048]{1,0:T(8,128)(2,1)}, u32[]{:S(2)}, u32[]{:S(2)}) collective-permute-start(bf16[128,2048]{1,0:T(8,128)(2,1)} %get-tuple-element.976), channel_id=1, source_target_pairs={{0,12},{1,13},{2,14},{3,15},{4,0},{5,1},{6,2},{7,3},{8,4},{9,5},{1... | collective-permute-start | bytes 1572872 | tf_op jit(solution)/shard_map/ppermute | solution.py:315
  130.1 29.8 %all-to-all-start = ((bf16[4,16,128,128]{3,2,1,0:T(8,128)(2,1)}), bf16[4,16,128,128]{3,2,1,0:T(8,128)(2,1)}, u32[]{:S(2)}, u32[]{:S(2)}) async-start(bf16[4,16,128,128]{3,2,1,0:T(8,128)(2,1)} %get-tuple-element.223), calls=%async_computation | async-start | bytes 4194304 | tf_op jit(solution)/shard_map/cond/branch_1_fun/all_to_all | solution.py:919
  189.8 59.5 %collective-permute-start.61 = (bf16[4,128,1024]{2,1,0:T(8,128)(2,1)}, bf16[4,128,1024]{2,1,0:T(8,128)(2,1)S(1)}, u32[]{:S(2)}, u32[]{:S(2)}) collective-permute-start(bf16[4,128,1024]{2,1,0:T(8,128)(2,1)} %get-tuple-element.663), channel_id=1, source_target_pairs={{0,1},{1,0},{2,3},{3,2},{4,5},{5,4},{6,7},{7,6},{8,9},{9,8},{10,11... | collective-permute-start | bytes 3145736 | tf_op jit(solution)/shard_map/ppermute | solution.py:286
  191.3 58.0 %collective-permute-start.62 = (bf16[4,128,1024]{2,1,0:T(8,128)(2,1)}, bf16[4,128,1024]{2,1,0:T(8,128)(2,1)}, u32[]{:S(2)}, u32[]{:S(2)}) collective-permute-start(bf16[4,128,1024]{2,1,0:T(8,128)(2,1)} %get-tuple-element.664), channel_id=1, source_target_pairs={{0,2},{1,3},{2,0},{3,1},{4,6},{5,7},{6,4},{7,5},{8,10},{9,11},{10,... | collective-permute-start | bytes 3145736 | tf_op jit(solution)/shard_map/ppermute | solution.py:286
  252.8 49.8 %collective-permute-start.63 = (bf16[2,4,128,1024]{3,2,1,0:T(8,128)(2,1)}, bf16[2,4,128,1024]{3,2,1,0:T(8,128)(2,1)}, u32[]{:S(2)}, u32[]{:S(2)}) collective-permute-start(bf16[2,4,128,1024]{3,2,1,0:T(8,128)(2,1)} %get-tuple-element.670), channel_id=1, source_target_pairs={{0,2},{1,3},{2,0},{3,1},{4,6},{5,7},{6,4},{7,5},{8,10},{9,11},{10,... | collective-permute-start | bytes 6291464 | tf_op jit(solution)/shard_map/ppermute | solution.py:286
  254.3 48.3 %collective-permute-start.64 = (bf16[2,4,128,1024]{3,2,1,0:T(8,128)(2,1)}, bf16[2,4,128,1024]{3,2,1,0:T(8,128)(2,1)}, u32[]{:S(2)}, u32[]{:S(2)}) collective-permute-start(bf16[2,4,128,1024]{3,2,1,0:T(8,128)(2,1)} %get-tuple-element.671), channel_id=1, source_target_pairs={{0,1},{1,0},{2,3},{3,2},{4,5},{5,4},{6,7},{7,6},{8,9},{9,8},{10,11... | collective-permute-start | bytes 6291464 | tf_op jit(solution)/shard_map/ppermute | solution.py:286
  489.3 47.5 %collective-permute-start.79 = (bf16[2,4,128,1024]{3,2,1,0:T(8,128)(2,1)}, bf16[2,4,128,1024]{3,2,1,0:T(8,128)(2,1)S(1)}, u32[]{:S(2)}, u32[]{:S(2)}) collective-permute-start(bf16[2,4,128,1024]{3,2,1,0:T(8,128)(2,1)} %get-tuple-element.717), channel_id=1, source_target_pairs={{0,2},{1,3},{2,0},{3,1},{4,6},{5,7},{6,4},{7,5},{8,10},{9,11},{10,... | collective-permute-start | bytes 6291464 | tf_op jit(solution)/shard_map/ppermute | solution.py:286
  490.8 47.3 %collective-permute-start.80 = (bf16[2,4,128,1024]{3,2,1,0:T(8,128)(2,1)}, bf16[2,4,128,1024]{3,2,1,0:T(8,128)(2,1)}, u32[]{:S(2)}, u32[]{:S(2)}) collective-permute-start(bf16[2,4,128,1024]{3,2,1,0:T(8,128)(2,1)} %get-tuple-element.718), channel_id=1, source_target_pairs={{0,1},{1,0},{2,3},{3,2},{4,5},{5,4},{6,7},{7,6},{8,9},{9,8},{10,11... | collective-permute-start | bytes 6291464 | tf_op jit(solution)/shard_map/ppermute | solution.py:286
  542.7 41.9 %collective-permute-start.84 = (bf16[4,128,1024]{2,1,0:T(8,128)(2,1)}, bf16[4,128,1024]{2,1,0:T(8,128)(2,1)}, u32[]{:S(2)}, u32[]{:S(2)}) collective-permute-start(bf16[4,128,1024]{2,1,0:T(8,128)(2,1)} %get-tuple-element.735), channel_id=1, source_target_pairs={{0,1},{1,0},{2,3},{3,2},{4,5},{5,4},{6,7},{7,6},{8,9},{9,8},{10,11... | collective-permute-start | bytes 3145736 | tf_op jit(solution)/shard_map/ppermute | solution.py:286
  543.2 41.4 %collective-permute-start.85 = (bf16[4,128,1024]{2,1,0:T(8,128)(2,1)}, bf16[4,128,1024]{2,1,0:T(8,128)(2,1)}, u32[]{:S(2)}, u32[]{:S(2)}) collective-permute-start(bf16[4,128,1024]{2,1,0:T(8,128)(2,1)} %get-tuple-element.736), channel_id=1, source_target_pairs={{0,2},{1,3},{2,0},{3,1},{4,6},{5,7},{6,4},{7,5},{8,10},{9,11},{10,... | collective-permute-start | bytes 3145736 | tf_op jit(solution)/shard_map/ppermute | solution.py:286
  590.3 70.3 %collective-permute-start.86 = (bf16[128,2048]{1,0:T(8,128)(2,1)}, bf16[128,2048]{1,0:T(8,128)(2,1)}, u32[]{:S(2)}, u32[]{:S(2)}) collective-permute-start(bf16[128,2048]{1,0:T(8,128)(2,1)} %get-tuple-element.973), channel_id=1, source_target_pairs={{0,4},{1,5},{2,6},{3,7},{4,8},{5,9},{6,10},{7,11},{8,12},{9,13},{1... | collective-permute-start | bytes 1572872 | tf_op jit(solution)/shard_map/ppermute | solution.py:315
  590.3 70.3 %collective-permute-start.87 = (bf16[128,2048]{1,0:T(8,128)(2,1)}, bf16[128,2048]{1,0:T(8,128)(2,1)}, u32[]{:S(2)}, u32[]{:S(2)}) collective-permute-start(bf16[128,2048]{1,0:T(8,128)(2,1)} %get-tuple-element.972), channel_id=1, source_target_pairs={{0,8},{1,9},{2,10},{3,11},{4,12},{5,13},{6,14},{7,15},{8,0},{9,1},... | collective-permute-start | bytes 1572872 | tf_op jit(solution)/shard_map/ppermute | solution.py:315
  590.3 70.3 %collective-permute-start.88 = (bf16[128,2048]{1,0:T(8,128)(2,1)}, bf16[128,2048]{1,0:T(8,128)(2,1)}, u32[]{:S(2)}, u32[]{:S(2)}) collective-permute-start(bf16[128,2048]{1,0:T(8,128)(2,1)} %get-tuple-element.971), channel_id=1, source_target_pairs={{0,12},{1,13},{2,14},{3,15},{4,0},{5,1},{6,2},{7,3},{8,4},{9,5},{1... | collective-permute-start | bytes 1572872 | tf_op jit(solution)/shard_map/ppermute | solution.py:315
  664.1 38.3 %collective-permute-start.91 = (bf16[4,128,2048]{2,1,0:T(8,128)(2,1)}, bf16[4,128,2048]{2,1,0:T(8,128)(2,1)}, u32[]{:S(2)}, u32[]{:S(2)}) collective-permute-start(bf16[4,128,2048]{2,1,0:T(8,128)(2,1)} %get-tuple-element.764), channel_id=1, source_target_pairs={{0,16},{16,0},{1,17},{17,1},{2,18},{18,2},{3,19},{19,3},{4,20},{20... | collective-permute-start | bytes 6291464 | tf_op jit(solution)/shard_map/ppermute | solution.py:290
  664.1 37.5 %collective-permute-start.89 = (bf16[2,1,384,1024]{3,2,1,0:T(8,128)(2,1)}, bf16[2,1,384,1024]{3,2,1,0:T(8,128)(2,1)}, u32[]{:S(2)}, u32[]{:S(2)}) collective-permute-start(bf16[2,1,384,1024]{3,2,1,0:T(8,128)(2,1)} %get-tuple-element.756), channel_id=1, source_target_pairs={{0,2},{1,3},{2,0},{3,1},{4,6},{5,7},{6,4},{7,5},{8,10},{9,11},{10,... | collective-permute-start | bytes 4718600 | tf_op jit(solution)/shard_map/ppermute | solution.py:286
  665.6 36.8 %collective-permute-start.90 = (bf16[2,1,384,1024]{3,2,1,0:T(8,128)(2,1)}, bf16[2,1,384,1024]{3,2,1,0:T(8,128)(2,1)}, u32[]{:S(2)}, u32[]{:S(2)}) collective-permute-start(bf16[2,1,384,1024]{3,2,1,0:T(8,128)(2,1)} %get-tuple-element.757), channel_id=1, source_target_pairs={{0,1},{1,0},{2,3},{3,2},{4,5},{5,4},{6,7},{7,6},{8,9},{9,8},{10,11... | collective-permute-start | bytes 4718600 | tf_op jit(solution)/shard_map/ppermute | solution.py:286
  756.0 31.1 %all-to-all-start.5 = ((bf16[4,128,768]{2,1,0:T(8,128)(2,1)}), bf16[4,128,768]{2,1,0:T(8,128)(2,1)S(1)}, u32[]{:S(2)}, u32[]{:S(2)}) async-start(bf16[4,128,768]{2,1,0:T(8,128)(2,1)} %copy-done.43), calls=%async_computation.5 | async-start | bytes 1572864 | tf_op jit(solution)/shard_map/all_to_all | solution.py:450
  (143 other events, 1514.4 us)

commit v7 on v6

--- a/solution.py
+++ b/solution.py
@@ -361,6 +361,10 @@
 
 
 def gather_second(value, right, left):
+    return gather_whole(*(yield from gather_pieces(value, right, left)))
+
+
+def gather_pieces(value, right, left):
     place = line_place()
     further = jnp.where(place == 1, right, left)
     rights, lefts, further = yield [
@@ -368,10 +372,13 @@
         (left, line_move(LEFT[1:])),
         (further, line_move(((1, 3), (2, 0)))),
     ]
-    rows, width = value.shape
-    shape = jax.ShapeDtypeStruct((LINE * rows, width), value.dtype)
-    arrays = [value, right, left, rights, lefts, further]
-    return whole_call(gather_kernel, [shape], [place.astype(jnp.int32).reshape(1)], arrays)
+    return value, right, left, rights, lefts, further
+
+
+def gather_whole(*pieces):
+    rows, width = pieces[0].shape
+    shape = jax.ShapeDtypeStruct((LINE * rows, width), pieces[0].dtype)
+    return whole_call(gather_kernel, [shape], [line_place().astype(jnp.int32).reshape(1)], list(pieces))
 
 
 def gather_kernel(place_ref, own_ref, right_ref, left_ref, rights_ref, lefts_ref, further_ref, out_ref):
@@ -411,9 +418,14 @@
     return join(own, swap_core(own))
 
 
-def scatter_first(total):
+def scatter_further(total):
     parts = total.reshape(LINE, -1, total.shape[-1])
-    further = jnp.where(line_place() == 0, parts[1], parts[3])
+    return jnp.where(line_place() == 0, parts[1], parts[3])
+
+
+def scatter_first(total, further=None):
+    parts = total.reshape(LINE, -1, total.shape[-1])
+    further = scatter_further(total) if further is None else further
     return (
         yield [
             (parts[2], line_move(RIGHT[:2])),
@@ -433,8 +445,8 @@
     return add_wide(parts[0], right, left)
 
 
-def scatter_line(total):
-    came = yield from scatter_first(total)
+def scatter_line(total, further=None):
+    came = yield from scatter_first(total, further)
     return (yield from scatter_second(total, *came))
 
 
@@ -1076,7 +1088,7 @@
 
     branch = across_cores(parts_of(mixed), out_w, dot)
     branch, down_w = region(
-        lambda total, rows: (alone(scatter_line(total)), rows[:, ROWS:].reshape(-1, width)), branch, rows_w
+        lambda total, further, rows: (alone(scatter_line(total, further)), rows[:, ROWS:].reshape(-1, width)), branch, scatter_further(branch), rows_w
     )
     branch, hidden_came = together(branch, hidden_came)
     hidden_later = square_second(hidden_own, hidden_came)
@@ -1084,13 +1096,14 @@
     def state_of(branch):
         branch_scale = lax.rsqrt(jnp.mean(branch * branch, axis=-1, keepdims=True) + 1e-06)
         hidden_state = inputs.astype(f32) + branch * branch_scale * gains[2]
-        state = alone(gather_line(hidden_state.astype(bf16)))
+        state = alone(gather_pieces(*alone(gather_first(hidden_state.astype(bf16)))))
         return branch_scale, hidden_state, state
 
     branch_scale, hidden_state, state = region(state_of, branch)
     state, hidden_later = together(state, hidden_later)
     hidden_w = square_join(from_slots, hidden_own, hidden_came, hidden_later).reshape(width, -1)
 
+    state = gather_whole(*state)
     state = (state, swap_core(state))
     both = [dot(part, hidden_w) for part in state]
     active = [(jax.nn.silu(in_two(part)[0]) * in_two(part)[1]).astype(bf16) for part in both]

time: 804 us -> 809 us (level)
  transfers between devices with their start and end apart: 99 -> 99, of which waited for: 49 -> 50; matrix products, arithmetic and copies ran while one was open for 15% -> 15% of each run, Pallas kernels for 13% -> 13%
where the time goes in v7:
time: 809 us; the launch traced here: 797 us
  waiting for transfers between devices  286 us (35%)
  starting transfers between devices  170 us (21%)
  Pallas kernels  133 us (16%)
  matrix products  89.5 us (11%)
  other arithmetic  60.5 us (7%)
  local copies, waits for them, and re-layouts  53.6 us (7%)
    ppermute x40, waiting for transfers between devices, line_move(): return lambda value: lax.ppermute(value, 'shard', pairs)  173 us
    pallas_call x36, Pallas kernels, whole_call(): pl.pallas_call(kernel, out_shape=shapes[0] if single else shapes, in_spec...  129 us
    ppermute x40, starting transfers between devices, line_move(): return lambda value: lax.ppermute(value, 'shard', pairs)  101 us
    ppermute x32, waiting for transfers between devices, swap(): lax.ppermute(value, 'shard', [(source, source ^ bit) for source in range(...  61.5 us
    all_to_all x4, waiting for transfers between devices, turn_square(): lax.all_to_all(message, 'shard', 0, 0, tiled=True, axis_index_groups=SQUA...  41.6 us
    dot_general x8, matrix products, dot(): return jnp.dot(left, right, preferred_element_type=f32)  36.4 us
    ppermute x32, starting transfers between devices, swap(): lax.ppermute(value, 'shard', [(source, source ^ bit) for source in range(...  33 us
    dot_general x7, matrix products, along_last(): lax.dot_general(left, right, (((1,), (1,)), ((), ())), preferred_element_...  27.4 us
  transfers between devices with their start and end apart: 99, of which 50 were waited for; matrix products, arithmetic and copies ran while one was open for 15% of the time, Pallas kernels for 13%

profile of v7, /device:TPU:0, one launch (start us, length us, event | category | flops | bytes accessed | tf_op | source)
XLA Modules:
  0.0 797.4 jit_solution(2307935288415429154)
XLA Ops:
  15.2 16.2 %collective-permute-done.43.first_ref = bf16[1,384,1024]{2,1,0:T(8,128)(2,1)S(1)} collective-permute-done((bf16[1,384,1024]{2,1,0:T(8,128)(2,1)}, bf16[1,384,1024]{2,1,0:T(8,128)(2,1)S(1)}, u32[]{:S(2)}, u32[]{:S(2)}) %collective-permute-start.43) | collective-permute-done | bytes 786464 | tf_op jit(solution)/shard_map/ppermute | solution.py:286
  79.4 9.2 %collective-permute-done.51.further_ref = bf16[128,2048]{1,0:T(8,128)(2,1)} collective-permute-done((bf16[128,2048]{1,0:T(8,128)(2,1)}, bf16[128,2048]{1,0:T(8,128)(2,1)}, u32[]{:S(2)}, u32[]{:S(2)}) %collective-permute-start.51) | collective-permute-done | bytes 524320 | tf_op jit(solution)/shard_map/ppermute | solution.py:307
  97.3 19.9 %conditional.12 = (bf16[512,2048]{1,0:T(8,128)(2,1)}, f32[2,4,128,768]{3,2,1,0:T(8,128)}, f32[4,2,2,128]{3,2,1,0:T(2,128)S(1)}, f32[2,4,128,128]{3,2,1,0:T(8,128)S(1)}, f32[2,4,128,128]{3,2,1,0:T(8,128)S(1)}) conditional(s32[]{:T(128)} %bitcast.43, () %tuple.169, (bf16[512,2048]{1,0:T(8,128)(2,1)}, bf16[2048,768]{1,0:T(8,128)(2,1)}, ...), branch_computations={%region_0.1_spmd, %region_1.4_spmd} | conditional | flops 3223876096 | bytes 49536476 | solution.py:988
  130.1 53.7 %conditional.13 = (bf16[4,16,128,128]{3,2,1,0:T(8,128)(2,1)}, f32[16,128,1]{2,1,0:T(8,128)}, bf16[1024,256]{1,0:T(8,128)(2,1)}, bf16[4,384,2048]{2,1,0:T(8,128)(2,1)}) conditional(s32[]{:T(128)} %bitcast.43, () %tuple.168, (bf16[4,16,128,128]{3,2,1,0:T(8,128)(2,1)}, s32[1]{0:T(128)}, s32[16,128,1]{1,0,2:T(8,128)S(1)}, s32[1]{0:T(128)}, ...), branch_computations={%region_4.5_spmd, %region_5.6_spmd} | conditional | bytes 27820156 | solution.py:988
  135.0 24.9 %all-to-all-done.message_ref = bf16[4,16,128,128]{3,2,1,0:T(8,128)(2,1)} async-done(((bf16[4,16,128,128]{3,2,1,0:T(8,128)(2,1)}), bf16[4,16,128,128]{3,2,1,0:T(8,128)(2,1)}, u32[]{:S(2)}, u32[]{:S(2)}) %all-to-all-start) | async-done | bytes 2097184 | tf_op jit(solution)/shard_map/cond/branch_1_fun/all_to_all | solution.py:931
  159.9 11.1 %branch_1_fun.15 = (bf16[4,4,128,128]{3,2,1,0:T(8,128)(2,1)S(1)}, f32[16,128,1]{2,1,0:T(8,128)}) custom-call(s32[1]{0:T(128)} %get-tuple-element.232.place_ref, bf16[4,16,128,128]{3,2,1,0:T(8,128)(2,1)} %all-to-all-done.message_ref, s32[16,128,1]{2,1,0:T(8,128)S(1)} %copy.48.pos_ref), custom_call_target="tpu_custom_call" | custom-call | bytes 4210688 | tf_op jit(solution)/shard_map/cond/branch_1_fun/pallas_call | solution.py:602
  198.8 53.4 %conditional.14 = (f32[128,2048]{1,0:T(8,128)}, bf16[1024,2048]{1,0:T(8,128)(2,1)}) conditional(s32[]{:T(128)} %bitcast.43, () %tuple.167, (bf16[512,2048]{1,0:T(8,128)(2,1)S(1)}, pred[]{:T(512)}, bf16[4,384,2048]{2,1,0:T(8,128)(2,1)}) %tuple.181), branch_computations={%region_6.7_spmd, %region_7.8_spmd} | conditional | flops 5242899 | bytes 36176304 | solution.py:988
  216.3 10.3 %collective-permute-done.2 = bf16[128,2048]{1,0:T(8,128)(2,1)} collective-permute-done((bf16[128,2048]{1,0:T(8,128)(2,1)}, bf16[128,2048]{1,0:T(8,128)(2,1)}, u32[]{:S(2)}, u32[]{:S(2)}) %collective-permute-start.2) | collective-permute-done | bytes 524320 | tf_op jit(solution)/shard_map/cond/branch_1_fun/ppermute | solution.py:307
  257.8 45.4 %conditional.15 = (f32[128,1]{0,1:T(1,128)S(1)}, f32[128,2048]{1,0:T(8,128)}, bf16[128,2048]{1,0:T(8,128)(2,1)}, bf16[128,2048]{1,0:T(8,128)(2,1)}, bf16[128,204...) conditional(s32[]{:T(128)} %bitcast.43, () %tuple.166, ...), branch_computations={%region_8.9_spmd, %region_9.11_spmd} | conditional | flops 2097298 | bytes 16280508 | solution.py:988
  282.5 13.7 %collective-permute-done.22 = bf16[128,2048]{1,0:T(8,128)(2,1)} collective-permute-done((bf16[128,2048]{1,0:T(8,128)(2,1)}, bf16[128,2048]{1,0:T(8,128)(2,1)}, u32[]{:S(2)}, u32[]{:S(2)}) %collective-permute-start.22) | collective-permute-done | bytes 524320 | tf_op jit(solution)/shard_map/cond/branch_1_fun/ppermute | solution.py:307
  411.3 13.8 %collective-permute-done.75.lefts_ref = bf16[128,2048]{1,0:T(8,128)(2,1)S(1)} collective-permute-done((bf16[128,2048]{1,0:T(8,128)(2,1)S(1)}, bf16[128,2048]{1,0:T(8,128)(2,1)S(1)}, u32[]{:S(2)}, u32[]{:S(2)}) %collective-permute-start.75) | collective-permute-done | bytes 524320 | tf_op jit(solution)/shard_map/ppermute | solution.py:307
  425.1 9.9 %collective-permute-done.76.further_ref = bf16[128,2048]{1,0:T(8,128)(2,1)S(1)} collective-permute-done((bf16[128,2048]{1,0:T(8,128)(2,1)S(1)}, bf16[128,2048]{1,0:T(8,128)(2,1)S(1)}, u32[]{:S(2)}, u32[]{:S(2)}) %collective-permute-start.76) | collective-permute-done | bytes 524320 | tf_op jit(solution)/shard_map/ppermute | solution.py:307
  467.4 26.4 %conditional.16 = (bf16[128,2048]{1,0:T(8,128)(2,1)}, bf16[128,2048]{1,0:T(8,128)(2,1)}, bf16[128,2048]{1,0:T(8,128)(2,1)}, bf16[2,4,128,1024]{3,2,1,0:T(8,128)(...) conditional(s32[]{:T(128)} %bitcast.43, () %tuple.198, ...), branch_computations={%region_14.15_spmd, %region_15.16_spmd} | conditional | flops 8594391040 | bytes 42467684 | solution.py:988
  477.4 12.0 %convolution_convert_fusion = bf16[2048,2048]{1,0:T(8,128)(2,1)S(1)} fusion(bf16[1024,2048]{1,0:T(8,128)(2,1)} %get-tuple-element.277, bf16[1024,2048]{1,0:T(8,128)(2,1)} %get-tuple-element.278), kind=kOutput, calls=%fused_computation.35 | convolution fusion | flops 8594128896 | bytes 16777216 | tf_op jit(solution)/shard_map/cond/branch_1_fun/dot_general | solution.py:51
  495.8 44.0 %conditional.17 = (f32[128,2048]{1,0:T(8,128)}, bf16[128,2048]{1,0:T(8,128)(2,1)}, bf16[128,2048]{1,0:T(8,128)(2,1)}, bf16[128,2048]{1,0:T(8,128)(2,1)}) conditional(s32[]{:T(128)} %bitcast.43, () %tuple.195, (bf16[128,2048]{1,0:T(8,128)(2,1)S(1)}, bf16[512,2048]{1,0:T(8,128)(2,1)}, bf16[128,2048]{1,0:T(8,128)(2,1)}, bf16[128,2048]{1,0:T(8,128)(2,1)}, ...), branch_computations={%region_16.17_spmd, %region_17.19_spmd} | conditional | flops 7864595 | bytes 18911614 | solution.py:988
  553.6 16.7 %collective-permute-done.82.lefts_ref = bf16[128,2048]{1,0:T(8,128)(2,1)S(1)} collective-permute-done((bf16[128,2048]{1,0:T(8,128)(2,1)}, bf16[128,2048]{1,0:T(8,128)(2,1)S(1)}, u32[]{:S(2)}, u32[]{:S(2)}) %collective-permute-start.82) | collective-permute-done | bytes 524320 | tf_op jit(solution)/shard_map/ppermute | solution.py:307
  570.3 10.2 %collective-permute-done.83.further_ref = bf16[128,2048]{1,0:T(8,128)(2,1)S(1)} collective-permute-done((bf16[128,2048]{1,0:T(8,128)(2,1)S(1)}, bf16[128,2048]{1,0:T(8,128)(2,1)S(1)}, u32[]{:S(2)}, u32[]{:S(2)}) %collective-permute-start.83) | collective-permute-done | bytes 524320 | tf_op jit(solution)/shard_map/ppermute | solution.py:307
  598.7 66.4 %conditional.19 = (f32[2,2,4,128,256]{4,3,2,1,0:T(8,128)}, bf16[2,4,128,256]{3,2,1,0:T(8,128)(2,1)}, f32[2,2,4,128,1]{4,3,2,1,0:T(8,128)}, f32[2,256]{1,0:T(2,12...) conditional(s32[]{:T(128)} %bitcast.43, () %tuple.193, ...), branch_computations={%region_22.23_spmd, %region_23.24_spmd} | conditional | flops 5372903424 | bytes 96588040 | solution.py:988
  613.0 13.7 %branch_1_fun.20 = bf16[4,16,128,128]{3,2,1,0:T(8,128)(2,1)S(1)} custom-call(s32[1]{0:T(128)} %get-tuple-element.306.place_ref, bf16[4,16,128,128]{3,2,1,0:T(8,128)(2,1)} %get-tuple-element.307.message_ref, s32[16,128,1]{2,1,0:T(8,128)S(1)} %copy-done.12, f32[16,128,1]{2,1,0:T(8,128)} %get-tuple-element.309.lse_ref, ...), custom_call_target="tpu_custom_call" | custom-call | bytes 5275648 | tf_op jit(solution)/shard_map/cond/branch_1_fun/pallas_call | solution.py:602
  670.6 35.5 %conditional.20 = (bf16[512,2048]{1,0:T(8,128)(2,1)S(1)}, bf16[2,4,128,384]{3,2,1,0:T(8,128)(2,1)}, bf16[2,4,128,384]{3,2,1,0:T(8,128)(2,1)}, bf16[2,4,128,384]{...) conditional(s32[]{:T(128)} %bitcast.43, () %tuple.192, ...), branch_computations={%region_24.25_spmd, %region_25.26_spmd} | conditional | flops 6450374656 | bytes 111975696 | solution.py:988
  707.5 26.4 %conditional.21 = (bf16[128,2048]{1,0:T(8,128)(2,1)}, bf16[128,2048]{1,0:T(8,128)(2,1)}, bf16[128,2048]{1,0:T(8,128)(2,1)}, bf16[2,4,128,384]{3,2,1,0:T(8,128)(2...) conditional(s32[]{:T(128)} %bitcast.43, () %tuple.210, ...), branch_computations={%region_26.27_spmd, %region_27.28_spmd} | conditional | flops 262182 | bytes 36176388 | solution.py:988
  733.9 25.7 %conditional.22 = (f32[128,2048]{1,0:T(8,128)S(1)}, bf16[4,128,768]{2,1,0:T(8,128)(2,1)S(1)}) conditional(s32[]{:T(128)} %bitcast.43, () %tuple.191, (bf16[512,2048]{1,0:T(8,128)(2,1)}, bf16[128,2048]{1,0:T(8,128)(2,1)}, bf16[128,2048]{1,0:T(8,128)(2,1)}, bf16[128,2048]{1,0:T(8,128)(2,1)}, f32[128,2048]{1,0:T(8,128)}, ...), branch_computations={%region_28.29_spmd, %region_29.30_spmd} | conditional | flops 5242899 | bytes 24117614 | solution.py:988
  764.1 27.4 %conditional.23 = (f32[128,2048]{1,0:T(8,128)}, f32[512,2048]{1,0:T(8,128)}, f32[40,128]{1,0:T(8,128)S(1)}) conditional(s32[]{:T(128)} %bitcast.43, () %tuple.213, (bf16[1,384,1024]{2,1,0:T(8,128)(2,1)}, bf16[1,384,1024]{2,1,0:T(8,128)(2,1)}, bf16[1,384,1024]{2,1,0:T(8,128)(2,1)}, f32[40,128]{1,0:T(8,128)S(1)}, bf16[1,384,1024]{2,1,0:T(8,128)(2,1)}, ...), branch_computations={%region_30.31_spmd, %region_31.32_spmd} | conditional | flops 17573888 | bytes 34889952 | solution.py:988
  767.3 13.3 %collective-permute-done.16 = f32[40,128]{1,0:T(8,128)S(1)} collective-permute-done((f32[40,128]{1,0:T(8,128)S(1)}, f32[40,128]{1,0:T(8,128)S(1)}, u32[]{:S(2)}, u32[]{:S(2)}) %collective-permute-start.16) | collective-permute-done | bytes 20512 | tf_op jit(solution)/shard_map/cond/branch_1_fun/ppermute | solution.py:286
  (512 shorter events, 625.1 us)
Async XLA Ops:
  5.7 28.7 %all-to-all-start.4 = ((bf16[4,144,768]{2,1,0:T(8,128)(2,1)}), bf16[4,144,768]{2,1,0:T(8,128)(2,1)S(1)}, u32[]{:S(2)}, u32[]{:S(2)}) async-start(bf16[4,144,768]{2,1,0:T(8,128)(2,1)} %shard_map.237), calls=%async_computation.4 | async-start | bytes 1769472 | tf_op jit(solution)/shard_map/all_to_all | solution.py:462
  57.1 31.5 %collective-permute-start.52 = (bf16[2,4,144,384]{3,2,1,0:T(8,128)(2,1)}, bf16[2,4,144,384]{3,2,1,0:T(8,128)(2,1)}, u32[]{:S(2)}, u32[]{:S(2)}) collective-permute-start(bf16[2,4,144,384]{3,2,1,0:T(8,128)(2,1)} %get-tuple-element.653), channel_id=1, source_target_pairs={{0,2},{1,3},{2,0},{3,1},{4,6},{5,7},{6,4},{7,5},{8,10},{9,11},{10,... | collective-permute-start | bytes 2654216 | tf_op jit(solution)/shard_map/ppermute | solution.py:286
  58.6 30.0 %collective-permute-start.53 = (bf16[2,4,144,384]{3,2,1,0:T(8,128)(2,1)}, bf16[2,4,144,384]{3,2,1,0:T(8,128)(2,1)}, u32[]{:S(2)}, u32[]{:S(2)}) collective-permute-start(bf16[2,4,144,384]{3,2,1,0:T(8,128)(2,1)} %get-tuple-element.654), channel_id=1, source_target_pairs={{0,1},{1,0},{2,3},{3,2},{4,5},{5,4},{6,7},{7,6},{8,9},{9,8},{10,11... | collective-permute-start | bytes 2654216 | tf_op jit(solution)/shard_map/ppermute | solution.py:286
  90.5 39.6 %collective-permute-start.55 = (bf16[2,1,384,1024]{3,2,1,0:T(8,128)(2,1)}, bf16[2,1,384,1024]{3,2,1,0:T(8,128)(2,1)}, u32[]{:S(2)}, u32[]{:S(2)}) collective-permute-start(bf16[2,1,384,1024]{3,2,1,0:T(8,128)(2,1)} %get-tuple-element.669), channel_id=1, source_target_pairs={{0,2},{1,3},{2,0},{3,1},{4,6},{5,7},{6,4},{7,5},{8,10},{9,11},{10,... | collective-permute-start | bytes 4718600 | tf_op jit(solution)/shard_map/ppermute | solution.py:286
  91.1 39.0 %collective-permute-start.56 = (bf16[2,1,384,1024]{3,2,1,0:T(8,128)(2,1)}, bf16[2,1,384,1024]{3,2,1,0:T(8,128)(2,1)}, u32[]{:S(2)}, u32[]{:S(2)}) collective-permute-start(bf16[2,1,384,1024]{3,2,1,0:T(8,128)(2,1)} %get-tuple-element.670), channel_id=1, source_target_pairs={{0,1},{1,0},{2,3},{3,2},{4,5},{5,4},{6,7},{7,6},{8,9},{9,8},{10,11... | collective-permute-start | bytes 4718600 | tf_op jit(solution)/shard_map/ppermute | solution.py:286
  118.6 65.1 %collective-permute-start.57 = (bf16[128,2048]{1,0:T(8,128)(2,1)}, bf16[128,2048]{1,0:T(8,128)(2,1)}, u32[]{:S(2)}, u32[]{:S(2)}) collective-permute-start(bf16[128,2048]{1,0:T(8,128)(2,1)} %get-tuple-element.1007), channel_id=1, source_target_pairs={{0,4},{1,5},{2,6},{3,7},{4,8},{5,9},{6,10},{7,11},{8,12},{9,13},{1... | collective-permute-start | bytes 1572872 | tf_op jit(solution)/shard_map/ppermute | solution.py:315
  118.6 65.1 %collective-permute-start.58 = (bf16[128,2048]{1,0:T(8,128)(2,1)}, bf16[128,2048]{1,0:T(8,128)(2,1)}, u32[]{:S(2)}, u32[]{:S(2)}) collective-permute-start(bf16[128,2048]{1,0:T(8,128)(2,1)} %get-tuple-element.1006), channel_id=1, source_target_pairs={{0,8},{1,9},{2,10},{3,11},{4,12},{5,13},{6,14},{7,15},{8,0},{9,1},... | collective-permute-start | bytes 1572872 | tf_op jit(solution)/shard_map/ppermute | solution.py:315
  118.9 64.8 %collective-permute-start.59 = (bf16[128,2048]{1,0:T(8,128)(2,1)}, bf16[128,2048]{1,0:T(8,128)(2,1)}, u32[]{:S(2)}, u32[]{:S(2)}) collective-permute-start(bf16[128,2048]{1,0:T(8,128)(2,1)} %get-tuple-element.1005), channel_id=1, source_target_pairs={{0,12},{1,13},{2,14},{3,15},{4,0},{5,1},{6,2},{7,3},{8,4},{9,5},{1... | collective-permute-start | bytes 1572872 | tf_op jit(solution)/shard_map/ppermute | solution.py:315
  130.1 29.8 %all-to-all-start = ((bf16[4,16,128,128]{3,2,1,0:T(8,128)(2,1)}), bf16[4,16,128,128]{3,2,1,0:T(8,128)(2,1)}, u32[]{:S(2)}, u32[]{:S(2)}) async-start(bf16[4,16,128,128]{3,2,1,0:T(8,128)(2,1)} %get-tuple-element.231), calls=%async_computation | async-start | bytes 4194304 | tf_op jit(solution)/shard_map/cond/branch_1_fun/all_to_all | solution.py:931
  192.4 59.8 %collective-permute-start.61 = (bf16[4,128,1024]{2,1,0:T(8,128)(2,1)}, bf16[4,128,1024]{2,1,0:T(8,128)(2,1)S(1)}, u32[]{:S(2)}, u32[]{:S(2)}) collective-permute-start(bf16[4,128,1024]{2,1,0:T(8,128)(2,1)} %get-tuple-element.682), channel_id=1, source_target_pairs={{0,1},{1,0},{2,3},{3,2},{4,5},{5,4},{6,7},{7,6},{8,9},{9,8},{10,11... | collective-permute-start | bytes 3145736 | tf_op jit(solution)/shard_map/ppermute | solution.py:286
  193.8 58.4 %collective-permute-start.62 = (bf16[4,128,1024]{2,1,0:T(8,128)(2,1)}, bf16[4,128,1024]{2,1,0:T(8,128)(2,1)}, u32[]{:S(2)}, u32[]{:S(2)}) collective-permute-start(bf16[4,128,1024]{2,1,0:T(8,128)(2,1)} %get-tuple-element.683), channel_id=1, source_target_pairs={{0,2},{1,3},{2,0},{3,1},{4,6},{5,7},{6,4},{7,5},{8,10},{9,11},{10,... | collective-permute-start | bytes 3145736 | tf_op jit(solution)/shard_map/ppermute | solution.py:286
  255.7 47.5 %collective-permute-start.63 = (bf16[2,4,128,1024]{3,2,1,0:T(8,128)(2,1)}, bf16[2,4,128,1024]{3,2,1,0:T(8,128)(2,1)}, u32[]{:S(2)}, u32[]{:S(2)}) collective-permute-start(bf16[2,4,128,1024]{3,2,1,0:T(8,128)(2,1)} %get-tuple-element.694), channel_id=1, source_target_pairs={{0,2},{1,3},{2,0},{3,1},{4,6},{5,7},{6,4},{7,5},{8,10},{9,11},{10,... | collective-permute-start | bytes 6291464 | tf_op jit(solution)/shard_map/ppermute | solution.py:286
  257.2 46.0 %collective-permute-start.64 = (bf16[2,4,128,1024]{3,2,1,0:T(8,128)(2,1)}, bf16[2,4,128,1024]{3,2,1,0:T(8,128)(2,1)}, u32[]{:S(2)}, u32[]{:S(2)}) collective-permute-start(bf16[2,4,128,1024]{3,2,1,0:T(8,128)(2,1)} %get-tuple-element.695), channel_id=1, source_target_pairs={{0,1},{1,0},{2,3},{3,2},{4,5},{5,4},{6,7},{7,6},{8,9},{9,8},{10,11... | collective-permute-start | bytes 6291464 | tf_op jit(solution)/shard_map/ppermute | solution.py:286
  493.8 47.5 %collective-permute-start.79 = (bf16[2,4,128,1024]{3,2,1,0:T(8,128)(2,1)}, bf16[2,4,128,1024]{3,2,1,0:T(8,128)(2,1)S(1)}, u32[]{:S(2)}, u32[]{:S(2)}) collective-permute-start(bf16[2,4,128,1024]{3,2,1,0:T(8,128)(2,1)} %get-tuple-element.746), channel_id=1, source_target_pairs={{0,2},{1,3},{2,0},{3,1},{4,6},{5,7},{6,4},{7,5},{8,10},{9,11},{10,... | collective-permute-start | bytes 6291464 | tf_op jit(solution)/shard_map/ppermute | solution.py:286
  495.3 47.4 %collective-permute-start.80 = (bf16[2,4,128,1024]{3,2,1,0:T(8,128)(2,1)}, bf16[2,4,128,1024]{3,2,1,0:T(8,128)(2,1)}, u32[]{:S(2)}, u32[]{:S(2)}) collective-permute-start(bf16[2,4,128,1024]{3,2,1,0:T(8,128)(2,1)} %get-tuple-element.747), channel_id=1, source_target_pairs={{0,1},{1,0},{2,3},{3,2},{4,5},{5,4},{6,7},{7,6},{8,9},{9,8},{10,11... | collective-permute-start | bytes 6291464 | tf_op jit(solution)/shard_map/ppermute | solution.py:286
  547.2 41.9 %collective-permute-start.84 = (bf16[4,128,1024]{2,1,0:T(8,128)(2,1)}, bf16[4,128,1024]{2,1,0:T(8,128)(2,1)}, u32[]{:S(2)}, u32[]{:S(2)}) collective-permute-start(bf16[4,128,1024]{2,1,0:T(8,128)(2,1)} %get-tuple-element.764), channel_id=1, source_target_pairs={{0,1},{1,0},{2,3},{3,2},{4,5},{5,4},{6,7},{7,6},{8,9},{9,8},{10,11... | collective-permute-start | bytes 3145736 | tf_op jit(solution)/shard_map/ppermute | solution.py:286
  547.7 41.4 %collective-permute-start.85 = (bf16[4,128,1024]{2,1,0:T(8,128)(2,1)}, bf16[4,128,1024]{2,1,0:T(8,128)(2,1)}, u32[]{:S(2)}, u32[]{:S(2)}) collective-permute-start(bf16[4,128,1024]{2,1,0:T(8,128)(2,1)} %get-tuple-element.765), channel_id=1, source_target_pairs={{0,2},{1,3},{2,0},{3,1},{4,6},{5,7},{6,4},{7,5},{8,10},{9,11},{10,... | collective-permute-start | bytes 3145736 | tf_op jit(solution)/shard_map/ppermute | solution.py:286
  594.8 70.3 %collective-permute-start.86 = (bf16[128,2048]{1,0:T(8,128)(2,1)}, bf16[128,2048]{1,0:T(8,128)(2,1)}, u32[]{:S(2)}, u32[]{:S(2)}) collective-permute-start(bf16[128,2048]{1,0:T(8,128)(2,1)} %get-tuple-element.1002), channel_id=1, source_target_pairs={{0,4},{1,5},{2,6},{3,7},{4,8},{5,9},{6,10},{7,11},{8,12},{9,13},{1... | collective-permute-start | bytes 1572872 | tf_op jit(solution)/shard_map/ppermute | solution.py:315
  594.8 70.3 %collective-permute-start.87 = (bf16[128,2048]{1,0:T(8,128)(2,1)}, bf16[128,2048]{1,0:T(8,128)(2,1)}, u32[]{:S(2)}, u32[]{:S(2)}) collective-permute-start(bf16[128,2048]{1,0:T(8,128)(2,1)} %get-tuple-element.1001), channel_id=1, source_target_pairs={{0,8},{1,9},{2,10},{3,11},{4,12},{5,13},{6,14},{7,15},{8,0},{9,1},... | collective-permute-start | bytes 1572872 | tf_op jit(solution)/shard_map/ppermute | solution.py:315
  594.9 70.3 %collective-permute-start.88 = (bf16[128,2048]{1,0:T(8,128)(2,1)}, bf16[128,2048]{1,0:T(8,128)(2,1)}, u32[]{:S(2)}, u32[]{:S(2)}) collective-permute-start(bf16[128,2048]{1,0:T(8,128)(2,1)} %get-tuple-element.1000), channel_id=1, source_target_pairs={{0,12},{1,13},{2,14},{3,15},{4,0},{5,1},{6,2},{7,3},{8,4},{9,5},{1... | collective-permute-start | bytes 1572872 | tf_op jit(solution)/shard_map/ppermute | solution.py:315
  668.6 38.3 %collective-permute-start.91 = (bf16[4,128,2048]{2,1,0:T(8,128)(2,1)}, bf16[4,128,2048]{2,1,0:T(8,128)(2,1)}, u32[]{:S(2)}, u32[]{:S(2)}) collective-permute-start(bf16[4,128,2048]{2,1,0:T(8,128)(2,1)} %get-tuple-element.793), channel_id=1, source_target_pairs={{0,16},{16,0},{1,17},{17,1},{2,18},{18,2},{3,19},{19,3},{4,20},{20... | collective-permute-start | bytes 6291464 | tf_op jit(solution)/shard_map/ppermute | solution.py:290
  668.6 37.5 %collective-permute-start.89 = (bf16[2,1,384,1024]{3,2,1,0:T(8,128)(2,1)}, bf16[2,1,384,1024]{3,2,1,0:T(8,128)(2,1)}, u32[]{:S(2)}, u32[]{:S(2)}) collective-permute-start(bf16[2,1,384,1024]{3,2,1,0:T(8,128)(2,1)} %get-tuple-element.785), channel_id=1, source_target_pairs={{0,2},{1,3},{2,0},{3,1},{4,6},{5,7},{6,4},{7,5},{8,10},{9,11},{10,... | collective-permute-start | bytes 4718600 | tf_op jit(solution)/shard_map/ppermute | solution.py:286
  670.1 36.8 %collective-permute-start.90 = (bf16[2,1,384,1024]{3,2,1,0:T(8,128)(2,1)}, bf16[2,1,384,1024]{3,2,1,0:T(8,128)(2,1)}, u32[]{:S(2)}, u32[]{:S(2)}) collective-permute-start(bf16[2,1,384,1024]{3,2,1,0:T(8,128)(2,1)} %get-tuple-element.786), channel_id=1, source_target_pairs={{0,1},{1,0},{2,3},{3,2},{4,5},{5,4},{6,7},{7,6},{8,9},{9,8},{10,11... | collective-permute-start | bytes 4718600 | tf_op jit(solution)/shard_map/ppermute | solution.py:286
  760.5 31.1 %all-to-all-start.5 = ((bf16[4,128,768]{2,1,0:T(8,128)(2,1)}), bf16[4,128,768]{2,1,0:T(8,128)(2,1)S(1)}, u32[]{:S(2)}, u32[]{:S(2)}) async-start(bf16[4,128,768]{2,1,0:T(8,128)(2,1)} %copy-done.44), calls=%async_computation.5 | async-start | bytes 1572864 | tf_op jit(solution)/shard_map/all_to_all | solution.py:462
  (144 other events, 1466.2 us)
